TPU v7x, 32 devices: a whole 2x2x4 slice. The times are simulated.
32 devices in a mesh: dp: 4 (over y, x), expert: 8 (over z, core).
Axes of the slice: x: 2, y: 2, z: 4, core: 2. Of those that a mesh axis runs over, the one named last changes fastest.
Arguments:
- tokens: bfloat16 [8, 1408, 1536], P('expert', 'dp'), may hold values from -6 to 6
- cotangent: bfloat16 [8, 1408, 1536], P('expert', 'dp'), may hold values from -6 to 6
- parents: int32 [8, 44], P('expert'), may hold values from 0 to 35, as said below
- routes: int32 [8, 1408, 4], P('expert', 'dp'), may hold values from 0 to 7, all different within a row; in each aligned block of 352 rows (0 to 351, 352 to 703, ..., all dimensions but the last counted through in order) at most 264 rows name the same one
- first_gain: bfloat16 [1536], P(('dp', 'expert')), may hold values from 0.099609375 to 1.8984375
- second_gain: bfloat16 [1536], P(('dp', 'expert')), may hold values from 0.099609375 to 1.8984375
- query_weight: bfloat16 [1536, 1536], P(('dp', 'expert')), may hold values from -0.15625 to 0.15625
- key_matrix: bfloat16 [1536, 256], P(('dp', 'expert')), may hold values from -0.15625 to 0.15625
- value_matrix: bfloat16 [1536, 256], P(('dp', 'expert')), may hold values from -0.15625 to 0.15625
- out_weight: bfloat16 [1536, 1536], P(('dp', 'expert')), may hold values from -2.5 to 2.5
- router_weight: bfloat16 [1536, 8], P(('dp', 'expert')), may hold values from -0.078125 to 0.078125
- gate_weight: bfloat16 [8, 1536, 768], P('expert'), may hold values from -0.15625 to 0.15625
- up_weight: bfloat16 [8, 1536, 768], P('expert'), may hold values from -0.15625 to 0.15625
- down_weight: bfloat16 [8, 768, 1536], P('expert'), may hold values from -0.625 to 0.625
Outputs:
- output: bfloat16 [8, 1408, 1536], P('expert', 'dp')
- grad_tokens: float32 [8, 1408, 1536], P('expert', 'dp')
- grad_first_gain: float32 [1536], P(('dp', 'expert'))
- grad_second_gain: float32 [1536], P(('dp', 'expert'))
- grad_query: float32 [1536, 1536], P(('dp', 'expert'))
- grad_key: float32 [1536, 256], P(('dp', 'expert'))
- grad_value: float32 [1536, 256], P(('dp', 'expert'))
- grad_out: float32 [1536, 1536], P(('dp', 'expert'))
- grad_router: float32 [1536, 8], P(('dp', 'expert'))
- grad_gate: float32 [8, 1536, 768], P('expert')
- grad_up: float32 [8, 1536, 768], P('expert')
- grad_down: float32 [8, 768, 1536], P('expert')
Inputs may be any that keep to these rules, and one draw needn't show every extreme that they name: `parents`: block 0 has parent 0; each other trunk block b < 32 has parent b - 1; the next 4 blocks are branches with parent 1024 // 32 - 1; the last 8 blocks are leaves, two to each branch, whose parent is a branch. `routes`: the 4 experts of a token are distinct. Among the 352 tokens of one device at most 264 name the same expert, a bound that some block reaches.
All inputs are finite; a program needn't handle non-finite values.
Results may differ from a plain program's by a relative error of at most 0.019.
Values may be sent and summed in bfloat16 or wider, within the bound.
A program may use at most 320 MiB of HBM per device.

v0:
```python
import jax
import jax.numpy as jnp
from jax import lax
from jax.sharding import PartitionSpec as P

MODEL_WIDTH = 1536
QUERY_HEADS = 12
KEY_VALUE_HEADS = 2
HEAD_SIZE = 128
FF = 768
TOPK = 4
SEG = 32


EPS = 1e-06
THETA = 10000.0
HIGH_PRECISION = lax.Precision.HIGHEST
NEGATIVE = -1e30


def ancestry(parent_row):
    block_count = parent_row.shape[0]
    block_ids = jnp.arange(block_count, dtype=jnp.int32)

    def advance(counter, carried):
        current, ancestors = carried
        ancestors = jnp.maximum(
            ancestors, (current[:, None] == block_ids[None, :]).astype(jnp.float32)
        )
        return (jnp.take(parent_row, current), ancestors)

    start_pair = (block_ids, jnp.zeros((block_count, block_count), jnp.float32))
    current, ancestors = lax.fori_loop(0, block_count, advance, start_pair)
    depths = (jnp.sum(ancestors, axis=1) - 1.0).astype(jnp.int32)
    return (ancestors, depths)


def apply_rotation(values, positions):
    half_width = values.shape[-1] // 2
    frequency = jnp.power(
        THETA, -(jnp.arange(half_width, dtype=jnp.float32) * 2.0 / values.shape[-1])
    )
    angles = positions.astype(jnp.float32)[:, None] * frequency[None, :]
    cosine = jnp.cos(angles)[:, None, :]
    sine_part = jnp.sin(angles)[:, None, :]
    first_half = values[..., :half_width]
    second_half = values[..., half_width:]
    return jnp.concatenate(
        [
            first_half * cosine - second_half * sine_part,
            second_half * cosine + first_half * sine_part,
        ],
        axis=-1,
    )


def normalize(values, scales):
    return values * lax.rsqrt(jnp.mean(values * values, axis=-1, keepdims=True) + EPS) * scales


def place(route_ids, experts, capacity):
    one_hot = (route_ids[..., None] == jnp.arange(experts, dtype=jnp.int32)).astype(jnp.int32)
    earlier = jnp.cumsum(one_hot, axis=-2) - one_hot
    slot_rank = jnp.sum(earlier * one_hot, axis=-1)
    return route_ids * capacity + slot_rank


def visibility(ancestors, depths, query_ids, key_ids):
    block_ids = jnp.arange(ancestors.shape[0], dtype=jnp.int32)
    query_hit = (query_ids // SEG)[:, None] == block_ids[None, :]
    key_hit = (key_ids // SEG)[:, None] == block_ids[None, :]
    query_positions = (
        jnp.sum(jnp.where(query_hit, depths[None, :], 0), axis=1) * SEG + query_ids % SEG
    )
    key_pos = jnp.sum(jnp.where(key_hit, depths[None, :], 0), axis=1) * SEG + key_ids % SEG
    reach = jnp.dot(query_hit.astype(jnp.float32), ancestors, precision=HIGH_PRECISION)
    reach_keys = jnp.repeat(reach, SEG, axis=1)
    visible = (reach_keys > 0.5) & (key_pos[None, :] <= query_positions[:, None])
    return (visible, query_positions)


def head_scores(query_rotated, keys_all, visible, key_value_head, query_group_width):
    query_part = query_rotated[
        :, key_value_head * query_group_width : (key_value_head + 1) * query_group_width, :
    ]
    key_part = keys_all[:, key_value_head * HEAD_SIZE : (key_value_head + 1) * HEAD_SIZE]
    scores = jnp.einsum(
        "rgd,kd->grk", query_part, key_part, preferred_element_type=jnp.float32
    ) * HEAD_SIZE ** (-0.5)
    return jnp.where(visible[None], scores, NEGATIVE)


def gelu_product(gate_pre, up_pre):
    return jax.nn.gelu(gate_pre, approximate=True) * up_pre


def expert_hidden(received, local_gate, local_up):
    local_count = local_gate.shape[0]
    slot_count = received.shape[1]
    grouped_queries = received.reshape(-1, local_count, slot_count, MODEL_WIDTH)
    gate_pre = jnp.einsum(
        "sjcd,jdf->sjcf", grouped_queries, local_gate, preferred_element_type=jnp.float32
    )
    up_pre = jnp.einsum(
        "sjcd,jdf->sjcf", grouped_queries, local_up, preferred_element_type=jnp.float32
    )
    hidden = gelu_product(gate_pre, up_pre).astype(jnp.bfloat16)
    flat_shape = (received.shape[0], slot_count, FF)
    return (gate_pre.reshape(flat_shape), up_pre.reshape(flat_shape), hidden.reshape(flat_shape))


def expert_result(hidden, local_down):
    local_count = local_down.shape[0]
    grouped_queries = hidden.reshape(-1, local_count, hidden.shape[1], FF)
    result = jnp.einsum(
        "sjcf,jfd->sjcd", grouped_queries, local_down, preferred_element_type=jnp.float32
    )
    return result.astype(jnp.bfloat16).reshape(hidden.shape[0], hidden.shape[1], MODEL_WIDTH)


def on_device(
    tokens,
    cotangent,
    parents,
    routes,
    first_gain,
    second_gain,
    query_weight,
    key_matrix,
    value_matrix,
    out_weight,
    router_weight,
    gate_weight,
    up_weight,
    down_weight,
):
    gathered = (
        lax.all_gather(query_weight, ("dp", "expert"), axis=0, tiled=True),
        lax.all_gather(key_matrix, ("dp", "expert"), axis=0, tiled=True),
        lax.all_gather(value_matrix, ("dp", "expert"), axis=0, tiled=True),
        lax.all_gather(out_weight, ("dp", "expert"), axis=0, tiled=True),
        lax.all_gather(router_weight, ("dp", "expert"), axis=0, tiled=True),
        lax.all_gather(first_gain, ("dp", "expert"), axis=0, tiled=True),
        lax.all_gather(second_gain, ("dp", "expert"), axis=0, tiled=True),
    )
    query_full, key_complete, value_complete, out_full, router_full, gain_one, gain_two = gathered
    scale_one = gain_one.astype(jnp.float32)
    scale_two = gain_two.astype(jnp.float32)
    inputs = tokens[0].astype(jnp.float32)
    total_rows = inputs.shape[0]
    query_group_width = QUERY_HEADS // KEY_VALUE_HEADS
    ancestors, depths = ancestry(parents[0])
    tree_length = ancestors.shape[0] * SEG
    query_ids = lax.axis_index("dp") * total_rows + jnp.arange(total_rows, dtype=jnp.int32)
    key_ids = jnp.arange(tree_length, dtype=jnp.int32)
    visible, query_positions = visibility(ancestors, depths, query_ids, key_ids)
    first_normed = normalize(inputs, scale_one).astype(jnp.bfloat16)
    query_proj = jnp.dot(first_normed, query_full, preferred_element_type=jnp.float32).reshape(
        total_rows, QUERY_HEADS, HEAD_SIZE
    )
    key_projected = jnp.dot(first_normed, key_complete, preferred_element_type=jnp.float32).reshape(
        total_rows, KEY_VALUE_HEADS, HEAD_SIZE
    )
    value_projected = jnp.dot(first_normed, value_complete, preferred_element_type=jnp.float32)
    query_rotated = apply_rotation(query_proj, query_positions).astype(jnp.bfloat16)
    key_rotated = (
        apply_rotation(key_projected, query_positions)
        .astype(jnp.bfloat16)
        .reshape(total_rows, KEY_VALUE_HEADS * HEAD_SIZE)
    )
    value_low = value_projected.astype(jnp.bfloat16)
    keys_all, values_all = (
        lax.all_gather(key_rotated, "dp", axis=0, tiled=True),
        lax.all_gather(value_low, "dp", axis=0, tiled=True),
    )
    mixed_parts = []
    log_totals = []
    for key_value_head in range(KEY_VALUE_HEADS):
        scores = head_scores(query_rotated, keys_all, visible, key_value_head, query_group_width)
        row_max = jnp.max(scores, axis=-1, keepdims=True)
        exponent = jnp.exp(scores - row_max)
        row_total = jnp.sum(exponent, axis=-1, keepdims=True)
        log_totals.append(row_max + jnp.log(row_total))
        softmax_out = (exponent / row_total).astype(jnp.bfloat16)
        value_part = values_all[:, key_value_head * HEAD_SIZE : (key_value_head + 1) * HEAD_SIZE]
        mixed_parts.append(
            jnp.einsum("grk,kd->rgd", softmax_out, value_part, preferred_element_type=jnp.float32)
        )
    mixed_out = (
        jnp.concatenate(mixed_parts, axis=1)
        .reshape(total_rows, QUERY_HEADS * HEAD_SIZE)
        .astype(jnp.bfloat16)
    )
    middle = inputs + jnp.dot(mixed_out, out_full, preferred_element_type=jnp.float32)
    normed_two = normalize(middle, scale_two).astype(jnp.bfloat16)
    logits = jnp.dot(normed_two, router_full, preferred_element_type=jnp.float32)
    route_ids = routes[0]
    experts = gate_weight.shape[0] * lax.axis_size("expert")
    capacity = 3 * total_rows * TOPK // (2 * experts)
    expert_ids = jnp.arange(experts, dtype=jnp.int32)
    route_hits = route_ids[:, :, None] == expert_ids[None, None, :]
    chosen = jnp.sum(jnp.where(route_hits, logits[:, None, :], 0.0), axis=2)
    chosen_max = jnp.max(chosen, axis=1, keepdims=True)
    chosen_exp = jnp.exp(chosen - chosen_max)
    gate_weights = chosen_exp / jnp.sum(chosen_exp, axis=1, keepdims=True)
    pair_count = total_rows * TOPK
    slot_index = place(route_ids.reshape(pair_count), experts, capacity)
    slot_source = (
        jnp.full((experts * capacity,), pair_count, jnp.int32)
        .at[slot_index]
        .set(jnp.arange(pair_count, dtype=jnp.int32))
    )
    slot_used = slot_source < pair_count
    slot_pair = jnp.where(slot_used, slot_source, 0)
    slot_token = slot_pair // TOPK
    zero_low = jnp.zeros((), jnp.bfloat16)
    outgoing = jnp.where(slot_used[:, None], normed_two[slot_token], zero_low).reshape(
        experts, capacity, MODEL_WIDTH
    )
    gate_pre, up_pre, hidden = expert_hidden(
        lax.all_to_all(outgoing, "expert", split_axis=0, concat_axis=0, tiled=True),
        gate_weight,
        up_weight,
    )
    dispatched = expert_result(hidden, down_weight)
    returned = lax.all_to_all(dispatched, "expert", split_axis=0, concat_axis=0, tiled=True)
    expert_rows = (
        returned.reshape(experts * capacity, MODEL_WIDTH)[slot_index]
        .astype(jnp.float32)
        .reshape(total_rows, TOPK, MODEL_WIDTH)
    )
    final = middle + jnp.sum(gate_weights[:, :, None] * expert_rows, axis=1)
    output = final.astype(jnp.bfloat16)[None]
    upstream = cotangent[0].astype(jnp.float32)
    gate_grad = jnp.sum(upstream[:, None, :] * expert_rows, axis=2)
    chosen_grad = gate_weights * (
        gate_grad - jnp.sum(gate_weights * gate_grad, axis=1, keepdims=True)
    )
    logit_grad = jnp.sum(jnp.where(route_hits, chosen_grad[:, :, None], 0.0), axis=1)
    pair_grad = (
        (gate_weights[:, :, None] * upstream[:, None, :])
        .astype(jnp.bfloat16)
        .reshape(pair_count, MODEL_WIDTH)
    )
    grad_outgoing = jnp.where(slot_used[:, None], pair_grad[slot_pair], zero_low).reshape(
        experts, capacity, MODEL_WIDTH
    )
    received, grad_in = (
        lax.all_to_all(outgoing, "expert", split_axis=0, concat_axis=0, tiled=True),
        lax.all_to_all(grad_outgoing, "expert", split_axis=0, concat_axis=0, tiled=True),
    )
    gate_pre, up_pre, hidden = expert_hidden(received, gate_weight, up_weight)
    local_count = gate_weight.shape[0]
    slot_count = received.shape[1]
    grouped_rows = received.reshape(-1, local_count, slot_count, MODEL_WIDTH)
    grouped_hidden = hidden.reshape(-1, local_count, slot_count, FF)
    grouped_grad = grad_in.reshape(-1, local_count, slot_count, MODEL_WIDTH)
    down_grad = jnp.einsum(
        "sjcf,sjcd->jfd", grouped_hidden, grouped_grad, preferred_element_type=jnp.float32
    )
    hidden_grad = jnp.einsum(
        "sjcd,jfd->sjcf", grouped_grad, down_weight, preferred_element_type=jnp.float32
    )
    _, product_pull = jax.vjp(gelu_product, gate_pre, up_pre)
    gate_pre_grad, up_pre_grad = product_pull(hidden_grad.reshape(gate_pre.shape))
    gate_low = gate_pre_grad.astype(jnp.bfloat16).reshape(-1, local_count, slot_count, FF)
    up_low = up_pre_grad.astype(jnp.bfloat16).reshape(-1, local_count, slot_count, FF)
    gate_w_grad = jnp.einsum(
        "sjcd,sjcf->jdf", grouped_rows, gate_low, preferred_element_type=jnp.float32
    )
    up_w_grad = jnp.einsum(
        "sjcd,sjcf->jdf", grouped_rows, up_low, preferred_element_type=jnp.float32
    )
    row_grad = jnp.einsum(
        "sjcf,jdf->sjcd", gate_low, gate_weight, preferred_element_type=jnp.float32
    ) + jnp.einsum("sjcf,jdf->sjcd", up_low, up_weight, preferred_element_type=jnp.float32)
    row_grad = row_grad.astype(jnp.bfloat16).reshape(received.shape)
    returned_grad = lax.all_to_all(row_grad, "expert", split_axis=0, concat_axis=0, tiled=True)
    pair_rows = (
        returned_grad.reshape(experts * capacity, MODEL_WIDTH)[slot_index]
        .astype(jnp.float32)
        .reshape(total_rows, TOPK, MODEL_WIDTH)
    )
    summed_experts = (
        lax.psum(gate_w_grad.astype(jnp.bfloat16), "dp").astype(jnp.float32),
        lax.psum(up_w_grad.astype(jnp.bfloat16), "dp").astype(jnp.float32),
        lax.psum(down_grad.astype(jnp.bfloat16), "dp").astype(jnp.float32),
    )
    router_wide = router_full.astype(jnp.float32)
    normed_two_grad = jnp.dot(logit_grad, router_wide.T, precision=HIGH_PRECISION) + jnp.sum(
        pair_rows, axis=1
    )
    router_grad = jnp.dot(normed_two.astype(jnp.float32).T, logit_grad, precision=HIGH_PRECISION)
    _, second_pull = jax.vjp(normalize, middle, scale_two)
    middle_norm_grad, second_gain_grad = second_pull(normed_two_grad)
    middle_grad = upstream + middle_norm_grad
    attended_low = middle_grad.astype(jnp.bfloat16)
    out_grad = jnp.einsum("rd,re->de", mixed_out, attended_low, preferred_element_type=jnp.float32)
    mixed_grad = jnp.einsum("re,de->rd", attended_low, out_full, preferred_element_type=jnp.float32)
    mixed_grad = mixed_grad.astype(jnp.bfloat16).reshape(total_rows, QUERY_HEADS, HEAD_SIZE)
    query_parts = []
    key_parts = []
    value_parts = []
    for key_value_head in range(KEY_VALUE_HEADS):
        scores = head_scores(query_rotated, keys_all, visible, key_value_head, query_group_width)
        softmax_out = jnp.exp(scores - log_totals[key_value_head])
        query_part = query_rotated[
            :, key_value_head * query_group_width : (key_value_head + 1) * query_group_width, :
        ]
        key_part = keys_all[:, key_value_head * HEAD_SIZE : (key_value_head + 1) * HEAD_SIZE]
        value_part = values_all[:, key_value_head * HEAD_SIZE : (key_value_head + 1) * HEAD_SIZE]
        grad_part = mixed_grad[
            :, key_value_head * query_group_width : (key_value_head + 1) * query_group_width, :
        ]
        value_parts.append(
            jnp.einsum(
                "grk,rgd->kd",
                softmax_out.astype(jnp.bfloat16),
                grad_part,
                preferred_element_type=jnp.float32,
            )
        )
        attn_grad = jnp.einsum(
            "rgd,kd->grk", grad_part, value_part, preferred_element_type=jnp.float32
        )
        score_grad = softmax_out * (
            attn_grad - jnp.sum(softmax_out * attn_grad, axis=-1, keepdims=True)
        )
        score_low = score_grad.astype(jnp.bfloat16)
        query_parts.append(
            jnp.einsum("grk,kd->rgd", score_low, key_part, preferred_element_type=jnp.float32)
            * HEAD_SIZE ** (-0.5)
        )
        key_parts.append(
            jnp.einsum("grk,rgd->kd", score_low, query_part, preferred_element_type=jnp.float32)
            * HEAD_SIZE ** (-0.5)
        )
    key_total_sum, value_sum = (
        lax.psum_scatter(
            jnp.concatenate(key_parts, axis=1).astype(jnp.bfloat16),
            "dp",
            scatter_dimension=0,
            tiled=True,
        ).astype(jnp.float32),
        lax.psum_scatter(
            jnp.concatenate(value_parts, axis=1).astype(jnp.bfloat16),
            "dp",
            scatter_dimension=0,
            tiled=True,
        ).astype(jnp.float32),
    )
    _, query_pull = jax.vjp(lambda values: apply_rotation(values, query_positions), query_proj)
    _, key_pullback = jax.vjp(lambda values: apply_rotation(values, query_positions), key_projected)
    query_grad = (
        query_pull(jnp.concatenate(query_parts, axis=1))[0]
        .astype(jnp.bfloat16)
        .reshape(total_rows, QUERY_HEADS * HEAD_SIZE)
    )
    key_grad = (
        key_pullback(key_total_sum.reshape(total_rows, KEY_VALUE_HEADS, HEAD_SIZE))[0]
        .astype(jnp.bfloat16)
        .reshape(total_rows, KEY_VALUE_HEADS * HEAD_SIZE)
    )
    value_grad = value_sum.astype(jnp.bfloat16)
    query_w_grad = jnp.einsum(
        "rd,re->de", first_normed, query_grad, preferred_element_type=jnp.float32
    )
    key_w_grad = jnp.einsum("rd,re->de", first_normed, key_grad, preferred_element_type=jnp.float32)
    value_w_grad = jnp.einsum(
        "rd,re->de", first_normed, value_grad, preferred_element_type=jnp.float32
    )
    normed_one_grad = (
        jnp.einsum("re,de->rd", query_grad, query_full, preferred_element_type=jnp.float32)
        + jnp.einsum("re,de->rd", key_grad, key_complete, preferred_element_type=jnp.float32)
        + jnp.einsum("re,de->rd", value_grad, value_complete, preferred_element_type=jnp.float32)
    )
    _, first_pull = jax.vjp(normalize, inputs, scale_one)
    input_norm_grad, first_gain_grad = first_pull(normed_one_grad)
    input_grad = (middle_grad + input_norm_grad)[None]
    shares = (
        lax.psum_scatter(query_w_grad, ("dp", "expert"), scatter_dimension=0, tiled=True),
        lax.psum_scatter(key_w_grad, ("dp", "expert"), scatter_dimension=0, tiled=True),
        lax.psum_scatter(value_w_grad, ("dp", "expert"), scatter_dimension=0, tiled=True),
        lax.psum_scatter(out_grad, ("dp", "expert"), scatter_dimension=0, tiled=True),
        lax.psum_scatter(router_grad, ("dp", "expert"), scatter_dimension=0, tiled=True),
        lax.psum_scatter(first_gain_grad, ("dp", "expert"), scatter_dimension=0, tiled=True),
        lax.psum_scatter(second_gain_grad, ("dp", "expert"), scatter_dimension=0, tiled=True),
    )
    return (
        output,
        input_grad,
        shares[5],
        shares[6],
        shares[0],
        shares[1],
        shares[2],
        shares[3],
        shares[4],
        summed_experts[0],
        summed_experts[1],
        summed_experts[2],
    )


def solution(mesh):
    return jax.shard_map(
        on_device,
        mesh=mesh,
        in_specs=(
            P("expert", "dp", None),
            P("expert", "dp", None),
            P("expert", None),
            P("expert", "dp", None),
            P(("dp", "expert")),
            P(("dp", "expert")),
            P(("dp", "expert"), None),
            P(("dp", "expert"), None),
            P(("dp", "expert"), None),
            P(("dp", "expert"), None),
            P(("dp", "expert"), None),
            P("expert", None, None),
            P("expert", None, None),
            P("expert", None, None),
        ),
        out_specs=(
            P("expert", "dp", None),
            P("expert", "dp", None),
            P(("dp", "expert")),
            P(("dp", "expert")),
            P(("dp", "expert"), None),
            P(("dp", "expert"), None),
            P(("dp", "expert"), None),
            P(("dp", "expert"), None),
            P(("dp", "expert"), None),
            P("expert", None, None),
            P("expert", None, None),
            P("expert", None, None),
        ),
        check_vma=False,
    )
```

profile of v0, /device:TPU:0, one launch (start us, length us, event | category | flops | bytes accessed | tf_op | source)
XLA Modules:
  0.0 1896.3 jit_solution(13441532928320123674)
XLA Ops:
  23.2 42.3 %all-reduce.9 = (bf16[1536]{0:T(1024)(128)(2,1)S(1)}, bf16[1536]{0:T(1024)(128)(2,1)S(1)}) all-reduce(bf16[1536]{0:T(1024)(128)(2,1)S(1)} %dynamic-update-slice, bf16[1536]{0:T(1024)(128)(2,1)S(1)} %dynamic-update-slice.1), channel_id=1, replica_groups=mesh['dp'=4,'expert'=8] {'dp','expert'}, use_global_device_ids=true, to_apply=%add.4 | all-reduce | flops 3072 | bytes 12288
  65.6 68.9 %while.13 = (s32[]{:T(128)}, s32[44]{0:T(128)S(1)}, f32[44,44]{1,0:T(8,128)S(1)}, s32[44]{0:T(128)}, s32[]{:T(128)}, /*index=5*/s32[]{:T(128)}) while((s32[]{:T(128)}, s32[44]{0:T(128)S(1)}, f32[44,44]{1,0:T(8,128)S(1)}, s32[44]{0:T(128)}, s32[]{:T(128)}, /*index=5*/s32[]{:T(128)}) %tuple.73), condition=%wide.region_2.3_spmd.clone, body=%wide.region_1.0_spmd.clone.sunk | while | flops 9211 | bytes 21423 | solution.py:33
  135.1 43.5 %all_gather.30 = bf16[1536,256]{1,0:T(8,128)(2,1)S(1)} all-gather(bf16[48,256]{1,0:T(8,128)(2,1)S(1)} %copy-done.66), channel_id=1, replica_groups=mesh['dp'=4,'expert'=8] {'dp','expert'}, dimensions={0}, use_global_device_ids=true | all-gather | bytes 811008 | tf_op jit(solution)/shard_map/all_gather | solution.py:139
  181.8 36.9 %all-gather = bf16[32,48,8]{1,2,0:T(8,128)(2,1)S(1)} all-gather(bf16[1,48,8]{1,2,0:T(8,128)(2,1)S(1)} %bitcast.339), channel_id=1, replica_groups=mesh['dp'=4,'expert'=8] {'dp','expert'}, dimensions={0}, use_global_device_ids=true | all-gather | bytes 25344 | tf_op jit(solution)/shard_map/all_gather | solution.py:142
  230.3 10.2 mul.543
  243.7 41.2 %all_gather.28 = bf16[1536,256]{1,0:T(8,128)(2,1)S(1)} all-gather(bf16[48,256]{1,0:T(8,128)(2,1)S(1)} %copy-done.67), channel_id=1, replica_groups=mesh['dp'=4,'expert'=8] {'dp','expert'}, dimensions={0}, use_global_device_ids=true | all-gather | bytes 811008 | tf_op jit(solution)/shard_map/all_gather | solution.py:140
  286.3 12.6 all_gather.29
  298.9 11.6 all_gather.31
  363.3 8.5 gather_fusion.1
  377.8 17.5 gather_fusion.3
  403.7 146.7 %all_to_all.21 = bf16[8,264,1536]{2,1,0:T(8,128)(2,1)} all-to-all(bf16[8,264,1536]{2,1,0:T(8,128)(2,1)S(1)} %get-tuple-element.98), channel_id=1, replica_groups=mesh['dp'=4,'expert'=8] {'expert'}, dimensions={0} | all-to-all | bytes 12976128 | tf_op jit(solution)/shard_map/all_to_all | solution.py:221
  555.4 9.8 fusion.67
  565.1 133.4 %all-to-all-done.2 = bf16[8,264,1536]{2,1,0:T(8,128)(2,1)} async-done(((bf16[8,264,1536]{2,1,0:T(8,128)(2,1)}), bf16[8,264,1536]{2,1,0:T(8,128)(2,1)}, u32[]{:S(2)}, u32[]{:S(2)}) %all-to-all-start.2) | async-done | bytes 6488096 | tf_op jit(solution)/shard_map/all_to_all | solution.py:250
  707.0 14.9 fusion.32
  751.0 127.9 %all-to-all-done.1 = bf16[8,264,1536]{2,1,0:T(8,128)(2,1)} async-done(((bf16[8,264,1536]{2,1,0:T(8,128)(2,1)}), bf16[8,264,1536]{2,1,0:T(8,128)(2,1)}, u32[]{:S(2)}, u32[]{:S(2)}) %all-to-all-start.1) | async-done | bytes 6488096 | tf_op jit(solution)/shard_map/all_to_all | solution.py:226
  883.9 10.6 fusion.39
  894.5 8.9 fusion.36
  903.4 13.9 gather_fusion.2
  917.3 8.5 reshape.596
  925.9 10.4 multiply_reduce_fusion
  936.5 90.4 %all-to-all-done.3 = bf16[8,264,1536]{2,1,0:T(8,128)(2,1)} async-done(((bf16[8,264,1536]{2,1,0:T(8,128)(2,1)}), bf16[8,264,1536]{2,1,0:T(8,128)(2,1)}, u32[]{:S(2)}, u32[]{:S(2)}) %all-to-all-start.3) | async-done | bytes 6488096 | tf_op jit(solution)/shard_map/all_to_all | solution.py:278
  1026.9 14.1 gather_fusion.4
  1049.4 10.1 reduce_sum.230
  1093.2 9.4 fusion.7
  1121.4 10.3 fusion.40
  1178.1 124.0 %all-reduce.13.cloned.1.call-done = (bf16[1,1536,768]{2,1,0:T(8,128)(2,1)}, bf16[1,1536,768]{2,1,0:T(8,128)(2,1)}, bf16[1,768,1536]{2,1,0:T(8,128)(2,1)}) async-done(((bf16[1,1536,768]{2,1,0:T(8,128)(2,1)}, bf16[1,1536,768]{2,1,0:T(8,128)(2,1)}, bf16[1,768,1536]{2,1,0:T(8,128)(2,1)}), (bf16[1,1536,768]{2,1,0:T(8,128)(2,1)}, bf16[1,1536,768]{2,1,0:T(8,128)(2,1)}, ...) | async-done | bytes 7077904 | tf_op jit(solution)/shard_map/psum | solution.py:285
  1315.3 87.2 %reduce-scatter.26.cloned.1.call-done = f32[48,8]{1,0:T(8,128)} async-done(((f32[1536,8]{1,0:T(8,128)}), f32[48,8]{1,0:T(8,128)}) %reduce-scatter.26.cloned.1.call-update) | async-done | bytes 1552
  1408.5 40.1 %all-reduce.8 = (f32[1536]{0:T(1024)S(1)}, f32[1536]{0:T(1024)S(1)}) all-reduce(f32[1536]{0:T(1024)S(1)} %get-tuple-element.61, f32[1536]{0:T(1024)S(1)} %get-tuple-element.59), channel_id=4, replica_groups=mesh['dp'=4,'expert'=8] {'dp','expert'}, use_global_device_ids=true, to_apply=%region_30.31.clone | all-reduce | flops 3072 | bytes 24576
  1454.1 50.2 %reduce-scatter.18.cloned.1.call-done = f32[48,256]{1,0:T(8,128)} async-done(((f32[1536,256]{1,0:T(8,128)}), f32[48,256]{1,0:T(8,128)}) %reduce-scatter.18.cloned.1.call-update) | async-done | bytes 49168 | tf_op jit(solution)/shard_map/reduce_scatter | solution.py:383
  1504.4 101.9 %reduce-scatter.16.cloned.1.call-done = f32[48,256]{1,0:T(8,128)} async-done(((f32[1536,256]{1,0:T(8,128)}), f32[48,256]{1,0:T(8,128)}) %reduce-scatter.16.cloned.1.call-update) | async-done | bytes 49168 | tf_op jit(solution)/shard_map/reduce_scatter | solution.py:382
  1606.3 141.0 %reduce-scatter.20.cloned.1.call-done = f32[48,1536]{1,0:T(8,128)} async-done(((f32[1536,1536]{1,0:T(8,128)}), f32[48,1536]{1,0:T(8,128)}) %reduce-scatter.20.cloned.1.call-update) | async-done | bytes 294928 | tf_op jit(solution)/shard_map/reduce_scatter | solution.py:384
  1747.3 142.0 %reduce-scatter.14.cloned.1.call-done = f32[48,1536]{1,0:T(8,128)} async-done(((f32[1536,1536]{1,0:T(8,128)}), f32[48,1536]{1,0:T(8,128)}) %reduce-scatter.14.cloned.1.call-update) | async-done | bytes 294928 | tf_op jit(solution)/shard_map/reduce_scatter | solution.py:381
  (557 shorter events, 348.9 us)
Async XLA Ops:
  7.2 699.8 %copy-start = (bf16[1,1536,768]{2,1,0:T(8,128)(2,1)S(1)}, bf16[1,1536,768]{2,1,0:T(8,128)(2,1)}, u32[]{:S(2)}) copy-start(bf16[1,1536,768]{2,1,0:T(8,128)(2,1)} %param.27) | copy-start | bytes 7077892
  7.2 303.3 %all-gather.4.cloned.1.call-start = ((), (), s32[]{:S(2)}) async-start(), calls=%async_computation.11 | async-start | bytes 4866048 | tf_op jit(solution)/shard_map/all_gather | solution.py:138
  7.9 346.6 %all-gather.6.cloned.1.call-start = ((), (), s32[]{:S(2)}) async-start(), calls=%async_computation.12 | async-start | bytes 4866048 | tf_op jit(solution)/shard_map/all_gather | solution.py:141
  10.2 124.9 %copy-start.66 = (bf16[48,256]{1,0:T(8,128)(2,1)S(1)}, bf16[48,256]{1,0:T(8,128)(2,1)}, u32[]{:S(2)}) copy-start(bf16[48,256]{1,0:T(8,128)(2,1)} %param.23) | copy-start | bytes 73732
  13.8 121.4 %copy-start.62 = (s32[1408]{0:T(1024)}, s32[1408]{0:T(1024)S(1)}, u32[]{:S(2)}) copy-start(s32[1408]{0:T(1024)S(1)} %fusion.131) | copy-start | bytes 16900
  65.5 251.5 %copy-start.45 = (f32[1536]{0:T(1024)}, f32[1536]{0:T(1024)S(1)}, u32[]{:S(2)}) copy-start(f32[1536]{0:T(1024)S(1)} %convert_element_type.198) | copy-start | bytes 18436
  65.6 293.7 %copy-start.48 = (f32[1536]{0:T(1024)}, f32[1536]{0:T(1024)S(1)}, u32[]{:S(2)}) copy-start(f32[1536]{0:T(1024)S(1)} %convert_element_type.210) | copy-start | bytes 18436
  134.5 47.3 %copy-start.72 = (bf16[48,8]{0,1:T(8,128)(2,1)S(1)}, bf16[48,8]{0,1:T(8,128)(2,1)}, u32[]{:S(2)}) copy-start(bf16[48,8]{0,1:T(8,128)(2,1)} %param.26) | copy-start | bytes 2308
  178.6 43.9 %copy-start.20 = (bf16[1536,256]{1,0:T(8,128)(2,1)}, bf16[1536,256]{1,0:T(8,128)(2,1)S(1)}, u32[]{:S(2)}) copy-start(bf16[1536,256]{1,0:T(8,128)(2,1)S(1)} %all_gather.30) | copy-start | bytes 2359300
  218.8 142.0 %copy-start.41 = (bf16[1536,8]{0,1:T(8,128)(2,1)}, bf16[1536,8]{0,1:T(8,128)(2,1)S(1)}, u32[]{:S(2)}) copy-start(bf16[1536,8]{0,1:T(8,128)(2,1)S(1)} %reshape.657) | copy-start | bytes 73732
  240.8 76.2 %copy-start.56 = (f32[352]{0:T(512)}, f32[352]{0:T(512)S(1)}, u32[]{:S(2)}) copy-start(f32[352]{0:T(512)S(1)} %fusion.137) | copy-start | bytes 4228
  550.4 148.1 %all-to-all-start.2 = ((bf16[8,264,1536]{2,1,0:T(8,128)(2,1)}), bf16[8,264,1536]{2,1,0:T(8,128)(2,1)}, u32[]{:S(2)}, u32[]{:S(2)}) async-start(bf16[8,264,1536]{2,1,0:T(8,128)(2,1)} %get-tuple-element.97), calls=%async_computation.2 | async-start | bytes 12976128 | tf_op jit(solution)/shard_map/all_to_all | solution.py:250
  707.0 16.6 copy-start.73
  730.7 148.2 %all-to-all-start.1 = ((bf16[8,264,1536]{2,1,0:T(8,128)(2,1)}), bf16[8,264,1536]{2,1,0:T(8,128)(2,1)}, u32[]{:S(2)}, u32[]{:S(2)}) async-start(bf16[8,264,1536]{2,1,0:T(8,128)(2,1)} %convolution_convert_fusion), calls=%async_computation.1 | async-start | bytes 12976128 | tf_op jit(solution)/shard_map/all_to_all | solution.py:226
  751.0 132.8 %copy-start.63 = (s32[1408]{0:T(1024)S(1)}, s32[1408]{0:T(1024)}, u32[]{:S(2)}) copy-start(s32[1408]{0:T(1024)} %copy-done.62) | copy-start | bytes 16900
  751.0 132.8 %copy-start.51 = (f32[6,352]{1,0:T(8,128)S(1)}, f32[6,352]{1,0:T(8,128)}, u32[]{:S(2)}) copy-start(f32[6,352]{1,0:T(8,128)} %copy-done.50) | copy-start | bytes 25348
  751.0 132.8 %copy-start.59 = (f32[6,352]{1,0:T(8,128)S(1)}, f32[6,352]{1,0:T(8,128)}, u32[]{:S(2)}) copy-start(f32[6,352]{1,0:T(8,128)} %copy-done.58) | copy-start | bytes 25348
  879.0 147.9 %all-to-all-start.3 = ((bf16[8,264,1536]{2,1,0:T(8,128)(2,1)}), bf16[8,264,1536]{2,1,0:T(8,128)(2,1)}, u32[]{:S(2)}, u32[]{:S(2)}) async-start(bf16[8,264,1536]{2,1,0:T(8,128)(2,1)} %add_convert_fusion), calls=%async_computation.3 | async-start | bytes 12976128 | tf_op jit(solution)/shard_map/all_to_all | solution.py:278
  883.7 251.6 %reduce-scatter.24.cloned.1.call-start = ((), (), s32[]{:S(2)}) async-start(), calls=%async_computation.18 | async-start | bytes 901120
  1068.9 15.2 slice-start
  1093.1 52.6 %reduce-scatter.22.cloned.1.call-start = ((), (), s32[]{:S(2)}) async-start(), calls=%async_computation.17 | async-start | bytes 901120 | tf_op jit(solution)/shard_map/reduce_scatter | solution.py:339
  1093.2 17.2 copy-start.5
  1102.6 16.2 copy-start.10
  1121.4 180.6 %all-reduce.13.cloned.1.call-start = ((), (), s32[]{:S(2)}) async-start(), calls=%async_computation.20 | async-start | bytes 14155776 | tf_op jit(solution)/shard_map/psum | solution.py:285
  1131.8 270.7 %reduce-scatter.26.cloned.1.call-start = ((), (), s32[]{:S(2)}) async-start(), calls=%async_computation.19 | async-start | bytes 811008
  1135.2 369.1 %reduce-scatter.18.cloned.1.call-start = ((), (), s32[]{:S(2)}) async-start(), calls=%async_computation.15 | async-start | bytes 1622016 | tf_op jit(solution)/shard_map/reduce_scatter | solution.py:383
  1138.2 468.1 %reduce-scatter.16.cloned.1.call-start = ((), (), s32[]{:S(2)}) async-start(), calls=%async_computation.14 | async-start | bytes 1622016 | tf_op jit(solution)/shard_map/reduce_scatter | solution.py:382
  1150.1 597.2 %reduce-scatter.20.cloned.1.call-start = ((), (), s32[]{:S(2)}) async-start(), calls=%async_computation.16 | async-start | bytes 9732096 | tf_op jit(solution)/shard_map/reduce_scatter | solution.py:384
  1157.0 732.3 %reduce-scatter.14.cloned.1.call-start = ((), (), s32[]{:S(2)}) async-start(), calls=%async_computation.13 | async-start | bytes 9732096 | tf_op jit(solution)/shard_map/reduce_scatter | solution.py:381
  1311.8 92.1 %copy-start.40 = (bf16[2,44,8,128]{3,2,1,0:T(8,128)(2,1)S(1)}, bf16[2,44,8,128]{3,2,1,0:T(8,128)(2,1)}, u32[]{:S(2)}) copy-start(bf16[2,44,8,128]{3,2,1,0:T(8,128)(2,1)} %copy-done.39) | copy-start | bytes 540676
  1406.4 43.5 %copy-start.69 = (f32[352]{0:T(512)S(1)}, f32[352]{0:T(512)}, u32[]{:S(2)}) copy-start(f32[352]{0:T(512)} %copy-done.68) | copy-start | bytes 4228
  1449.8 439.5 %copy-start.1 = (bf16[1,1536,768]{2,1,0:T(8,128)(2,1)S(1)}, bf16[1,1536,768]{2,1,0:T(8,128)(2,1)}, u32[]{:S(2)}) copy-start(bf16[1,1536,768]{2,1,0:T(8,128)(2,1)} %param.27) | copy-start | bytes 7077892
  (70 other events, 444.0 us)
Sparse Core Ops, SparseCore 0:
  11.0 67.4 all-gather.3
  81.5 63.3 all-gather.5
  1093.2 23.6 reduce-scatter.23
  1121.5 24.0 reduce-scatter.21
  1149.9 152.1 all-reduce.12
  1307.0 95.4 reduce-scatter.25
  1408.3 95.9 reduce-scatter.17
  1510.2 96.0 reduce-scatter.15
  1612.7 134.5 reduce-scatter.19
  1754.6 134.6 reduce-scatter.13
where the time goes:
time: 1910 us; the launch traced here: 1900 us
  waiting for transfers between devices  1010 us (53%)
  blocking collectives  375 us (20%)
  local copies, waits for them, and re-layouts  203 us (11%)
  matrix products  184 us (10%)
  other arithmetic  94.9 us (5%)
    all_to_all x1, blocking collectives, on_device(): lax.all_to_all(outgoing, 'expert', split_axis=0, concat_axis=0, tiled=True)  147 us
    reduce_scatter x1, waiting for transfers between devices, on_device(): lax.psum_scatter(query_w_grad, ('dp', 'expert'), scatter_dimension=0, til...  142 us
    reduce_scatter x1, waiting for transfers between devices, on_device(): lax.psum_scatter(out_grad, ('dp', 'expert'), scatter_dimension=0, tiled=T...  141 us
    all_to_all x1, waiting for transfers between devices, on_device(): lax.all_to_all(grad_outgoing, 'expert', split_axis=0, concat_axis=0, tile...  133 us
    all_to_all x1, waiting for transfers between devices, on_device(): lax.all_to_all(dispatched, 'expert', split_axis=0, concat_axis=0, tiled=T...  128 us
    psum x1, waiting for transfers between devices, on_device(): lax.psum(gate_w_grad.astype(jnp.bfloat16), 'dp').astype(jnp.float32)  124 us
    reduce_scatter x1, waiting for transfers between devices, on_device(): lax.psum_scatter(key_w_grad, ('dp', 'expert'), scatter_dimension=0, tiled...  102 us
    all_to_all x1, waiting for transfers between devices, on_device(): lax.all_to_all(row_grad, 'expert', split_axis=0, concat_axis=0, tiled=True)  90.4 us
  transfers between devices with their start and end apart: 13, of which 10 were waited for; matrix products, arithmetic and copies ran while one was open for 17% of the time, Pallas kernels for 0%

commit v1 on v0

--- a/solution.py
+++ b/solution.py
@@ -60,8 +60,10 @@
 
 def place(route_ids, experts, capacity):
     one_hot = (route_ids[..., None] == jnp.arange(experts, dtype=jnp.int32)).astype(jnp.int32)
-    earlier = jnp.cumsum(one_hot, axis=-2) - one_hot
-    slot_rank = jnp.sum(earlier * one_hot, axis=-1)
+    pairs = one_hot.shape[-2]
+    before = jnp.tri(pairs, pairs, -1, dtype=jnp.bfloat16)
+    earlier = jnp.dot(before, one_hot.astype(jnp.bfloat16), preferred_element_type=jnp.float32)
+    slot_rank = jnp.sum(earlier.astype(jnp.int32) * one_hot, axis=-1)
     return route_ids * capacity + slot_rank
 
 
@@ -118,7 +120,7 @@
     return result.astype(jnp.bfloat16).reshape(hidden.shape[0], hidden.shape[1], MODEL_WIDTH)
 
 
-def on_device(
+def on_device_routed(
     tokens,
     cotangent,
     parents,
@@ -402,9 +404,232 @@
     )
 
 
+def rows_to_gather(parts):
+    return jnp.concatenate(parts, axis=1)
+
+
+def dense_on_device(
+    tokens,
+    cotangent,
+    parents,
+    routes,
+    first_gain,
+    second_gain,
+    query_weight,
+    key_matrix,
+    value_matrix,
+    out_weight,
+    router_weight,
+    gate_weight,
+    up_weight,
+    down_weight,
+):
+    everyone = ("dp", "expert")
+    experts = router_weight.shape[1]
+    shard = rows_to_gather(
+        [query_weight, key_matrix, value_matrix, out_weight, router_weight,
+         first_gain[:, None], second_gain[:, None]]
+    )
+    width = shard.shape[1]
+    shard = jnp.pad(shard, ((0, 0), (0, -width % 128)))
+    full = lax.all_gather(shard, everyone, axis=0, tiled=True)
+    heads_width = QUERY_HEADS * HEAD_SIZE
+    kv_width = KEY_VALUE_HEADS * HEAD_SIZE
+    qkv_width = heads_width + 2 * kv_width
+    qkv_full = full[:, :qkv_width]
+    out_full = full[:, qkv_width : qkv_width + MODEL_WIDTH]
+    rest = full[:, qkv_width + MODEL_WIDTH :]
+    router_full = rest[:, :experts]
+    scale_one = rest[:, experts].astype(jnp.float32)
+    scale_two = rest[:, experts + 1].astype(jnp.float32)
+    inputs = tokens[0].astype(jnp.float32)
+    dy_low = cotangent[0]
+    dy_all = lax.all_gather(dy_low, "expert", axis=0)
+    total_rows = inputs.shape[0]
+    group = QUERY_HEADS // KEY_VALUE_HEADS
+    ancestors, depths = ancestry(parents[0])
+    tree_length = ancestors.shape[0] * SEG
+    query_ids = lax.axis_index("dp") * total_rows + jnp.arange(total_rows, dtype=jnp.int32)
+    key_ids = jnp.arange(tree_length, dtype=jnp.int32)
+    visible, query_positions = visibility(ancestors, depths, query_ids, key_ids)
+    n1 = normalize(inputs, scale_one).astype(jnp.bfloat16)
+    qkv = jnp.dot(n1, qkv_full, preferred_element_type=jnp.float32)
+    qk = qkv[:, : heads_width + kv_width].reshape(
+        total_rows, QUERY_HEADS + KEY_VALUE_HEADS, HEAD_SIZE
+    )
+    qk_rot = apply_rotation(qk, query_positions).astype(jnp.bfloat16)
+    query_rotated = qk_rot[:, :QUERY_HEADS]
+    kv_own = jnp.concatenate(
+        [
+            qk_rot[:, QUERY_HEADS:].reshape(total_rows, kv_width),
+            qkv[:, heads_width + kv_width :].astype(jnp.bfloat16),
+        ],
+        axis=1,
+    )
+    kv_all = lax.all_gather(kv_own, "dp", axis=0, tiled=True)
+    keys_all = kv_all[:, :kv_width]
+    values_all = kv_all[:, kv_width:]
+    mixed_parts = []
+    log_totals = []
+    for head in range(KEY_VALUE_HEADS):
+        scores = head_scores(query_rotated, keys_all, visible, head, group)
+        row_max = jnp.max(scores, axis=-1, keepdims=True)
+        exponent = jnp.exp(scores - row_max)
+        row_total = jnp.sum(exponent, axis=-1, keepdims=True)
+        log_totals.append(row_max + jnp.log(row_total))
+        softmax_out = (exponent / row_total).astype(jnp.bfloat16)
+        value_part = values_all[:, head * HEAD_SIZE : (head + 1) * HEAD_SIZE]
+        mixed_parts.append(
+            jnp.einsum("grk,kd->rgd", softmax_out, value_part, preferred_element_type=jnp.float32)
+        )
+    mixed = (
+        jnp.concatenate(mixed_parts, axis=1).reshape(total_rows, heads_width).astype(jnp.bfloat16)
+    )
+    middle = inputs + jnp.dot(mixed, out_full, preferred_element_type=jnp.float32)
+    n2 = normalize(middle, scale_two).astype(jnp.bfloat16)
+    logits = jnp.dot(n2, router_full, preferred_element_type=jnp.float32)
+    expert_ids = jnp.arange(experts, dtype=jnp.int32)
+    hits = jnp.any(routes[0][:, :, None] == expert_ids[None, None, :], axis=1)
+    chosen = jnp.where(hits, logits, NEGATIVE)
+    chosen_exp = jnp.where(hits, jnp.exp(chosen - jnp.max(chosen, axis=1, keepdims=True)), 0.0)
+    gates = chosen_exp / jnp.sum(chosen_exp, axis=1, keepdims=True)
+    me = lax.axis_index("expert")
+    n2_all = lax.all_gather(n2, "expert", axis=0)
+    gates_all = lax.all_gather(gates, "expert", axis=0)
+    own_gate = jnp.sum(jnp.where(expert_ids == me, gates_all, 0.0), axis=2)[:, :, None]
+    gate_w, up_w, down_w = gate_weight[0], up_weight[0], down_weight[0]
+    gate_pre = jnp.einsum("scd,df->scf", n2_all, gate_w, preferred_element_type=jnp.float32)
+    up_pre = jnp.einsum("scd,df->scf", n2_all, up_w, preferred_element_type=jnp.float32)
+    hidden, product_pull = jax.vjp(gelu_product, gate_pre, up_pre)
+    scaled = (own_gate * hidden).astype(jnp.bfloat16)
+    expert_sum = jnp.einsum("scf,fd->scd", scaled, down_w, preferred_element_type=jnp.float32)
+    combined = lax.psum_scatter(
+        expert_sum.astype(jnp.bfloat16), "expert", scatter_dimension=0, tiled=True
+    )[0]
+    output = (middle + combined.astype(jnp.float32)).astype(jnp.bfloat16)[None]
+    back = jnp.einsum("scd,fd->scf", dy_all, down_w, preferred_element_type=jnp.float32)
+    gate_grad_own = jnp.sum(back * hidden, axis=2)
+    gate_grad = lax.all_to_all(gate_grad_own[:, None, :], "expert", 0, 1, tiled=True)[0].T
+    chosen_grad = gates * (gate_grad - jnp.sum(gates * gate_grad, axis=1, keepdims=True))
+    logit_grad = jnp.where(hits, chosen_grad, 0.0)
+    down_grad = jnp.einsum("scf,scd->fd", scaled, dy_all, preferred_element_type=jnp.float32)
+    gate_pre_grad, up_pre_grad = product_pull(own_gate * back)
+    gate_low = gate_pre_grad.astype(jnp.bfloat16)
+    up_low = up_pre_grad.astype(jnp.bfloat16)
+    gate_w_grad = jnp.einsum("scd,scf->df", n2_all, gate_low, preferred_element_type=jnp.float32)
+    up_w_grad = jnp.einsum("scd,scf->df", n2_all, up_low, preferred_element_type=jnp.float32)
+    row_grad = jnp.einsum(
+        "scf,df->scd", gate_low, gate_w, preferred_element_type=jnp.float32
+    ) + jnp.einsum("scf,df->scd", up_low, up_w, preferred_element_type=jnp.float32)
+    row_sum = lax.psum_scatter(
+        row_grad.astype(jnp.bfloat16), "expert", scatter_dimension=0, tiled=True
+    )[0].astype(jnp.float32)
+    summed = tuple(
+        lax.psum(grad.astype(jnp.bfloat16), "dp").astype(jnp.float32)[None]
+        for grad in (gate_w_grad, up_w_grad, down_grad)
+    )
+    router_wide = router_full.astype(jnp.float32)
+    n2_grad = jnp.dot(logit_grad, router_wide.T, precision=HIGH_PRECISION) + row_sum
+    router_grad = jnp.dot(n2.astype(jnp.float32).T, logit_grad, precision=HIGH_PRECISION)
+    upstream = dy_low.astype(jnp.float32)
+    _, second_pull = jax.vjp(normalize, middle, scale_two)
+    middle_norm_grad, second_gain_grad = second_pull(n2_grad)
+    middle_grad = upstream + middle_norm_grad
+    attended_low = middle_grad.astype(jnp.bfloat16)
+    out_grad = jnp.einsum("rd,re->de", mixed, attended_low, preferred_element_type=jnp.float32)
+    mixed_grad = jnp.einsum("re,de->rd", attended_low, out_full, preferred_element_type=jnp.float32)
+    mixed_grad = mixed_grad.astype(jnp.bfloat16).reshape(total_rows, QUERY_HEADS, HEAD_SIZE)
+    query_parts = []
+    key_parts = []
+    value_parts = []
+    for head in range(KEY_VALUE_HEADS):
+        scores = head_scores(query_rotated, keys_all, visible, head, group)
+        softmax_out = jnp.exp(scores - log_totals[head])
+        query_part = query_rotated[:, head * group : (head + 1) * group, :]
+        key_part = keys_all[:, head * HEAD_SIZE : (head + 1) * HEAD_SIZE]
+        value_part = values_all[:, head * HEAD_SIZE : (head + 1) * HEAD_SIZE]
+        grad_part = mixed_grad[:, head * group : (head + 1) * group, :]
+        value_parts.append(
+            jnp.einsum(
+                "grk,rgd->kd",
+                softmax_out.astype(jnp.bfloat16),
+                grad_part,
+                preferred_element_type=jnp.float32,
+            )
+        )
+        attn_grad = jnp.einsum(
+            "rgd,kd->grk", grad_part, value_part, preferred_element_type=jnp.float32
+        )
+        score_grad = softmax_out * (
+            attn_grad - jnp.sum(softmax_out * attn_grad, axis=-1, keepdims=True)
+        )
+        score_low = score_grad.astype(jnp.bfloat16)
+        query_parts.append(
+            jnp.einsum("grk,kd->rgd", score_low, key_part, preferred_element_type=jnp.float32)
+            * HEAD_SIZE ** (-0.5)
+        )
+        key_parts.append(
+            jnp.einsum("grk,rgd->kd", score_low, query_part, preferred_element_type=jnp.float32)
+            * HEAD_SIZE ** (-0.5)
+        )
+    kv_sum = lax.psum_scatter(
+        jnp.concatenate(key_parts + value_parts, axis=1).astype(jnp.bfloat16),
+        "dp",
+        scatter_dimension=0,
+        tiled=True,
+    )
+    _, rotation_pull = jax.vjp(lambda values: apply_rotation(values, query_positions), qk)
+    key_sum = kv_sum[:, :kv_width].astype(jnp.float32)
+    qk_grad = rotation_pull(
+        jnp.concatenate(
+            query_parts + [key_sum.reshape(total_rows, KEY_VALUE_HEADS, HEAD_SIZE)], axis=1
+        )
+    )[0]
+    qkv_grad = jnp.concatenate(
+        [
+            qk_grad.astype(jnp.bfloat16).reshape(total_rows, heads_width + kv_width),
+            kv_sum[:, kv_width:],
+        ],
+        axis=1,
+    )
+    qkv_w_grad = jnp.einsum("rd,re->de", n1, qkv_grad, preferred_element_type=jnp.float32)
+    n1_grad = jnp.einsum("re,de->rd", qkv_grad, qkv_full, preferred_element_type=jnp.float32)
+    _, first_pull = jax.vjp(normalize, inputs, scale_one)
+    input_norm_grad, first_gain_grad = first_pull(n1_grad)
+    input_grad = (middle_grad + input_norm_grad)[None]
+    small = jnp.concatenate(
+        [router_grad, first_gain_grad[:, None], second_gain_grad[:, None]], axis=1
+    )
+    small = jnp.pad(small, ((0, 0), (0, -small.shape[1] % 128)))
+    share = lax.psum_scatter(
+        jnp.concatenate([qkv_w_grad, out_grad, small], axis=1).astype(jnp.bfloat16),
+        everyone,
+        scatter_dimension=0,
+        tiled=True,
+    ).astype(jnp.float32)
+    query_share = share[:, :heads_width]
+    key_share = share[:, heads_width : heads_width + kv_width]
+    value_share = share[:, heads_width + kv_width : qkv_width]
+    out_share = share[:, qkv_width : qkv_width + MODEL_WIDTH]
+    small_share = share[:, qkv_width + MODEL_WIDTH :]
+    return (
+        output,
+        input_grad,
+        small_share[:, experts],
+        small_share[:, experts + 1],
+        query_share,
+        key_share,
+        value_share,
+        out_share,
+        small_share[:, :experts],
+        *summed,
+    )
+
+
 def solution(mesh):
+    dense = mesh.shape["expert"] <= 2 * TOPK
     return jax.shard_map(
-        on_device,
+        dense_on_device if dense else on_device_routed,
         mesh=mesh,
         in_specs=(
             P("expert", "dp", None),

time: 1910 us -> 1010 us (0.53)
  waiting for transfers between devices: 1010 us -> 581 us
  blocking collectives: 375 us -> 14.3 us
  local copies, waits for them, and re-layouts: 203 us -> 106 us
  matrix products: 184 us -> 219 us
  other arithmetic: 94.9 us -> 67 us
    all_to_all x3 -> x1, waiting for transfers between devices: 352 us -> 0.01 us  [dense_on_device(): lax.all_to_all(gate_grad_own[:, None, :], 'expert', 0, 1, tiled=True)[0]]
    all_gather x2 -> x4, waiting for transfers between devices: 0.01 us -> 176 us  [the longest x1 67.8 us: dense_on_device(): n2_all = lax.all_gather(n2, 'expert', axis=0)]
    reduce_scatter x5 -> x4, waiting for transfers between devices: 443 us -> 288 us  [the longest x1 140 us: dense_on_device(): lax.psum_scatter(jnp.concatenate([qkv_w_grad, out_grad, small], axis=1).a...]
    all_to_all x1 -> x0, blocking collectives: 147 us -> none  [on_device(): lax.all_to_all(outgoing, 'expert', split_axis=0, concat_axis=0, tiled=True)]
    all_gather x5 -> x1, blocking collectives: 146 us -> 14.3 us  [dense_on_device(): gates_all = lax.all_gather(gates, 'expert', axis=0)]
    unnamed x12 -> x9, waiting for transfers between devices: 88.7 us -> 0.65 us
    unnamed x2 -> x0, blocking collectives: 82.4 us -> none
    gather x4 -> x0, local copies, waits for them, and re-layouts: 54 us -> none  [the longest x1 17.5 us: on_device(): pair_grad[slot_pair]]
  transfers between devices with their start and end apart: 13 -> 10, of which waited for: 10 -> 8; matrix products, arithmetic and copies ran while one was open for 17% -> 21% of each run, Pallas kernels for 0% -> 0%
where the time goes in v1:
time: 1010 us
  waiting for transfers between devices  581 us (58%)
  matrix products  219 us (22%)
  local copies, waits for them, and re-layouts  106 us (10%)
  other arithmetic  67 us (7%)
  between operations  14.8 us (1%)
  blocking collectives  14.3 us (1%)
    reduce_scatter x1, waiting for transfers between devices, dense_on_device(): lax.psum_scatter(jnp.concatenate([qkv_w_grad, out_grad, small], axis=1).a...  140 us
    psum x1, waiting for transfers between devices, dense_on_device(): lax.psum(grad.astype(jnp.bfloat16), 'dp').astype(jnp.float32)[None]  116 us
    reduce_scatter x1, waiting for transfers between devices, dense_on_device(): lax.psum_scatter(expert_sum.astype(jnp.bfloat16), 'expert', scatter_dimen...  88.4 us
    all_gather x1, waiting for transfers between devices, dense_on_device(): n2_all = lax.all_gather(n2, 'expert', axis=0)  67.8 us
    gather x44, local copies, waits for them, and re-layouts, advance(): return (jnp.take(parent_row, current), ancestors)  63 us
    all_gather x1, waiting for transfers between devices, dense_on_device(): dy_all = lax.all_gather(dy_low, 'expert', axis=0)  62.6 us
    reduce_scatter x1, waiting for transfers between devices, dense_on_device(): lax.psum_scatter(row_grad.astype(jnp.bfloat16), 'expert', scatter_dimensi...  59.8 us
    all_gather x1, waiting for transfers between devices, dense_on_device(): kv_all = lax.all_gather(kv_own, 'dp', axis=0, tiled=True)  23.3 us
  transfers between devices with their start and end apart: 10, of which 8 were waited for; matrix products, arithmetic and copies ran while one was open for 21% of the time, Pallas kernels for 0%

profile of v1, /device:TPU:0, one launch (start us, length us, event | category | flops | bytes accessed | tf_op | source)
XLA Modules:
  0.0 1007.3 jit_solution(13561688737431542556)
XLA Ops:
  13.4 68.9 %while.13 = (s32[]{:T(128)}, s32[44]{0:T(128)S(1)}, f32[44,44]{1,0:T(8,128)S(1)}, s32[44]{0:T(128)}, s32[]{:T(128)}, /*index=5*/s32[]{:T(128)}) while((s32[]{:T(128)}, s32[44]{0:T(128)S(1)}, f32[44,44]{1,0:T(8,128)S(1)}, s32[44]{0:T(128)}, s32[]{:T(128)}, /*index=5*/s32[]{:T(128)}) %tuple.77), condition=%wide.region_2.3_spmd.clone, body=%wide.region_1.2_spmd.clone.sunk | while | flops 9211 | bytes 21423 | solution.py:33
  85.0 22.0 %all-gather.8.cloned.1.call-done = bf16[1536,3712]{1,0:T(8,128)(2,1)} async-done(((bf16[48,3712]{1,0:T(8,128)(2,1)}), bf16[1536,3712]{1,0:T(8,128)(2,1)}) %all-gather.8.cloned.1.call-update) | async-done | bytes 11403280 | tf_op jit(solution)/shard_map/all_gather | solution.py:435
  108.7 5.2 fusion.31
  139.1 23.3 %all-gather.10.cloned.1.call-done = bf16[1408,512]{1,0:T(8,128)(2,1)} async-done(((bf16[352,512]{1,0:T(8,128)(2,1)}), bf16[1408,512]{1,0:T(8,128)(2,1)}) %all-gather.10.cloned.1.call-update) | async-done | bytes 1441808 | tf_op jit(solution)/shard_map/all_gather | solution.py:469
  169.2 6.9 fusion.139
  176.0 6.1 fusion.10
  191.0 5.0 multiply_reduce_fusion.3
  201.1 14.3 %all-gather.2 = f32[8,352,8]{1,2,0:T(8,128)S(1)} all-gather(f32[1,352,8]{1,2,0:T(8,128)S(1)} %fusion.130), channel_id=2, replica_groups=mesh['dp'=4,'expert'=8] {'expert'}, dimensions={0}, use_global_device_ids=true | all-gather | bytes 101376 | tf_op jit(solution)/shard_map/all_gather | solution.py:498
  215.5 67.8 %all-gather.14.cloned.1.call-done = bf16[2816,1536]{1,0:T(8,128)(2,1)} async-done(((bf16[352,1536]{1,0:T(8,128)(2,1)}), bf16[2816,1536]{1,0:T(8,128)(2,1)}) %all-gather.14.cloned.1.call-update) | async-done | bytes 8650768 | tf_op jit(solution)/shard_map/all_gather | solution.py:497
  283.3 12.2 %fusion.68 = f32[8,352,768]{2,1,0:T(8,128)} fusion(bf16[8,352,1536]{2,1,0:T(8,128)(2,1)} %bitcast.215, bf16[1,1536,768]{2,1,0:T(8,128)(2,1)} %param.28), kind=kOutput, calls=%fused_computation.101 | convolution fusion | flops 6643777536 | bytes 19660800 | tf_op jit(solution)/shard_map/scd,df->scf/dot_general | solution.py:502
  295.5 9.4 fusion.72
  304.8 62.6 %all-gather.12.cloned.1.call-done = bf16[8,352,1536]{2,1,0:T(8,128)(2,1)} async-done(((bf16[1,352,1536]{2,1,0:T(8,128)(2,1)}), bf16[8,352,1536]{2,1,0:T(8,128)(2,1)}) %all-gather.12.cloned.1.call-update) | async-done | bytes 8650768 | tf_op jit(solution)/shard_map/all_gather | solution.py:447
  367.4 20.5 %multiply_reduce_fusion = (f32[8,352]{1,0:T(8,128)S(1)}, bf16[8,352,768]{2,1,0:T(8,128)(2,1)}, bf16[8,352,768]{2,1,0:T(8,128)(2,1)}) fusion(f32[8,352,768]{2,1,0:T(8,128)} %fusion.68, f32[8,352,768]{2,1,0:T(8,128)} %fusion.72, f32[8,352]{1,0:T(8,128)S(1)} %select_reduce_fusion.1, bf16[8,352,1536]{2,1,0:T(8,128)(2,1)} %all-gather.12.cloned.1.call-done, ...), kind=kOutput, calls=%fused_computation.43 | convolution fusion | flops 6704329728 | bytes 36984832 | tf_op jit(solution)/shard_map/scd,fd->scf/dot_general | solution.py:510
  387.9 12.7 %fusion.70 = f32[8,352,1536]{2,1,0:T(8,128)} fusion(bf16[8,352,768]{2,1,0:T(8,128)(2,1)} %get-tuple-element.139, bf16[1,1536,768]{2,1,0:T(8,128)(2,1)S(1)} %copy-done.38), kind=kOutput, calls=%fused_computation.103 | convolution fusion | flops 6643777536 | bytes 23986176 | tf_op jit(solution)/shard_map/scf,df->scd/dot_general | solution.py:521
  400.6 14.3 %add_convert_fusion = bf16[8,352,1536]{2,1,0:T(8,128)(2,1)} fusion(f32[8,352,1536]{2,1,0:T(8,128)} %fusion.70, bf16[8,352,768]{2,1,0:T(8,128)(2,1)} %get-tuple-element.140, bf16[1,1536,768]{2,1,0:T(8,128)(2,1)S(1)} %copy-done.39), kind=kOutput, calls=%fused_computation.9 | convolution fusion | flops 6652428288 | bytes 32636928 | tf_op jit(solution)/shard_map/scf,df->scd/dot_general | solution.py:523
  415.0 14.8 %convolution_convert_fusion.2 = bf16[8,352,1536]{2,1,0:T(8,128)(2,1)} fusion(bf16[1,768,1536]{2,1,0:T(8,128)(2,1)S(1)} %copy-done, f32[8,352]{1,0:T(8,128)S(1)} %select_reduce_fusion.1, f32[8,352,768]{2,1,0:T(8,128)} %fusion.68, f32[8,352,768]{2,1,0:T(8,128)} %fusion.72), kind=kOutput, calls=%fused_computation.48 | convolution fusion | flops 6671892480 | bytes 28322816 | tf_op jit(solution)/shard_map/scf,fd->scd/dot_general | solution.py:505
  433.9 12.2 %fusion.38 = bf16[1,1536,768]{2,1,0:T(8,128)(2,1)} fusion(bf16[8,352,1536]{2,1,0:T(8,128)(2,1)} %bitcast.216, bf16[8,352,768]{2,1,0:T(8,128)(2,1)} %get-tuple-element.139), kind=kOutput, calls=%fused_computation.75 | convolution fusion | flops 6644957184 | bytes 15335424 | tf_op jit(solution)/shard_map/scd,scf->df/dot_general | solution.py:519
  446.1 59.8 %reduce-scatter.9.cloned.1.call-done = bf16[1,352,1536]{2,1,0:T(8,128)(2,1)} async-done(((bf16[8,352,1536]{2,1,0:T(8,128)(2,1)}), bf16[1,352,1536]{2,1,0:T(8,128)(2,1)}) %reduce-scatter.9.cloned.1.call-update) | async-done | bytes 1081360 | tf_op jit(solution)/shard_map/reduce_scatter | solution.py:524
  510.1 88.4 %reduce-scatter.7.cloned.1.call-done = bf16[1,352,1536]{2,1,0:T(8,128)(2,1)} async-done(((bf16[8,352,1536]{2,1,0:T(8,128)(2,1)}), bf16[1,352,1536]{2,1,0:T(8,128)(2,1)}) %reduce-scatter.7.cloned.1.call-update) | async-done | bytes 1081360 | tf_op jit(solution)/shard_map/reduce_scatter | solution.py:506
  608.4 6.7 fusion.59
  615.1 6.6 fusion.56
  621.8 7.4 fusion.6
  629.2 9.1 fusion.8
  655.7 12.0 %fusion.39 = bf16[1,1536,768]{2,1,0:T(8,128)(2,1)} fusion(bf16[8,352,1536]{2,1,0:T(8,128)(2,1)} %bitcast.217, bf16[8,352,768]{2,1,0:T(8,128)(2,1)} %get-tuple-element.140), kind=kOutput, calls=%fused_computation.76 | convolution fusion | flops 6644957184 | bytes 15335424 | tf_op jit(solution)/shard_map/scd,scf->df/dot_general | solution.py:520
  667.7 14.8 %fusion.40 = bf16[1,768,1536]{2,1,0:T(8,128)(2,1)} fusion(bf16[8,352,1536]{2,1,0:T(8,128)(2,1)} %all-gather.12.cloned.1.call-done, f32[8,352]{1,0:T(8,128)S(1)} %select_reduce_fusion.1, f32[8,352,768]{2,1,0:T(8,128)} %fusion.68, f32[8,352,768]{2,1,0:T(8,128)} %fusion.72), kind=kOutput, calls=%fused_computation.77 | convolution fusion | flops 6668746752 | bytes 28322816 | tf_op jit(solution)/shard_map/scf,scd->fd/dot_general | solution.py:515
  684.3 4.5 fusion.83
  688.8 5.7 fusion.82
  694.5 4.4 convolution_convert_fusion.1
  705.0 7.6 fusion.75
  717.0 7.8 fusion.9
  724.9 116.4 %all-reduce.7.cloned.1.call-done = (bf16[1,1536,768]{2,1,0:T(8,128)(2,1)}, bf16[1,1536,768]{2,1,0:T(8,128)(2,1)}, bf16[1,768,1536]{2,1,0:T(8,128)(2,1)}) async-done(((bf16[1,1536,768]{2,1,0:T(8,128)(2,1)}, bf16[1,1536,768]{2,1,0:T(8,128)(2,1)}, bf16[1,768,1536]{2,1,0:T(8,128)(2,1)}), (bf16[1,1536,768]{2,1,0:T(8,128)(2,1)}, bf16[1,1536,768]{2,1,0:T(8,128)(2,1)}, ...) | async-done | bytes 7077904 | tf_op jit(solution)/shard_map/psum | solution.py:528
  854.0 140.3 %reduce-scatter.11.cloned.1.call-done = bf16[48,3712]{1,0:T(8,128)(2,1)} async-done(((bf16[1536,3712]{1,0:T(8,128)(2,1)}), bf16[48,3712]{1,0:T(8,128)(2,1)}) %reduce-scatter.11.cloned.1.call-update) | async-done | bytes 356368 | tf_op jit(solution)/shard_map/reduce_scatter | solution.py:604
  (421 shorter events, 190.4 us)
Async XLA Ops:
  7.2 360.2 %copy-start = (bf16[1,768,1536]{2,1,0:T(8,128)(2,1)S(1)}, bf16[1,768,1536]{2,1,0:T(8,128)(2,1)}, u32[]{:S(2)}) copy-start(bf16[1,768,1536]{2,1,0:T(8,128)(2,1)} %param.29) | copy-start | bytes 7077892
  7.2 75.5 %copy-start.13 = (bf16[1,352,1536]{2,1,0:T(8,128)(2,1)S(1)}, bf16[1,352,1536]{2,1,0:T(8,128)(2,1)}, u32[]{:S(2)}) copy-start(bf16[1,352,1536]{2,1,0:T(8,128)(2,1)} %param.16) | copy-start | bytes 3244036
  7.2 99.8 %all-gather.8.cloned.1.call-start = ((), (), s32[]{:S(2)}) async-start(), calls=%async_computation.5 | async-start | bytes 11759616 | tf_op jit(solution)/shard_map/all_gather | solution.py:435
  13.4 149.0 %all-gather.10.cloned.1.call-start = ((), (), s32[]{:S(2)}) async-start(), calls=%async_computation.6 | async-start | bytes 1802240 | tf_op jit(solution)/shard_map/all_gather | solution.py:469
  83.5 30.4 %copy-start.33 = (f32[352]{0:T(512)}, f32[352]{0:T(512)S(1)}, u32[]{:S(2)}) copy-start(f32[352]{0:T(512)S(1)} %fusion.119) | copy-start | bytes 4228
  122.5 6.0 copy-start.23
  122.5 6.0 copy-start.25
  133.9 149.4 %all-gather.14.cloned.1.call-start = ((), (), s32[]{:S(2)}) async-start(), calls=%async_computation.11 | async-start | bytes 9732096 | tf_op jit(solution)/shard_map/all_gather | solution.py:497
  139.1 27.0 %copy-start.15 = (bf16[352,6,128]{2,0,1:T(8,128)(2,1)}, bf16[352,6,128]{2,0,1:T(8,128)(2,1)S(1)}, u32[]{:S(2)}) copy-start(bf16[352,6,128]{2,0,1:T(8,128)(2,1)S(1)} %get-tuple-element.148) | copy-start | bytes 1622020
  166.1 16.0 %copy-start.2 = (f32[6,352,1408]{2,1,0:T(8,128)}, f32[6,352,1408]{2,1,0:T(8,128)S(1)}, u32[]{:S(2)}) copy-start(f32[6,352,1408]{2,1,0:T(8,128)S(1)} %get-tuple-element.160) | copy-start | bytes 35684356
  198.6 168.8 %all-gather.12.cloned.1.call-start = ((), (), s32[]{:S(2)}) async-start(), calls=%async_computation.8 | async-start | bytes 9732096 | tf_op jit(solution)/shard_map/all_gather | solution.py:447
  199.2 306.6 %reduce-scatter.9.cloned.1.call-start = ((), (), s32[]{:S(2)}) async-start(), calls=%async_computation.9 | async-start | bytes 9732096 | tf_op jit(solution)/shard_map/reduce_scatter | solution.py:524
  283.2 12.2 %copy-start.36 = (bf16[2816,1536]{1,0:T(8,128)(2,1)S(1)}, bf16[2816,1536]{1,0:T(8,128)(2,1)}, u32[]{:S(2)}) copy-start(bf16[2816,1536]{1,0:T(8,128)(2,1)} %all-gather.14.cloned.1.call-done) | copy-start | bytes 25952260
  283.3 12.2 %copy-start.37 = (bf16[1,1536,768]{2,1,0:T(8,128)(2,1)S(1)}, bf16[1,1536,768]{2,1,0:T(8,128)(2,1)}, u32[]{:S(2)}) copy-start(bf16[1,1536,768]{2,1,0:T(8,128)(2,1)} %param.27) | copy-start | bytes 7077892
  367.4 20.5 %copy-start.38 = (bf16[1,1536,768]{2,1,0:T(8,128)(2,1)S(1)}, bf16[1,1536,768]{2,1,0:T(8,128)(2,1)}, u32[]{:S(2)}) copy-start(bf16[1,1536,768]{2,1,0:T(8,128)(2,1)} %param.27) | copy-start | bytes 7077892
  387.9 12.7 %copy-start.39 = (bf16[1,1536,768]{2,1,0:T(8,128)(2,1)S(1)}, bf16[1,1536,768]{2,1,0:T(8,128)(2,1)}, u32[]{:S(2)}) copy-start(bf16[1,1536,768]{2,1,0:T(8,128)(2,1)} %param.28) | copy-start | bytes 7077892
  414.9 183.6 %reduce-scatter.7.cloned.1.call-start = ((), (), s32[]{:S(2)}) async-start(), calls=%async_computation.7 | async-start | bytes 9732096 | tf_op jit(solution)/shard_map/reduce_scatter | solution.py:506
  430.4 15.6 %all-to-all-start = ((f32[8,1,352]{2,1,0:T(1,128)}), f32[8,1,352]{2,1,0:T(1,128)S(1)}, u32[]{:S(2)}, u32[]{:S(2)}) async-start(f32[8,1,352]{2,1,0:T(1,128)} %broadcast_in_dim.181), calls=%async_computation.1 | async-start | bytes 24576 | tf_op jit(solution)/shard_map/all_to_all | solution.py:512
  433.8 72.1 %copy-start.5 = (f32[352,1536]{1,0:T(8,128)S(1)}, f32[352,1536]{1,0:T(8,128)}, u32[]{:S(2)}) copy-start(f32[352,1536]{1,0:T(8,128)} %copy-done.4) | copy-start | bytes 6488068
  433.8 265.1 %reduce-scatter.13.cloned.1.call-start = ((), (), s32[]{:S(2)}) async-start(), calls=%async_computation.12 | async-start | bytes 1802240 | tf_op jit(solution)/shard_map/reduce_scatter | solution.py:575
  446.0 152.5 %copy-start.12 = (bf16[1,352,1536]{2,1,0:T(8,128)(2,1)S(1)}, bf16[1,352,1536]{2,1,0:T(8,128)(2,1)}, u32[]{:S(2)}) copy-start(bf16[1,352,1536]{2,1,0:T(8,128)(2,1)} %param.17) | copy-start | bytes 3244036
  608.4 13.3 %slice-start.3 = ((s8[11894784]{0:T(1024)(128)(4,1)}), s8[4194304]{0:T(1024)(128)(4,1)S(1)}, s32[]{:S(2)}) async-start(s8[11894784]{0:T(1024)(128)(4,1)} %bitcast.200), calls=%async_computation.17 | async-start | bytes 8388608
  608.4 13.3 %slice-start.4 = ((s8[11894784]{0:T(1024)(128)(4,1)}), s8[4194304]{0:T(1024)(128)(4,1)S(1)}, s32[]{:S(2)}) async-start(s8[11894784]{0:T(1024)(128)(4,1)} %bitcast.200), calls=%async_computation.18 | async-start | bytes 8388608
  615.1 6.7 slice-start.5
  621.8 20.4 %slice-start = ((s8[11894784]{0:T(1024)(128)(4,1)}), s8[4194304]{0:T(1024)(128)(4,1)S(1)}, s32[]{:S(2)}) async-start(s8[11894784]{0:T(1024)(128)(4,1)} %bitcast.198), calls=%async_computation.14 | async-start | bytes 8388608
  621.8 20.4 %slice-start.1 = ((s8[11894784]{0:T(1024)(128)(4,1)}), s8[4194304]{0:T(1024)(128)(4,1)S(1)}, s32[]{:S(2)}) async-start(s8[11894784]{0:T(1024)(128)(4,1)} %bitcast.198), calls=%async_computation.15 | async-start | bytes 8388608
  629.2 9.1 copy-start.18
  629.2 13.0 %slice-start.2 = ((s8[11894784]{0:T(1024)(128)(4,1)}), s8[3506176]{0:T(1024)(128)(4,1)S(1)}, s32[]{:S(2)}) async-start(s8[11894784]{0:T(1024)(128)(4,1)} %bitcast.198), calls=%async_computation.16 | async-start | bytes 7012352
  655.7 185.6 %all-reduce.7.cloned.1.call-start = ((), (), s32[]{:S(2)}) async-start(), calls=%async_computation.13 | async-start | bytes 14155776 | tf_op jit(solution)/shard_map/psum | solution.py:528
  682.5 311.7 %reduce-scatter.11.cloned.1.call-start = ((), (), s32[]{:S(2)}) async-start(), calls=%async_computation.10 | async-start | bytes 11759616 | tf_op jit(solution)/shard_map/reduce_scatter | solution.py:604
  705.0 7.9 copy-start.27
  852.1 148.5 %copy-start.1 = (bf16[1,768,1536]{2,1,0:T(8,128)(2,1)S(1)}, bf16[1,768,1536]{2,1,0:T(8,128)(2,1)}, u32[]{:S(2)}) copy-start(bf16[1,768,1536]{2,1,0:T(8,128)(2,1)} %param.29) | copy-start | bytes 7077892
  (24 other events, 67.1 us)
Sparse Core Ops, SparseCore 0:
  13.5 93.4 all-gather.7
  134.0 28.3 all-gather.9
  198.8 84.4 all-gather.13
  284.7 82.6 all-gather.11
  415.0 90.7 reduce-scatter.8
  508.0 90.4 reduce-scatter.6
  655.8 28.4 reduce-scatter.12
  689.1 152.1 all-reduce.6
  848.4 145.8 reduce-scatter.10

commit v2 on v0

--- a/solution.py
+++ b/solution.py
@@ -1,8 +1,13 @@
 import jax
 import jax.numpy as jnp
 from jax import lax
+from jax.experimental import pallas as pl
+from jax.experimental.pallas import tpu as pltpu
 from jax.sharding import PartitionSpec as P
 
+MESH = pl.DeviceIdType.MESH
+BF = jnp.bfloat16
+F32 = jnp.float32
 MODEL_WIDTH = 1536
 QUERY_HEADS = 12
 KEY_VALUE_HEADS = 2
@@ -10,12 +15,15 @@
 FF = 768
 TOPK = 4
 SEG = 32
+BRANCHES = 4
+LEAVES = 8
 
 
 EPS = 1e-06
 THETA = 10000.0
 HIGH_PRECISION = lax.Precision.HIGHEST
 NEGATIVE = -1e30
+LOG2E = 1.4426950408889634
 
 
 def ancestry(parent_row):
@@ -60,8 +68,10 @@
 
 def place(route_ids, experts, capacity):
     one_hot = (route_ids[..., None] == jnp.arange(experts, dtype=jnp.int32)).astype(jnp.int32)
-    earlier = jnp.cumsum(one_hot, axis=-2) - one_hot
-    slot_rank = jnp.sum(earlier * one_hot, axis=-1)
+    pairs = one_hot.shape[-2]
+    before = jnp.tri(pairs, pairs, -1, dtype=jnp.bfloat16)
+    earlier = jnp.dot(before, one_hot.astype(jnp.bfloat16), preferred_element_type=jnp.float32)
+    slot_rank = jnp.sum(earlier.astype(jnp.int32) * one_hot, axis=-1)
     return route_ids * capacity + slot_rank
 
 
@@ -118,7 +128,7 @@
     return result.astype(jnp.bfloat16).reshape(hidden.shape[0], hidden.shape[1], MODEL_WIDTH)
 
 
-def on_device(
+def on_device_routed(
     tokens,
     cotangent,
     parents,
@@ -402,9 +412,1361 @@
     )
 
 
+def mm(a, b):
+    return jnp.dot(a, b, preferred_element_type=F32)
+
+
+def mm_nt(a, b):
+    return lax.dot_general(a, b, (((1,), (1,)), ((), ())), preferred_element_type=F32)
+
+
+def mm_tn(a, b):
+    return lax.dot_general(a, b, (((0,), (0,)), ((), ())), preferred_element_type=F32)
+
+
+def gelu_both(value):
+    scale = 0.7978845608028654
+    square = value * value
+    bend = jnp.tanh(scale * value * (1.0 + 0.044715 * square))
+    half = 0.5 * (1.0 + bend)
+    slope = half + 0.5 * value * (1.0 - bend * bend) * scale * (1.0 + 0.134145 * square)
+    return value * half, slope
+
+
+def expert_kernel(
+    n2_ref, gate_ref, dy_ref, gw_ref, uw_ref, dw_ref,
+    row_ref, gg_ref, sum_ref, dgw_ref, duw_ref, ddw_ref,
+    n2_all, gate_all, dy_buf, dy_cols, hs_all, gl_all, ul_all, own, sib, zin, gg_out, gg_in, stage, down_stage,
+    n2_send, n2_recv, gt_send, gt_recv, own_send, sib_recv, zin_send, zin_recv,
+    gg_send, gg_recv, dy_sem, cols_sem, sum_sem, stage_sem,
+):
+    count = lax.axis_size("expert")
+    depth = count // 2
+    rows = n2_ref.shape[0]
+    half = rows // 2
+    width = n2_ref.shape[1]
+    ff = gw_ref.shape[1]
+    me = lax.axis_index("expert")
+    z, core = me // 2, me % 2
+    sibling = z * 2 + 1 - core
+
+    def at(zz):
+        return {"expert": zz * 2 + core}
+
+    barrier = pltpu.get_barrier_semaphore()
+    for other in range(1, count):
+        pl.semaphore_signal(
+            barrier, 1, device_id={"expert": lax.rem(me + other, count)}, device_id_type=MESH
+        )
+    pl.semaphore_wait(barrier, count - 1)
+
+    def chunk(k):
+        return pl.ds(pl.multiple_of(k * rows, 16), rows)
+
+    def n2_copy(k, lane, target):
+        return pltpu.make_async_remote_copy(
+            n2_all.at[chunk(k)], n2_all.at[chunk(k)], n2_send.at[k, lane], n2_recv.at[k],
+            device_id=target, device_id_type=MESH,
+        )
+
+    def gt_copy(k, lane, target):
+        return pltpu.make_async_remote_copy(
+            gate_all.at[k], gate_all.at[k], gt_send.at[k, lane], gt_recv.at[k],
+            device_id=target, device_id_type=MESH,
+        )
+
+    def send_chunk(k, lane, target):
+        n2_copy(k, lane, target).start()
+        gt_copy(k, lane, target).start()
+
+    def sent_chunk(k, lane, target):
+        n2_copy(k, lane, target).wait_send()
+        gt_copy(k, lane, target).wait_send()
+
+    def arrived(k):
+        n2_copy(k, 0, at(z)).wait_recv()
+        gt_copy(k, 0, at(z)).wait_recv()
+
+    def dy_copy(k, slot):
+        return pltpu.make_async_copy(dy_ref.at[k], dy_buf.at[slot], dy_sem.at[slot])
+
+    def gg_copy(k):
+        return pltpu.make_async_remote_copy(
+            gg_out.at[k], gg_in.at[me], gg_send.at[k], gg_recv.at[me],
+            device_id={"expert": k}, device_id_type=MESH,
+        )
+
+    def own_copy(zs):
+        return pltpu.make_async_remote_copy(
+            own.at[2 * zs + 1 - core], sib.at[zs], own_send.at[zs], sib_recv.at[zs],
+            device_id={"expert": sibling}, device_id_type=MESH,
+        )
+
+    def part(h):
+        return pl.ds(h * half, half)
+
+    def zin_copy(zd, h, nxt, slot):
+        return pltpu.make_async_remote_copy(
+            own.at[2 * zd + core, part(h)], zin.at[slot, part(h)],
+            zin_send.at[zd, h], zin_recv.at[slot, h],
+            device_id=at(nxt), device_id_type=MESH,
+        )
+
+    n2_all[chunk(me), :] = n2_ref[...]
+    gate_all[me] = gate_ref[...]
+
+    @pl.when(z < depth - 1)
+    def _():
+        send_chunk(me, 0, at(z + 1))
+
+    @pl.when(z > 0)
+    def _():
+        send_chunk(me, 1, at(z - 1))
+
+    send_chunk(me, 2, {"expert": sibling})
+
+    row_ids = lax.broadcasted_iota(jnp.int32, (count, gate_ref.shape[1]), 0)
+
+    def compute(k, slot):
+        r = chunk(k)
+        gate_row = jnp.sum(jnp.where(row_ids == me, gate_all[k], 0.0), axis=0, keepdims=True)
+        gate_col = jnp.transpose(jnp.broadcast_to(gate_row, (128, gate_row.shape[1])))[:rows]
+        tile = 256
+        gate_wide = jnp.concatenate([gate_col] * (tile // 128), axis=1)
+        total = jnp.zeros((rows, 128), F32)
+        for j in range(ff // tile):
+            cols = slice(j * tile, (j + 1) * tile)
+            back = mm_nt(dy_buf[slot], dw_ref[cols, :])
+            gate_pre = mm(n2_all[r, :], gw_ref[:, cols])
+            up_pre = mm(n2_all[r, :], uw_ref[:, cols])
+            act, slope = gelu_both(gate_pre)
+            hidden = act * up_pre
+            hs_all[r, cols] = (gate_wide * hidden).astype(BF)
+            product = hidden * back
+            for i in range(tile // 128):
+                total = total + product[:, i * 128 : (i + 1) * 128]
+            back = gate_wide * back
+            gl_all[r, cols] = (back * up_pre * slope).astype(BF)
+            ul_all[r, cols] = (back * act).astype(BF)
+        padded = jnp.concatenate(
+            [total, jnp.zeros((gate_ref.shape[1] - rows, 128), F32)], axis=0
+        )
+        gg_row = jnp.sum(jnp.transpose(padded), axis=0, keepdims=True)
+        gg_tile = jnp.where(row_ids == me, gg_row, 0.0)
+        gg_out[k] = gg_tile
+
+        @pl.when(k == me)
+        def _():
+            gg_in[me] = gg_tile
+
+        @pl.when(k != me)
+        def _():
+            gg_copy(k).start()
+
+        wide = 512
+        for j in range(width // wide):
+            cols = slice(j * wide, (j + 1) * wide)
+            own[k, :, cols] = (
+                mm_nt(gl_all[r, :], gw_ref[cols, :]) + mm_nt(ul_all[r, :], uw_ref[cols, :])
+            ).astype(BF)
+
+    block = 16
+
+    def combine(zd, h, with_in):
+        def step(i, _):
+            rr = pl.ds(pl.multiple_of(h * half + i * block, block), block)
+            value = own[2 * zd + core, rr, :].astype(F32) + sib[zd, rr, :].astype(F32)
+            if with_in:
+                value = value + zin[zd, rr, :].astype(F32)
+            own[2 * zd + core, rr, :] = value.astype(BF)
+            return 0
+
+        lax.fori_loop(0, half // block, step, 0)
+
+    def slot_for(zd, nxt):
+        return jnp.where((nxt == zd) & (nxt < z), depth, zd)
+
+    def pass_on(zd, h, nxt, with_in):
+        if h == 0:
+            own_copy(zd).wait_recv()
+        if with_in:
+            zin_copy(zd, h, nxt, zd).wait_recv()
+        combine(zd, h, with_in)
+        zin_copy(zd, h, nxt, slot_for(zd, nxt)).start()
+
+    def pair(zs):
+        def one(w, _):
+            k = 2 * zs + jnp.where(w == 0, 1 - core, core)
+
+            @pl.when(w == 0)
+            def _():
+                arrived(k)
+
+            dy_copy(k, w).wait()
+            compute(k, w)
+
+            @pl.when(w == 0)
+            def _():
+                own_copy(zs).start()
+
+            return 0
+
+        lax.fori_loop(0, 2, one, 0)
+
+    def start_dy(zs):
+        dy_copy(2 * zs + 1 - core, 0).start()
+        dy_copy(2 * zs + core, 1).start()
+
+    def by_distance(d, _):
+        left, right = z - d, z + d
+        has_left, has_right = left >= 0, (right < depth) & (d > 0)
+
+        @pl.when(has_left)
+        def _():
+            start_dy(left)
+
+        @pl.when(has_left & (d > 0))
+        def _():
+            k = 2 * left + core
+            arrived(k)
+
+            @pl.when(z < depth - 1)
+            def _():
+                send_chunk(k, 0, at(z + 1))
+
+            send_chunk(k, 2, {"expert": sibling})
+
+        @pl.when(has_right)
+        def _():
+            k = 2 * right + core
+            arrived(k)
+
+            @pl.when(z > 0)
+            def _():
+                send_chunk(k, 1, at(z - 1))
+
+            send_chunk(k, 2, {"expert": sibling})
+
+        def side(s, _):
+            zs = jnp.where(s == 0, left, right)
+
+            @pl.when(jnp.where(s == 0, has_left, has_right))
+            def _():
+                @pl.when(s == 1)
+                def _():
+                    start_dy(right)
+
+                pair(zs)
+
+                @pl.when((d > 0) & ((z == 0) | (z == depth - 1)))
+                def _():
+                    nxt = jnp.where(z == 0, 1, depth - 2)
+                    for h in range(2):
+                        pass_on(zs, h, nxt, False)
+
+            return 0
+
+        lax.fori_loop(0, 2, side, 0)
+        return 0
+
+    lax.fori_loop(0, depth, by_distance, 0)
+
+    def sum_copy(k, slot):
+        return pltpu.make_async_copy(own.at[slot], sum_ref.at[k], sum_sem.at[slot])
+
+    def sums(i, _):
+        slot = 2 * lax.rem(i, depth) + 1 - core
+
+        @pl.when(i < depth)
+        def _():
+            own_copy(i).wait_send()
+
+        @pl.when(i >= depth)
+        def _():
+            sum_copy(i, slot).wait()
+
+        wide = 512
+        for j in range(width // wide):
+            cols = slice(j * wide, (j + 1) * wide)
+            own[slot, :, cols] = mm(hs_all[chunk(i), :], dw_ref[:, cols]).astype(BF)
+        sum_copy(i, slot).start()
+        return 0
+
+    lax.fori_loop(0, count, sums, 0)
+
+    tile = 256
+
+    def stage_copy(ref, i, slot):
+        return pltpu.make_async_copy(
+            stage.at[slot], ref.at[pl.ds(pl.multiple_of(i * tile, 16), tile)], stage_sem.at[slot]
+        )
+
+    def col_copy(i, slot):
+        return pltpu.make_async_copy(
+            dy_ref.at[:, :, pl.ds(pl.multiple_of(i * tile, 128), tile)], dy_cols.at[slot], cols_sem.at[slot]
+        )
+
+    def weight_tiles(ref, grads, low, high, fresh):
+        def step(i, _):
+            slot = lax.rem(i, 2)
+
+            @pl.when(i >= 2 if fresh else i >= 0)
+            def _():
+                stage_copy(ref, i, slot).wait()
+
+            cols = pl.ds(pl.multiple_of(i * tile, 128), tile)
+            stage[slot] = mm_tn(n2_all[:, cols], grads[...]).astype(BF)
+            stage_copy(ref, i, slot).start()
+            return 0
+
+        lax.fori_loop(low, high, step, 0)
+
+    def down_copy(i, slot):
+        return pltpu.make_async_copy(
+            down_stage.at[slot],
+            ddw_ref.at[:, pl.ds(pl.multiple_of(i * tile, 128), tile)],
+            stage_sem.at[slot],
+        )
+
+    def down_tiles(low, high):
+        def step(i, _):
+            slot = lax.rem(i, 2)
+            down_copy(i, slot).wait()
+            col_copy(i, slot).wait()
+            cols = dy_cols[slot].reshape(count * rows, tile)
+            down_stage[slot] = mm_tn(hs_all[...], cols).astype(BF)
+            down_copy(i, slot).start()
+
+            @pl.when(i + 2 < width // tile)
+            def _():
+                col_copy(i + 2, slot).start()
+
+            return 0
+
+        lax.fori_loop(low, high, step, 0)
+
+    def flow(r, first, h):
+        right = (z < depth - 1 - z) if first else (z >= depth - 1 - z)
+        zd = jnp.where(right, r, depth - 1 - r)
+        valid = jnp.where(right, (z < zd) & (z > 0), (z > zd) & (z < depth - 1))
+
+        @pl.when(valid)
+        def _():
+            pass_on(zd, h, jnp.where(right, z + 1, z - 1), True)
+
+    col_copy(0, 0).start()
+    col_copy(1, 1).start()
+    tiles = width // tile
+    jobs = [
+        lambda: weight_tiles(dgw_ref, gl_all, 0, tiles // 2, True),
+        lambda: weight_tiles(dgw_ref, gl_all, tiles // 2, tiles, True),
+        lambda: weight_tiles(duw_ref, ul_all, 0, tiles // 2, False),
+        lambda: weight_tiles(duw_ref, ul_all, tiles // 2, tiles, False),
+        lambda: down_tiles(0, tiles // 2),
+        lambda: down_tiles(tiles // 2, tiles),
+    ]
+    for r in range(2, depth):
+        for first in (True, False):
+            for h in range(2):
+                flow(r, first, h)
+                if jobs and (first or r == depth - 1):
+                    jobs.pop(0)()
+    while jobs:
+        jobs.pop(0)()
+
+    own_copy(z).wait_recv()
+    for h in range(2):
+
+        @pl.when(z > 0)
+        def _():
+            zin_copy(z, h, z, z).wait_recv()
+
+        @pl.when(z < depth - 1)
+        def _():
+            zin_copy(z, h, z, depth).wait_recv()
+
+    def last(i, _):
+        rr = pl.ds(pl.multiple_of(i * block, block), block)
+        row_ref[rr, :] = own[me, rr, :].astype(F32) + sib[z, rr, :].astype(F32)
+
+        @pl.when(z > 0)
+        def _():
+            row_ref[rr, :] += zin[z, rr, :].astype(F32)
+
+        @pl.when(z < depth - 1)
+        def _():
+            row_ref[rr, :] += zin[depth, rr, :].astype(F32)
+
+        return 0
+
+    lax.fori_loop(0, rows // block, last, 0)
+
+    for e in range(count):
+
+        @pl.when(e != me)
+        def _():
+            pltpu.make_async_remote_copy(
+                gg_out.at[e], gg_in.at[e], gg_send.at[e], gg_recv.at[e],
+                device_id={"expert": e}, device_id_type=MESH,
+            ).wait_recv()
+
+    gg_ref[...] = jnp.sum(gg_in[...], axis=0)
+
+    for e in range(count):
+
+        @pl.when(e != me)
+        def _():
+            gg_copy(e).wait_send()
+
+        zs = e // 2
+
+        @pl.when((e == me) | ((zs < z) & (e % 2 == core)))
+        def _():
+            @pl.when(z < depth - 1)
+            def _():
+                sent_chunk(e, 0, at(z + 1))
+
+        @pl.when((e == me) | ((zs > z) & (e % 2 == core)))
+        def _():
+            @pl.when(z > 0)
+            def _():
+                sent_chunk(e, 1, at(z - 1))
+
+        @pl.when(e % 2 == core)
+        def _():
+            sent_chunk(e, 2, {"expert": sibling})
+
+    for zd in range(depth):
+        sum_copy(zd, 2 * zd + 1 - core).wait()
+        for h in range(2):
+
+            @pl.when(zd != z)
+            def _():
+                zin_copy(zd, h, z, zd).wait_send()
+
+    for slot in range(2):
+        down_copy(0, slot).wait()
+
+
+def expert_pass(n2, gate_rows, dy_all, gate_w, up_w, down_w):
+    count = lax.axis_size("expert")
+    depth = count // 2
+    rows, width = n2.shape
+    ff = gate_w.shape[1]
+    lanes = gate_rows.shape[1]
+    dma = pltpu.SemaphoreType.DMA
+    vmem = pl.BlockSpec(memory_space=pltpu.VMEM)
+    anywhere = pl.BlockSpec(memory_space=pl.ANY)
+    outs = (
+        jax.ShapeDtypeStruct((rows, width), F32),
+        jax.ShapeDtypeStruct((count, lanes), F32),
+        jax.ShapeDtypeStruct((count, rows, width), BF),
+        jax.ShapeDtypeStruct((width, ff), BF),
+        jax.ShapeDtypeStruct((width, ff), BF),
+        jax.ShapeDtypeStruct((ff, width), BF),
+    )
+    return pl.pallas_call(
+        expert_kernel,
+        name="expert_pass",
+        out_shape=outs,
+        in_specs=[vmem, vmem, anywhere, vmem, vmem, vmem],
+        out_specs=(vmem, vmem, anywhere, anywhere, anywhere, anywhere),
+        scratch_shapes=[
+            pltpu.VMEM((count * rows, width), BF),
+            pltpu.VMEM((count, count, lanes), F32),
+            pltpu.VMEM((2, rows, width), BF),
+            pltpu.VMEM((2, count, rows, 256), BF),
+            pltpu.VMEM((count * rows, ff), BF),
+            pltpu.VMEM((count * rows, ff), BF),
+            pltpu.VMEM((count * rows, ff), BF),
+            pltpu.VMEM((count, rows, width), BF),
+            pltpu.VMEM((depth, rows, width), BF),
+            pltpu.VMEM((depth + 1, rows, width), BF),
+            pltpu.VMEM((count, count, lanes), F32),
+            pltpu.VMEM((count, count, lanes), F32),
+            pltpu.VMEM((2, 256, ff), BF),
+            pltpu.VMEM((2, ff, 256), BF),
+            dma((count, 3)), dma((count,)), dma((count, 3)), dma((count,)),
+            dma((depth,)), dma((depth,)), dma((depth, 2)), dma((depth + 1, 2)),
+            dma((count,)), dma((count,)), dma((2,)), dma((2,)), dma((count,)), dma((2,)),
+        ],
+        compiler_params=pltpu.CompilerParams(
+            collective_id=2, has_side_effects=True, vmem_limit_bytes=62 * 2**20
+        ),
+        cost_estimate=pl.CostEstimate(
+            flops=18 * count * rows * width * ff, bytes_accessed=60 * 2**20, transcendentals=0
+        ),
+    )(n2, gate_rows, dy_all, gate_w, up_w, down_w)
+
+
+def scatter_kernel(
+    w_ref, es_ref,
+    share_ref, sum_ref,
+    w, es, wsib, ra, rb, ra2, rb2, wz, esib, ez,
+    ws_send, ws_recv, a_send, a_recv, b_send, b_recv, a2_send, a2_recv, b2_send, b2_recv,
+    wz_send, wz_recv, es_send, es_recv, ez_send, ez_recv, w_sem, e_sem,
+):
+    depth = es_ref.shape[0] // 2
+    rows, width = es_ref.shape[1:]
+    shard, total = w_ref.shape[3:]
+    cut = ra.shape[3]
+    half = rows // 2
+    me, mine = lax.axis_index("expert"), lax.axis_index("dp")
+    z, core = me // 2, me % 2
+    y, x = mine // 2, mine % 2
+    xn, yn, diag = y * 2 + 1 - x, (1 - y) * 2 + x, (1 - y) * 2 + 1 - x
+    sibling = {"expert": z * 2 + 1 - core}
+
+    def at(zz):
+        return {"expert": zz * 2 + core}
+
+    greet(depth, z, at, (sibling, {"dp": xn}, {"dp": yn}))
+
+    def remote(src, dst, send, recv, target):
+        return pltpu.make_async_remote_copy(
+            src, dst, send, recv, device_id=target, device_id_type=MESH
+        )
+
+    def ws_copy(dp):
+        return remote(w_ref.at[dp, :, 1 - core], wsib.at[dp], ws_send.at[dp], ws_recv.at[dp], sibling)
+
+    def w_load(dp):
+        return pltpu.make_async_copy(w_ref.at[dp, :, core], w.at[dp], w_sem.at[dp])
+
+    def es_copy(zd):
+        return remote(es_ref.at[2 * zd + 1 - core], esib.at[zd], es_send.at[zd], es_recv.at[zd], sibling)
+
+    def es_load(zd):
+        return pltpu.make_async_copy(es_ref.at[2 * zd + core], es.at[zd], e_sem.at[zd])
+
+    first_cols, last_cols = slice(0, cut), slice(cut, total)
+
+    def a_copy(yy):
+        return remote(
+            w.at[yy * 2 + 1 - x, :, :, first_cols], ra.at[yy], a_send.at[yy], a_recv.at[yy], {"dp": xn}
+        )
+
+    def b_copy(xx):
+        return remote(
+            w.at[(1 - y) * 2 + xx, :, :, last_cols], rb.at[xx], b_send.at[xx], b_recv.at[xx], {"dp": yn}
+        )
+
+    def a2_copy():
+        return remote(w.at[yn, :, :, first_cols], ra2, a2_send, a2_recv, {"dp": yn})
+
+    def b2_copy():
+        return remote(w.at[xn, :, :, last_cols], rb2, b2_send, b2_recv, {"dp": xn})
+
+    def wz_copy(zd, nxt, slot):
+        return remote(w.at[mine, zd], wz.at[slot], wz_send.at[zd], wz_recv.at[slot], at(nxt))
+
+    def part(h):
+        return pl.ds(h * half, half)
+
+    def ez_copy(zd, h, nxt, slot):
+        return remote(
+            es.at[zd, part(h)], ez.at[slot, part(h)], ez_send.at[zd, h], ez_recv.at[slot, h], at(nxt)
+        )
+
+    for dp in (xn, diag, yn, mine):
+        ws_copy(dp).start()
+        w_load(dp).start()
+    for zd in range(depth):
+        es_copy(zd).start()
+        es_load(zd).start()
+
+    block = 16
+
+    def add(into, term):
+        def step(i, _):
+            zz, rr = i // (shard // block), pl.ds(pl.multiple_of(lax.rem(i, shard // block) * block, block), block)
+            into[zz, rr, :] = (into[zz, rr, :].astype(F32) + term[zz, rr, :].astype(F32)).astype(BF)
+            return 0
+
+        lax.fori_loop(0, depth * (shard // block), step, 0)
+
+    def combine(dp):
+        w_load(dp).wait()
+        ws_copy(dp).wait_recv()
+        add(w.at[dp], wsib.at[dp])
+
+    combine(xn)
+    a_copy(y).start()
+    combine(diag)
+    a_copy(1 - y).start()
+    b_copy(1 - x).start()
+    combine(yn)
+    b_copy(x).start()
+
+    def slot_for(zd, nxt):
+        return jnp.where((nxt == zd) & (nxt < z), depth, zd)
+
+    def rows_on(zd, h, nxt, with_in):
+        if h == 0:
+            es_load(zd).wait()
+            es_copy(zd).wait_recv()
+        if with_in:
+            ez_copy(zd, h, nxt, zd).wait_recv()
+
+        def step(i, _):
+            rr = pl.ds(pl.multiple_of(h * half + i * block, block), block)
+            value = es[zd, rr, :].astype(F32) + esib[zd, rr, :].astype(F32)
+            if with_in:
+                value = value + ez[zd, rr, :].astype(F32)
+            es[zd, rr, :] = value.astype(BF)
+            return 0
+
+        lax.fori_loop(0, half // block, step, 0)
+        ez_copy(zd, h, nxt, slot_for(zd, nxt)).start()
+
+    def shard_on(zd, nxt, with_in):
+        if with_in:
+            wz_copy(zd, nxt, zd).wait_recv()
+
+            def step(i, _):
+                rr = pl.ds(pl.multiple_of(i * block, block), block)
+                w[mine, zd, rr, :] = (w[mine, zd, rr, :].astype(F32) + wz[zd, rr, :].astype(F32)).astype(BF)
+                return 0
+
+            lax.fori_loop(0, shard // block, step, 0)
+        wz_copy(zd, nxt, slot_for(zd, nxt)).start()
+
+    end = (z == 0) | (z == depth - 1)
+
+    def from_end(d, action):
+        @pl.when(end)
+        def _():
+            action(jnp.where(z == 0, d, depth - 1 - d), jnp.where(z == 0, 1, depth - 2))
+
+    def flow(r, first, action):
+        right = (z < depth - 1 - z) if first else (z >= depth - 1 - z)
+        zd = jnp.where(right, r, depth - 1 - r)
+        valid = jnp.where(right, (z < zd) & (z > 0), (z > zd) & (z < depth - 1))
+
+        @pl.when(valid)
+        def _():
+            action(zd, jnp.where(right, z + 1, z - 1))
+
+    for d in range(1, depth):
+        for h in range(2):
+            from_end(d, lambda zd, nxt, h=h: rows_on(zd, h, nxt, False))
+    combine(mine)
+    for h in range(2):
+        flow(2, True, lambda zd, nxt, h=h: rows_on(zd, h, nxt, True))
+
+    a_copy(1 - y).wait_recv()
+    add(w.at[yn, :, :, first_cols], ra.at[1 - y])
+    a2_copy().start()
+    b_copy(1 - x).wait_recv()
+    add(w.at[xn, :, :, last_cols], rb.at[1 - x])
+    b2_copy().start()
+    a_copy(y).wait_recv()
+    add(w.at[mine, :, :, first_cols], ra.at[y])
+    b_copy(x).wait_recv()
+    add(w.at[mine, :, :, last_cols], rb.at[x])
+    for r in range(2, depth):
+        for first in (True, False):
+            if (r, first) == (2, True):
+                continue
+            for h in range(2):
+                flow(r, first, lambda zd, nxt, h=h: rows_on(zd, h, nxt, True))
+    a2_copy().wait_recv()
+    add(w.at[mine, :, :, first_cols], ra2)
+    b2_copy().wait_recv()
+    add(w.at[mine, :, :, last_cols], rb2)
+    for d in range(1, depth):
+        from_end(d, lambda zd, nxt: shard_on(zd, nxt, False))
+    for r in range(2, depth):
+        for first in (True, False):
+            flow(r, first, lambda zd, nxt: shard_on(zd, nxt, True))
+
+    es_load(z).wait()
+    es_copy(z).wait_recv()
+
+    @pl.when(z > 0)
+    def _():
+        for h in range(2):
+            ez_copy(z, h, z, z).wait_recv()
+
+    @pl.when(z < depth - 1)
+    def _():
+        for h in range(2):
+            ez_copy(z, h, z, depth).wait_recv()
+
+    def last_rows(i, _):
+        rr = pl.ds(pl.multiple_of(i * block, block), block)
+        sum_ref[rr, :] = es[z, rr, :].astype(F32) + esib[z, rr, :].astype(F32)
+
+        @pl.when(z > 0)
+        def _():
+            sum_ref[rr, :] += ez[z, rr, :].astype(F32)
+
+        @pl.when(z < depth - 1)
+        def _():
+            sum_ref[rr, :] += ez[depth, rr, :].astype(F32)
+
+        return 0
+
+    lax.fori_loop(0, rows // block, last_rows, 0)
+
+    @pl.when(z > 0)
+    def _():
+        wz_copy(z, z, z).wait_recv()
+
+    @pl.when(z < depth - 1)
+    def _():
+        wz_copy(z, z, depth).wait_recv()
+
+    share_ref[...] = w[mine, z].astype(F32)
+
+    @pl.when(z > 0)
+    def _():
+        share_ref[...] += wz[z].astype(F32)
+
+    @pl.when(z < depth - 1)
+    def _():
+        share_ref[...] += wz[depth].astype(F32)
+
+    for dp in range(w.shape[0]):
+        ws_copy(dp).wait_send()
+    for i in range(2):
+        a_copy(i).wait_send()
+        b_copy(i).wait_send()
+    a2_copy().wait_send()
+    b2_copy().wait_send()
+    for zd in range(depth):
+        es_copy(zd).wait_send()
+
+        @pl.when(zd != z)
+        def _():
+            wz_copy(zd, z, zd).wait_send()
+            for h in range(2):
+                ez_copy(zd, h, z, zd).wait_send()
+
+
+def scatter_pass(w_grads, sums):
+    planes = lax.axis_size("dp")
+    count = lax.axis_size("expert")
+    depth = count // 2
+    shard, total = w_grads.shape[1:]
+    rows, width = sums.shape[1:]
+    cut = total // 2 // 128 * 128 + 128
+    dma = pltpu.SemaphoreType.DMA
+    vmem = pl.BlockSpec(memory_space=pltpu.VMEM)
+    anywhere = pl.BlockSpec(memory_space=pl.ANY)
+    return pl.pallas_call(
+        scatter_kernel,
+        name="scatter_pass",
+        out_shape=(
+            jax.ShapeDtypeStruct((shard, total), F32),
+            jax.ShapeDtypeStruct((rows, width), F32),
+        ),
+        in_specs=[anywhere, anywhere],
+        out_specs=(vmem, vmem),
+        scratch_shapes=[
+            pltpu.VMEM((planes, depth, shard, total), BF),
+            pltpu.VMEM((depth, rows, width), BF),
+            pltpu.VMEM((planes, depth, shard, total), BF),
+            pltpu.VMEM((2, depth, shard, cut), BF),
+            pltpu.VMEM((2, depth, shard, total - cut), BF),
+            pltpu.VMEM((depth, shard, cut), BF),
+            pltpu.VMEM((depth, shard, total - cut), BF),
+            pltpu.VMEM((depth + 1, shard, total), BF),
+            pltpu.VMEM((depth, rows, width), BF),
+            pltpu.VMEM((depth + 1, rows, width), BF),
+            dma((planes,)), dma((planes,)), dma((2,)), dma((2,)), dma((2,)), dma((2,)),
+            dma, dma, dma, dma,
+            dma((depth,)), dma((depth + 1,)), dma((depth,)), dma((depth,)),
+            dma((depth, 2)), dma((depth + 1, 2)), dma((planes,)), dma((depth,)),
+        ],
+        compiler_params=pltpu.CompilerParams(
+            collective_id=3, has_side_effects=True, vmem_limit_bytes=60 * 2**20
+        ),
+        cost_estimate=pl.CostEstimate(
+            flops=10**9, bytes_accessed=200 * 2**20, transcendentals=0
+        ),
+    )(w_grads.reshape(planes, depth, 2, shard, total), sums)
+
+
+def greet(depth, z, at, targets):
+    barrier = pltpu.get_barrier_semaphore()
+    for target in targets:
+        pl.semaphore_signal(barrier, 1, device_id=target, device_id_type=MESH)
+
+    @pl.when(z > 0)
+    def _():
+        pl.semaphore_signal(barrier, 1, device_id=at(z - 1), device_id_type=MESH)
+
+    @pl.when(z < depth - 1)
+    def _():
+        pl.semaphore_signal(barrier, 1, device_id=at(z + 1), device_id_type=MESH)
+
+    ends = (z > 0).astype(jnp.int32) + (z < depth - 1).astype(jnp.int32)
+    pl.semaphore_wait(barrier, len(targets) + ends)
+
+
+def attention_kernel(
+    x_ref, shard_ref, cos_ref, sin_ref, bias_ref, hits_ref,
+    n1_ref, q_ref, kv_ref, mixed_ref, lse_ref, middle_ref, n2_ref, gate_ref, w_out,
+    w, n1, q, kv, mixed,
+    z_send, z_recv, x_send, x_recv, y_send, y_recv, a_send, a_recv, b_send, b_recv, s_send, s_recv,
+    kx_send, kx_recv, ky_send, ky_recv, ka_send, ka_recv, kb_send, kb_recv, out_sem, keep_sem,
+):
+    count = lax.axis_size("expert")
+    depth = count // 2
+    shard, total = shard_ref.shape
+    rows, width = x_ref.shape
+    heads = q.shape[1] // HEAD_SIZE
+    kv_width = kv.shape[1]
+    groups = kv_width // (2 * HEAD_SIZE)
+    group = heads // groups
+    wide = heads * HEAD_SIZE
+    qkv_width = wide + kv_width
+    split = qkv_width + 128
+    me, mine = lax.axis_index("expert"), lax.axis_index("dp")
+    z, core = me // 2, me % 2
+    y, x = mine // 2, mine % 2
+    xn, yn, diag = y * 2 + 1 - x, (1 - y) * 2 + x, (1 - y) * 2 + 1 - x
+    sibling = {"expert": z * 2 + 1 - core}
+
+    def at(zz):
+        return {"expert": zz * 2 + core}
+
+    greet(depth, z, at, (sibling, {"dp": xn}, {"dp": yn}))
+
+    def remote(src, dst, send, recv, target):
+        return pltpu.make_async_remote_copy(
+            src, dst, send, recv, device_id=target, device_id_type=MESH
+        )
+
+    bounds = ((0, split), (split, total))
+    cuts = (bounds[0][1] // 256 * 128, split + (total - split) // 256 * 128)
+
+    def place(dp, zz, cc):
+        return pl.ds(pl.multiple_of((dp * count + 2 * zz + cc) * shard, 16), shard)
+
+    def w_copy(dp, zz, low, high, send, recv, target, cc=core):
+        ref = w.at[place(dp, zz, cc), pl.ds(low, high - low)]
+        return remote(ref, ref, send, recv, target)
+
+    def z_copy(p, zz, lane, target):
+        return w_copy(mine, zz, *bounds[p], z_send.at[p, zz, lane], z_recv.at[p, zz], target)
+
+    def x_copy(p, zz, dp):
+        return w_copy(dp, zz, *bounds[p], x_send.at[p, zz], x_recv.at[p, zz], {"dp": xn})
+
+    def y_copy(p, zz, dp):
+        return w_copy(dp, zz, *bounds[p], y_send.at[p, zz], y_recv.at[p, zz], {"dp": yn})
+
+    def a_copy(p, zz, dp):
+        return w_copy(dp, zz, bounds[p][0], cuts[p], a_send.at[p, zz], a_recv.at[p, zz], {"dp": yn})
+
+    def b_copy(p, zz, dp):
+        return w_copy(dp, zz, cuts[p], bounds[p][1], b_send.at[p, zz], b_recv.at[p, zz], {"dp": xn})
+
+    def s_copy(p, dp, zz, cc=core):
+        return w_copy(dp, zz, *bounds[p], s_send.at[p, dp, zz], s_recv.at[p, dp, zz], sibling, cc)
+
+    def spread(p, zz):
+        x_copy(p, zz, mine).start()
+        y_copy(p, zz, mine).start()
+        s_copy(p, mine, zz).start()
+
+    def on_sides(d, action):
+        @pl.when(z - d >= 0)
+        def _():
+            action(z - d, True)
+
+        if d > 0:
+
+            @pl.when(z + d < depth)
+            def _():
+                action(z + d, False)
+
+    def z_step(p, d):
+        if d == 0:
+
+            @pl.when(z < depth - 1)
+            def _():
+                z_copy(p, z, 0, at(z + 1)).start()
+
+            @pl.when(z > 0)
+            def _():
+                z_copy(p, z, 1, at(z - 1)).start()
+
+            spread(p, z)
+            return
+
+        def action(zz, from_left):
+            z_copy(p, zz, 0, at(z)).wait_recv()
+            if from_left:
+
+                @pl.when(z < depth - 1)
+                def _():
+                    z_copy(p, zz, 0, at(z + 1)).start()
+            else:
+
+                @pl.when(z > 0)
+                def _():
+                    z_copy(p, zz, 1, at(z - 1)).start()
+
+            spread(p, zz)
+
+        on_sides(d, action)
+
+    def xy_step(p, d):
+        def action(zz, _):
+            x_copy(p, zz, xn).wait_recv()
+            a_copy(p, zz, xn).start()
+            s_copy(p, xn, zz).start()
+            y_copy(p, zz, yn).wait_recv()
+            b_copy(p, zz, yn).start()
+            s_copy(p, yn, zz).start()
+
+        on_sides(d, action)
+
+    def diag_step(p, d):
+        def action(zz, _):
+            a_copy(p, zz, diag).wait_recv()
+            b_copy(p, zz, diag).wait_recv()
+            s_copy(p, diag, zz).start()
+
+        on_sides(d, action)
+
+    def all_here(p):
+        for dp in range(4):
+            for zz in range(depth):
+                s_copy(p, dp, zz, 1 - core).wait_recv()
+
+    def all_sent(p):
+        for zz in range(depth):
+
+            @pl.when((zz <= z) & (z < depth - 1))
+            def _():
+                z_copy(p, zz, 0, at(z)).wait_send()
+
+            @pl.when((zz >= z) & (z > 0))
+            def _():
+                z_copy(p, zz, 1, at(z)).wait_send()
+
+            x_copy(p, zz, mine).wait_send()
+            y_copy(p, zz, mine).wait_send()
+            a_copy(p, zz, xn).wait_send()
+            b_copy(p, zz, yn).wait_send()
+            for dp in range(4):
+                s_copy(p, dp, zz).wait_send()
+
+    w[place(mine, z, core), :] = shard_ref[...]
+    z_step(0, 0)
+    z_step(0, 1)
+    xy_step(0, 0)
+    for d in range(2, depth):
+        z_step(0, d)
+        xy_step(0, d - 1)
+    xy_step(0, depth - 1)
+    for d in range(depth):
+        diag_step(0, d)
+    all_here(0)
+    z_step(1, 0)
+
+    def keep(p):
+        low, high = bounds[p]
+        return pltpu.make_async_copy(
+            w.at[:, pl.ds(low, high - low)], w_out.at[:, pl.ds(low, high - low)], keep_sem.at[p]
+        )
+
+    keep(0).start()
+    small = jnp.transpose(w[:, qkv_width:split].astype(F32))
+    experts = hits_ref.shape[0]
+    gain_one, gain_two = small[experts : experts + 1], small[experts + 1 : experts + 2]
+
+    block = 32
+
+    def first_norm(i, _):
+        rr = pl.ds(pl.multiple_of(i * block, block), block)
+        value = x_ref[rr, :].astype(F32)
+        scale = lax.rsqrt(jnp.mean(value * value, axis=1, keepdims=True) + EPS)
+        n1[rr, :] = (value * scale * gain_one).astype(BF)
+        return 0
+
+    lax.fori_loop(0, rows // block, first_norm, 0)
+
+    def turn(value):
+        return value * cos_ref[...] + pltpu.roll(value, HEAD_SIZE // 2, 1) * sin_ref[...]
+
+    own = pl.ds(pl.multiple_of(mine * rows, 16), rows)
+    projected = mm(n1[...], w[:, wide:qkv_width])
+    for g in range(groups):
+        low = 2 * g * HEAD_SIZE
+        kv[own, low : low + HEAD_SIZE] = turn(projected[:, low : low + HEAD_SIZE]).astype(BF)
+        kv[own, low + HEAD_SIZE : low + 2 * HEAD_SIZE] = projected[
+            :, low + HEAD_SIZE : low + 2 * HEAD_SIZE
+        ].astype(BF)
+
+    def kv_copy(g, dp, low, high, send, recv, target):
+        ref = kv.at[
+            pl.ds(pl.multiple_of(dp * rows, 16), rows),
+            pl.ds((2 * g + low) * HEAD_SIZE, (high - low) * HEAD_SIZE),
+        ]
+        return remote(ref, ref, send.at[g], recv.at[g], target)
+
+    def kx(g, dp):
+        return kv_copy(g, dp, 0, 2, kx_send, kx_recv, {"dp": xn})
+
+    def ky(g, dp):
+        return kv_copy(g, dp, 0, 2, ky_send, ky_recv, {"dp": yn})
+
+    def ka(g, dp):
+        return kv_copy(g, dp, 0, 1, ka_send, ka_recv, {"dp": yn})
+
+    def kb(g, dp):
+        return kv_copy(g, dp, 1, 2, kb_send, kb_recv, {"dp": xn})
+
+    def kv_on(g):
+        kx(g, xn).wait_recv()
+        ka(g, xn).start()
+        ky(g, yn).wait_recv()
+        kb(g, yn).start()
+
+    def kv_here(g):
+        ka(g, diag).wait_recv()
+        kb(g, diag).wait_recv()
+
+    for g in range(groups):
+        kx(g, mine).start()
+        ky(g, mine).start()
+
+    def project(h, _):
+        cols = pl.ds(pl.multiple_of(h * 2 * HEAD_SIZE, 2 * HEAD_SIZE), 2 * HEAD_SIZE)
+        value = mm(n1[...], w[:, cols])
+        q[:, cols] = jnp.concatenate(
+            [turn(value[:, :HEAD_SIZE]), turn(value[:, HEAD_SIZE:])], axis=1
+        ).astype(BF)
+        return 0
+
+    lax.fori_loop(0, heads // 2, project, 0)
+    kv_on(0)
+    z_step(1, 1)
+    kv_here(0)
+    later = [
+        lambda: (kv_on(1), xy_step(1, 0), z_step(1, 2)),
+        lambda: (xy_step(1, 1), z_step(1, 3)),
+        lambda: xy_step(1, 2),
+        lambda: xy_step(1, 3),
+        lambda: (diag_step(1, 0), diag_step(1, 1)),
+        lambda: (diag_step(1, 2), diag_step(1, 3)),
+        lambda: kv_here(1),
+    ]
+    lse_ref[...] = jnp.zeros_like(lse_ref)
+    lanes = lax.broadcasted_iota(jnp.int32, lse_ref.shape, 1)
+
+    def attend(h, _):
+        for i, job in enumerate(later):
+            pl.when(h == i)(lambda job=job: (job(), None)[1])
+        g = h // group
+        cols = pl.ds(pl.multiple_of(h * HEAD_SIZE, HEAD_SIZE), HEAD_SIZE)
+        k_cols = pl.ds(pl.multiple_of(g * 2 * HEAD_SIZE, HEAD_SIZE), HEAD_SIZE)
+        v_cols = pl.ds(pl.multiple_of(g * 2 * HEAD_SIZE + HEAD_SIZE, HEAD_SIZE), HEAD_SIZE)
+        scores = mm_nt(q[:, cols], kv[:, k_cols]) * (HEAD_SIZE**-0.5 * LOG2E) + bias_ref[...]
+        top = jnp.max(scores, axis=1, keepdims=True)
+        power = jnp.exp2(scores - top)
+        sums = jnp.sum(power, axis=1, keepdims=True)
+        mixed[:, cols] = (mm(power.astype(BF), kv[:, v_cols]) / sums).astype(BF)
+        lse_ref[...] = jnp.where(lanes == h, top + jnp.log2(sums), lse_ref[...])
+        return 0
+
+    lax.fori_loop(0, heads, attend, 0)
+    keeps = [
+        pltpu.make_async_copy(src, dst, out_sem.at[i])
+        for i, (src, dst) in enumerate(
+            ((n1, n1_ref), (q, q_ref), (kv, kv_ref), (mixed, mixed_ref))
+        )
+    ]
+    for copy in keeps:
+        copy.start()
+    all_here(1)
+    keep(1).start()
+    tile = 512
+
+    def project_out(i, _):
+        cols = pl.ds(pl.multiple_of(i * tile, tile), tile)
+        w_cols = pl.ds(pl.multiple_of(split + i * tile, 128), tile)
+        middle_ref[:, cols] = x_ref[:, cols].astype(F32) + mm(mixed[...], w[:, w_cols])
+        return 0
+
+    lax.fori_loop(0, width // tile, project_out, 0)
+
+    def second_norm(i, _):
+        rr = pl.ds(pl.multiple_of(i * block, block), block)
+        value = middle_ref[rr, :]
+        scale = lax.rsqrt(jnp.mean(value * value, axis=1, keepdims=True) + EPS)
+        n2_ref[rr, :] = (value * scale * gain_two).astype(BF)
+        return 0
+
+    lax.fori_loop(0, rows // block, second_norm, 0)
+    logits = mm_nt(small.astype(BF), n2_ref[...])[:experts]
+    hits = hits_ref[...] > 0.5
+    chosen = jnp.where(hits, logits, NEGATIVE)
+    power = jnp.where(hits, jnp.exp(chosen - jnp.max(chosen, axis=0, keepdims=True)), 0.0)
+    gate_ref[...] = jnp.zeros_like(gate_ref)
+    gate_ref[:, :rows] = power / jnp.sum(power, axis=0, keepdims=True)
+
+    for g in range(groups):
+        kx(g, mine).wait_send()
+        ky(g, mine).wait_send()
+        ka(g, xn).wait_send()
+        kb(g, yn).wait_send()
+    for p in range(2):
+        all_sent(p)
+        keep(p).wait()
+    for copy in keeps:
+        copy.wait()
+
+
+def attention_pass(x, shard, cos, sin, bias, hits, kv_width):
+    count = lax.axis_size("expert")
+    depth = count // 2
+    rows, width = x.shape
+    lanes = rows + -rows % 128
+    devices = 4 * count
+    wide = width
+    dma = pltpu.SemaphoreType.DMA
+    vmem = pl.BlockSpec(memory_space=pltpu.VMEM)
+    anywhere = pl.BlockSpec(memory_space=pl.ANY)
+    shape = jax.ShapeDtypeStruct
+    pair = dma((2, depth))
+    groups = kv_width // (2 * HEAD_SIZE)
+    tree = 4 * rows
+    total = shard.shape[1]
+    return pl.pallas_call(
+        attention_kernel,
+        name="attention_pass",
+        out_shape=(
+            shape((rows, width), BF),
+            shape((rows, wide), BF),
+            shape((tree, kv_width), BF),
+            shape((rows, wide), BF),
+            shape((rows, 128), F32),
+            shape((rows, width), F32),
+            shape((rows, width), BF),
+            shape((hits.shape[0], lanes), F32),
+            shape((devices * shard.shape[0], total), BF),
+        ),
+        in_specs=[vmem] * 6,
+        out_specs=(anywhere,) * 4 + (vmem,) * 4 + (anywhere,),
+        scratch_shapes=[
+            pltpu.VMEM((devices * shard.shape[0], total), BF),
+            pltpu.VMEM((rows, width), BF),
+            pltpu.VMEM((rows, wide), BF),
+            pltpu.VMEM((tree, kv_width), BF),
+            pltpu.VMEM((rows, wide), BF),
+            dma((2, depth, 2)), pair, pair, pair, pair, pair, pair, pair, pair, pair,
+            dma((2, 4, depth)), dma((2, 4, depth)),
+            *[dma((groups,)) for _ in range(8)],
+            dma((4,)), dma((2,)),
+        ],
+        compiler_params=pltpu.CompilerParams(
+            collective_id=1, has_side_effects=True, vmem_limit_bytes=56 * 2**20
+        ),
+        cost_estimate=pl.CostEstimate(
+            flops=10**10, bytes_accessed=300 * 2**20, transcendentals=0
+        ),
+    )(x, shard, cos, sin, bias, hits)
+
+
+def rotation_rows(positions):
+    half = HEAD_SIZE // 2
+    frequency = jnp.power(THETA, -(jnp.arange(half, dtype=jnp.float32) * 2.0 / HEAD_SIZE))
+    angles = positions.astype(jnp.float32)[:, None] * frequency[None, :]
+    cosine, sine = jnp.cos(angles), jnp.sin(angles)
+    return jnp.concatenate([cosine, cosine], axis=1), jnp.concatenate([-sine, sine], axis=1)
+
+
+def turn_back(values, cos, sin):
+    half = HEAD_SIZE // 2
+    swapped = jnp.concatenate([values[..., half:], values[..., :half]], axis=-1)
+    return values * cos - swapped * sin
+
+
+def tree_visibility(parent_row, query_ids, tree_length):
+    blocks = parent_row.shape[0]
+    trunk = blocks - BRANCHES - LEAVES
+    leaf_from = trunk + BRANCHES
+    query_block = query_ids // SEG
+    block_ids = jnp.arange(blocks, dtype=jnp.int32)
+    depth_of = jnp.minimum(query_block, trunk) + (query_block >= leaf_from).astype(jnp.int32)
+    positions = depth_of * SEG + query_ids % SEG
+    parent = jnp.sum(jnp.where(query_block[:, None] == block_ids, parent_row, 0), axis=1)
+    above = jnp.where(query_block >= leaf_from, parent, query_block)
+    key_ids = jnp.arange(tree_length, dtype=jnp.int32)[None, :]
+    key_block = key_ids // SEG
+    related = (
+        (key_block < trunk) | (key_block == query_block[:, None]) | (key_block == above[:, None])
+    )
+    return related & (key_ids <= query_ids[:, None]), positions
+
+
+def rows_to_gather(parts):
+    return jnp.concatenate(parts, axis=1)
+
+
+def dense_on_device(
+    tokens,
+    cotangent,
+    parents,
+    routes,
+    first_gain,
+    second_gain,
+    query_weight,
+    key_matrix,
+    value_matrix,
+    out_weight,
+    router_weight,
+    gate_weight,
+    up_weight,
+    down_weight,
+):
+    experts = router_weight.shape[1]
+    group = QUERY_HEADS // KEY_VALUE_HEADS
+    heads_width = QUERY_HEADS * HEAD_SIZE
+    kv_width = 2 * KEY_VALUE_HEADS * HEAD_SIZE
+    qkv_width = heads_width + kv_width
+    kv_shards = []
+    for head in range(KEY_VALUE_HEADS):
+        cols = slice(head * HEAD_SIZE, (head + 1) * HEAD_SIZE)
+        kv_shards += [key_matrix[:, cols], value_matrix[:, cols]]
+    small_shard = jnp.concatenate(
+        [router_weight, first_gain[:, None], second_gain[:, None]], axis=1
+    )
+    small_shard = jnp.pad(small_shard, ((0, 0), (0, -small_shard.shape[1] % 128)))
+    small_width = small_shard.shape[1]
+    shard = jnp.concatenate([query_weight, *kv_shards, small_shard, out_weight], axis=1)
+    dy_low = cotangent[0]
+    dy_all = lax.all_gather(dy_low, "expert", axis=0)
+    inputs_low = tokens[0]
+    total_rows = inputs_low.shape[0]
+    tree_length = parents.shape[1] * SEG
+    query_ids = lax.axis_index("dp") * total_rows + jnp.arange(total_rows, dtype=jnp.int32)
+    visible, query_positions = tree_visibility(parents[0], query_ids, tree_length)
+    bias = jnp.where(visible, 0.0, NEGATIVE)
+    cos, sin = rotation_rows(query_positions)
+    expert_ids = jnp.arange(experts, dtype=jnp.int32)
+    hit_rows = jnp.any(routes[0][None, :, :] == expert_ids[:, None, None], axis=2)
+    n1, query_low, kv_all, mixed, logs, middle, n2, gate_rows, full = attention_pass(
+        inputs_low, shard, cos, sin, bias, hit_rows.astype(F32), kv_width
+    )
+    row_sum, gate_grad_rows, sums, gate_w_grad, up_w_grad, down_grad = expert_pass(
+        n2, gate_rows, dy_all, gate_weight[0], up_weight[0], down_weight[0]
+    )
+    gates = gate_rows[:, :total_rows]
+    gate_grad = gate_grad_rows[:, :total_rows]
+    logit_grad = gates * (gate_grad - jnp.sum(gates * gate_grad, axis=0, keepdims=True))
+    qkv_full = full[:, :qkv_width]
+    small_full = full[:, qkv_width : qkv_width + small_width]
+    out_full = full[:, qkv_width + small_width :]
+    router_full = small_full[:, :experts]
+    scale_one = small_full[:, experts].astype(F32)
+    scale_two = small_full[:, experts + 1].astype(F32)
+    inputs = inputs_low.astype(F32)
+    summed = tuple(
+        lax.psum(grad, "dp").astype(jnp.float32)[None]
+        for grad in (gate_w_grad, up_w_grad, down_grad)
+    )
+    router_wide = router_full.astype(jnp.float32)
+    n2_grad = (
+        jnp.einsum("er,de->rd", logit_grad, router_wide, precision=HIGH_PRECISION) + row_sum
+    )
+    router_grad = jnp.einsum(
+        "rd,er->de", n2.astype(jnp.float32), logit_grad, precision=HIGH_PRECISION
+    )
+    upstream = dy_low.astype(jnp.float32)
+    _, second_pull = jax.vjp(normalize, middle, scale_two)
+    middle_norm_grad, second_gain_grad = second_pull(n2_grad)
+    middle_grad = upstream + middle_norm_grad
+    attended_low = middle_grad.astype(jnp.bfloat16)
+    out_grad = jnp.einsum("rd,re->de", mixed, attended_low, preferred_element_type=jnp.float32)
+    mixed_grad = jnp.einsum("re,de->rd", attended_low, out_full, preferred_element_type=jnp.float32)
+    mixed_grad = mixed_grad.astype(jnp.bfloat16).reshape(total_rows, QUERY_HEADS, HEAD_SIZE)
+    query_rotated = query_low.reshape(total_rows, QUERY_HEADS, HEAD_SIZE)
+    query_parts = []
+    kv_parts = []
+    for head in range(KEY_VALUE_HEADS):
+        query_part = query_rotated[:, head * group : (head + 1) * group, :]
+        key_part = kv_all[:, 2 * head * HEAD_SIZE : (2 * head + 1) * HEAD_SIZE]
+        value_part = kv_all[:, (2 * head + 1) * HEAD_SIZE : (2 * head + 2) * HEAD_SIZE]
+        grad_part = mixed_grad[:, head * group : (head + 1) * group, :]
+        scores = jnp.einsum("rgd,kd->grk", query_part, key_part, preferred_element_type=F32)
+        scores = scores * (HEAD_SIZE**-0.5 * LOG2E) + bias
+        log_rows = logs[:, head * group : (head + 1) * group].T[:, :, None]
+        softmax_out = jnp.exp2(scores - log_rows)
+        value_grad = jnp.einsum(
+            "grk,rgd->kd", softmax_out.astype(BF), grad_part, preferred_element_type=F32
+        )
+        attn_grad = jnp.einsum("rgd,kd->grk", grad_part, value_part, preferred_element_type=F32)
+        score_grad = softmax_out * (
+            attn_grad - jnp.sum(softmax_out * attn_grad, axis=-1, keepdims=True)
+        )
+        score_low = score_grad.astype(BF)
+        query_parts.append(
+            jnp.einsum("grk,kd->rgd", score_low, key_part, preferred_element_type=F32)
+            * HEAD_SIZE ** (-0.5)
+        )
+        key_grad = jnp.einsum("grk,rgd->kd", score_low, query_part, preferred_element_type=F32)
+        kv_parts += [key_grad * HEAD_SIZE ** (-0.5), value_grad]
+    kv_sum = lax.psum_scatter(
+        jnp.concatenate(kv_parts, axis=1).astype(BF), "dp", scatter_dimension=0, tiled=True
+    ).astype(F32)
+    query_grad = turn_back(
+        jnp.concatenate(query_parts, axis=1), cos[:, None, :], sin[:, None, :]
+    ).reshape(total_rows, heads_width)
+    kv_grads = []
+    for head in range(KEY_VALUE_HEADS):
+        key_sum = kv_sum[:, 2 * head * HEAD_SIZE : (2 * head + 1) * HEAD_SIZE]
+        kv_grads += [
+            turn_back(key_sum, cos, sin),
+            kv_sum[:, (2 * head + 1) * HEAD_SIZE : (2 * head + 2) * HEAD_SIZE],
+        ]
+    qkv_grad = jnp.concatenate([query_grad, *kv_grads], axis=1).astype(BF)
+    qkv_w_grad = jnp.einsum("rd,re->de", n1, qkv_grad, preferred_element_type=F32)
+    n1_grad = jnp.einsum("re,de->rd", qkv_grad, qkv_full, preferred_element_type=F32)
+    _, first_pull = jax.vjp(normalize, inputs, scale_one)
+    input_norm_grad, first_gain_grad = first_pull(n1_grad)
+    input_grad = (middle_grad + input_norm_grad)[None]
+    small = jnp.concatenate(
+        [router_grad, first_gain_grad[:, None], second_gain_grad[:, None]], axis=1
+    )
+    small = jnp.pad(small, ((0, 0), (0, small_width - small.shape[1])))
+    all_grads = jnp.concatenate([qkv_w_grad, small, out_grad], axis=1).astype(BF)
+    shards = lax.axis_size("dp") * lax.axis_size("expert")
+    share, combined = scatter_pass(all_grads.reshape(shards, -1, all_grads.shape[1]), sums)
+    output = (middle + combined).astype(BF)[None]
+    heads_of = [
+        share[:, heads_width + i * HEAD_SIZE : heads_width + (i + 1) * HEAD_SIZE]
+        for i in range(2 * KEY_VALUE_HEADS)
+    ]
+    query_share = share[:, :heads_width]
+    key_share = jnp.concatenate(heads_of[0::2], axis=1)
+    value_share = jnp.concatenate(heads_of[1::2], axis=1)
+    small_share = share[:, qkv_width : qkv_width + small_width]
+    out_share = share[:, qkv_width + small_width :]
+    return (
+        output,
+        input_grad,
+        small_share[:, experts],
+        small_share[:, experts + 1],
+        query_share,
+        key_share,
+        value_share,
+        out_share,
+        small_share[:, :experts],
+        *summed,
+    )
+
+
 def solution(mesh):
+    dense = mesh.shape["expert"] <= 2 * TOPK and mesh.shape["dp"] == 4
     return jax.shard_map(
-        on_device,
+        dense_on_device if dense else on_device_routed,
         mesh=mesh,
         in_specs=(
             P("expert", "dp", None),

time: 1910 us -> 609 us (0.32)
  waiting for transfers between devices: 1010 us -> 27.7 us
  Pallas kernels: 0 us -> 418 us
  blocking collectives: 375 us -> 0 us
  local copies, waits for them, and re-layouts: 203 us -> 28.7 us
  matrix products: 184 us -> 70.4 us
  other arithmetic: 94.9 us -> 44.4 us
    reduce_scatter x5 -> x1, waiting for transfers between devices: 443 us -> 8.84 us  [dense_on_device(): lax.psum_scatter(jnp.concatenate(kv_parts, axis=1).astype(BF), 'dp', scat...]
    pallas_call x0 -> x3, Pallas kernels: none -> 418 us  [the longest x1 156 us: expert_pass(): pl.pallas_call(expert_kernel, name='expert_pass', out_shape=outs, in_spec...]
    all_to_all x3 -> x0, waiting for transfers between devices: 352 us -> none  [the longest x1 133 us: on_device(): lax.all_to_all(grad_outgoing, 'expert', split_axis=0, concat_axis=0, tile...]
    all_to_all x1 -> x0, blocking collectives: 147 us -> none  [on_device(): lax.all_to_all(outgoing, 'expert', split_axis=0, concat_axis=0, tiled=True)]
    all_gather x5 -> x0, blocking collectives: 146 us -> none  [the longest x1 43.5 us: on_device(): lax.all_gather(key_matrix, ('dp', 'expert'), axis=0, tiled=True)]
    gather x48 -> x0, local copies, waits for them, and re-layouts: 117 us -> none  [the longest x44 63 us: advance(): return (jnp.take(parent_row, current), ancestors)]
    dot_general x36 -> x16, matrix products: 181 us -> 70.4 us  [the longest x2 15.8 us: dense_on_device(): jnp.einsum('rgd,kd->grk', query_part, key_part, preferred_element_type=F32)]
    psum x1, waiting for transfers between devices: 124 us -> 18.1 us  [dense_on_device(): lax.psum(grad, 'dp').astype(jnp.float32)[None]]
  transfers between devices with their start and end apart: 13 -> 3, of which waited for: 10 -> 2; matrix products, arithmetic and copies ran while one was open for 17% -> 12% of each run, Pallas kernels for 0% -> 43%
where the time goes in v2:
time: 609 us; the launch traced here: 604 us
  Pallas kernels  418 us (69%)
  matrix products  70.4 us (12%)
  other arithmetic  44.4 us (7%)
  local copies, waits for them, and re-layouts  28.7 us (5%)
  waiting for transfers between devices  27.7 us (5%)
  between operations  14.6 us (2%)
    pallas_call x1, Pallas kernels, expert_pass(): pl.pallas_call(expert_kernel, name='expert_pass', out_shape=outs, in_spec...  156 us
    pallas_call x1, Pallas kernels, scatter_pass(): pl.pallas_call(scatter_kernel, name='scatter_pass', out_shape=(jax.ShapeD...  138 us
    pallas_call x1, Pallas kernels, attention_pass(): pl.pallas_call(attention_kernel, name='attention_pass', out_shape=(shape(...  124 us
    psum x1, waiting for transfers between devices, dense_on_device(): lax.psum(grad, 'dp').astype(jnp.float32)[None]  18.1 us
    dot_general x2, matrix products, dense_on_device(): jnp.einsum('rgd,kd->grk', query_part, key_part, preferred_element_type=F32)  15.8 us
    unnamed x86, local copies, waits for them, and re-layouts  14.1 us
  transfers between devices with their start and end apart: 3, of which 2 were waited for; matrix products, arithmetic and copies ran while one was open for 12% of the time, Pallas kernels for 43%

profile of v2, /device:TPU:0, one launch (start us, length us, event | category | flops | bytes accessed | tf_op | source)
XLA Modules:
  0.0 604.3 jit_solution(16503976169793075495)
XLA Ops:
  17.1 2.2 fusion.52.bias_ref
  19.3 124.5 %attention_pass.1 = (bf16[352,1536]{1,0:T(8,128)(2,1)}, bf16[352,1536]{1,0:T(8,128)(2,1)}, bf16[1408,512]{1,0:T(8,128)(2,1)}, bf16[352,1536]{1,0:T(8,128)(2,1)},...) custom-call(bf16[352,1536]{1,0:T(8,128)(2,1)} %bitcast.132, ...), custom_call_target="tpu_custom_call" | custom-call | flops 10000000000 | bytes 314572800 | tf_op jit(solution)/shard_map/attention_pass/pallas_call | solution.py:1541
  143.8 2.5 copy.87
  149.7 156.0 %expert_pass.1 = (f32[352,1536]{1,0:T(8,128)}, f32[8,384]{1,0:T(8,128)}, bf16[8,352,1536]{2,1,0:T(8,128)(2,1)}, bf16[1536,768]{1,0:T(8,128)(2,1)}, bf16[1536,768]{1,0:T(8,128)(2,1)}, /*index=5*/bf16[768,1536]{1,0:T(8,128)(2,1)}) custom-call(bf16[352,1536]{1,0:T(8,128)(2,1)} %get-tuple-element.35.n2_ref, f32[8,384]{1,0:T(8,128)} %get-tuple-element.34.gate_ref, ...), custom_call_target="tpu_custom_call" | custom-call | flops 59793997824 | bytes 62914560 | tf_op jit(solution)/shard_map/expert_pass/pallas_call | solution.py:868
  306.4 4.2 multiply_reduce_fusion
  312.6 4.3 fusion.20
  318.3 3.0 fusion.63
  321.3 2.7 fusion.58
  324.1 9.4 %fusion.6 = (f32[6,352]{1,0:T(8,128)S(1)}, f32[6,352,1408]{2,1,0:T(8,128)}) fusion(f32[1408,352,6]{0,1,2:T(8,128)S(1)} %fusion.63, f32[6,352]{1,0:T(8,128)S(1)} %copy.89, f32[352,1408]{1,0:T(8,128)} %fusion.52.bias_ref, bf16[352,12,128]{0,2,1:T(8,128)(2,1)} %bitcast.124, bf16[1408,512]{1,0:T(8,128)(2,1)} %get-tuple-element.31), kind=kOutput, calls=%fused_computation.11 | convolution fusion | flops 779106240 | bytes 26739200 | tf_op jit(solution)/shard_map/rgd,kd->grk/dot_general | solution.py:1698
  333.5 7.2 %fusion.34 = bf16[1408,128]{1,0:T(8,128)(2,1)} fusion(f32[6,352,1408]{2,1,0:T(8,128)} %get-tuple-element.130, bf16[352,12,128]{0,2,1:T(8,128)(2,1)} %bitcast.120), kind=kOutput, calls=%fused_computation.49 | convolution fusion | flops 764420096 | bytes 12845056 | tf_op jit(solution)/shard_map/grk,rgd->kd/dot_general | solution.py:1702
  340.6 5.9 fusion.8
  346.5 2.5 copy-done.3
  349.1 2.7 fusion.37
  351.8 6.5 %fusion = (f32[6,352]{1,0:T(8,128)S(1)}, f32[6,352,1408]{2,1,0:T(8,128)S(1)}) fusion(f32[1408,352,6]{0,1,2:T(8,128)S(1)} %fusion.58, f32[6,352]{1,0:T(8,128)S(1)} %copy.93, f32[352,1408]{1,0:T(8,128)} %fusion.52.bias_ref, bf16[352,12,128]{0,2,1:T(8,128)(2,1)} %bitcast.125, bf16[1408,512]{1,0:T(8,128)(2,1)} %get-tuple-element.31), kind=kOutput, calls=%fused_computation.2 | convolution fusion | flops 779106240 | bytes 26739200 | tf_op jit(solution)/shard_map/rgd,kd->grk/dot_general | solution.py:1698
  358.3 3.1 fusion.31
  362.9 2.0 fusion.38
  367.6 4.6 fusion.54
  376.6 2.0 copy.95
  379.3 1.9 convolution_convert_fusion.2
  382.4 4.3 convolution_convert_fusion.1
  386.6 8.8 %reduce-scatter.2.cloned.1.call-done = bf16[352,512]{1,0:T(8,128)(2,1)} async-done(((bf16[1408,512]{1,0:T(8,128)(2,1)}), bf16[352,512]{1,0:T(8,128)(2,1)}) %reduce-scatter.2.cloned.1.call-update) | async-done | bytes 360464 | tf_op jit(solution)/shard_map/reduce_scatter | solution.py:1716
  401.2 7.6 %fusion.50 = (f32[352]{0:T(512)S(1)}, bf16[1536]{0:T(1024)(128)(2,1)S(1)}, f32[352,1536]{1,0:T(8,128)}) fusion(f32[1536]{0:T(1024)S(1)} %get-tuple-element.94, bf16[1,352,1536]{2,1,0:T(8,128)(2,1)S(1)} %copy-done.14, f32[352]{0:T(512)S(1)} %fusion.97, bf16[352,2048]{0,1:T(8,128)(2,1)} %constant_dynamic-update-slice_fusion.7, ...), kind=kOutput, calls=%fused_computation.64 | convolution fusion | flops 2218375424 | bytes 11120384 | tf_op jit(solution)/shard_map/re,de->rd/dot_general | solution.py:1731
  409.2 5.3 convolution_convert_fusion
  414.6 5.0 pad_maximum_fusion.w_ref
  419.6 137.9 %scatter_pass.1 = (f32[48,3712]{1,0:T(8,128)}, f32[352,1536]{1,0:T(8,128)}) custom-call(bf16[4,4,2,48,3712]{4,3,2,1,0:T(8,128)(2,1)} %pad_maximum_fusion.w_ref, bf16[8,352,1536]{2,1,0:T(8,128)(2,1)} %get-tuple-element.40.es_ref), custom_call_target="tpu_custom_call" | custom-call | flops 1000000000 | bytes 209715200 | tf_op jit(solution)/shard_map/scatter_pass/pallas_call | solution.py:1157
  562.5 1.9 fusion.99
  564.4 3.2 fusion.55
  567.8 1.9 fusion.46
  569.7 18.1 %all-reduce.5.cloned.1.call-done = (bf16[1,1536,768]{2,1,0:T(8,128)(2,1)}, bf16[1,1536,768]{2,1,0:T(8,128)(2,1)}, bf16[1,768,1536]{2,1,0:T(8,128)(2,1)}) async-done(((bf16[1,1536,768]{2,1,0:T(8,128)(2,1)}, bf16[1,1536,768]{2,1,0:T(8,128)(2,1)}, bf16[1,768,1536]{2,1,0:T(8,128)(2,1)}), (bf16[1,1536,768]{2,1,0:T(8,128)(2,1)}, bf16[1,1536,768]{2,1,0:T(8,128)(2,1)}, ...) | async-done | bytes 7077904 | tf_op jit(solution)/shard_map/psum | solution.py:1672
  587.8 4.4 broadcast_in_dim.95
  592.2 2.5 broadcast_in_dim.97
  594.7 2.8 broadcast_in_dim.99
  (144 shorter events, 38.9 us)
Async XLA Ops:
  7.2 9.9 %copy-start.29 = (bf16[48,1536]{1,0:T(8,128)(2,1)S(1)}, bf16[48,1536]{1,0:T(8,128)(2,1)}, u32[]{:S(2)}) copy-start(bf16[48,1536]{1,0:T(8,128)(2,1)} %param.23) | copy-start | bytes 442372
  7.2 142.5 %all-gather.2.cloned.1.call-start = ((), (), s32[]{:S(2)}) async-start(), calls=%async_computation.1 | async-start | bytes 9732096 | tf_op jit(solution)/shard_map/all_gather | solution.py:1645
  7.9 387.6 %reduce-scatter.2.cloned.1.call-start = ((), (), s32[]{:S(2)}) async-start(), calls=%async_computation.2 | async-start | bytes 1802240 | tf_op jit(solution)/shard_map/reduce_scatter | solution.py:1716
  15.5 1.6 copy-start.24
  17.1 2.2 copy-start.32
  143.8 5.6 copy-start
  149.7 156.0 %copy-start.30 = (f32[8,384]{1,0:T(8,128)S(1)}, f32[8,384]{1,0:T(8,128)}, u32[]{:S(2)}) copy-start(f32[8,384]{1,0:T(8,128)} %get-tuple-element.34.gate_ref) | copy-start | bytes 36868
  306.4 4.3 copy-start.1
  306.4 4.3 copy-start.13
  318.3 3.0 copy-start.6
  340.6 8.4 %copy-start.10 = (bf16[352,1536]{0,1:T(8,128)(2,1)S(1)}, bf16[352,1536]{0,1:T(8,128)(2,1)}, u32[]{:S(2)}) copy-start(bf16[352,1536]{0,1:T(8,128)(2,1)} %copy.87) | copy-start | bytes 3244036
  346.5 2.6 copy-start.3
  362.9 2.6 copy-start.4
  362.9 2.6 copy-start.18
  362.9 2.5 copy-start.28
  365.4 2.2 copy-start.15
  366.7 221.1 %all-reduce.5.cloned.1.call-start = ((), (), s32[]{:S(2)}) async-start(), calls=%async_computation.3 | async-start | bytes 14155776 | tf_op jit(solution)/shard_map/psum | solution.py:1672
  367.6 4.6 copy-start.5
  379.3 3.1 copy-start.8
  379.3 3.1 copy-start.33
  386.6 11.1 %copy-start.21 = (f32[352,64]{1,0:T(8,128)S(1)}, f32[352,64]{1,0:T(8,128)}, u32[]{:S(2)}) copy-start(f32[352,64]{1,0:T(8,128)} %copy-done.20) | copy-start | bytes 270340
  386.6 11.2 %copy-start.23 = (f32[352,64]{1,0:T(8,128)S(1)}, f32[352,64]{1,0:T(8,128)}, u32[]{:S(2)}) copy-start(f32[352,64]{1,0:T(8,128)} %copy-done.22) | copy-start | bytes 270340
  386.6 11.2 %copy-start.25 = (f32[352,64]{1,0:T(8,128)S(1)}, f32[352,64]{1,0:T(8,128)}, u32[]{:S(2)}) copy-start(f32[352,64]{1,0:T(8,128)} %copy-done.24) | copy-start | bytes 270340
  395.5 2.7 copy-start.12
  401.2 8.0 %copy-start.34 = (bf16[352,1536]{1,0:T(8,128)(2,1)S(1)}, bf16[352,1536]{1,0:T(8,128)(2,1)}, u32[]{:S(2)}) copy-start(bf16[352,1536]{1,0:T(8,128)(2,1)} %get-tuple-element.30) | copy-start | bytes 3244036
  409.2 5.4 slice-start
  409.2 5.4 slice-start.1
  419.6 144.8 %copy-start.2 = (f32[352,1536]{1,0:T(8,128)S(1)}, f32[352,1536]{1,0:T(8,128)}, u32[]{:S(2)}) copy-start(f32[352,1536]{1,0:T(8,128)} %get-tuple-element.29) | copy-start | bytes 6488068
  564.4 3.2 copy-start.9
  564.4 3.4 copy-start.19
  587.8 4.4 copy-start.17
  592.2 2.5 copy-start.16
  (8 other events, 9.6 us)
Sparse Core Ops, SparseCore 0:
  9.7 106.1 all-gather.1
  366.8 28.5 reduce-scatter.1
  399.7 188.0 all-reduce.4

commit v3 on v2

--- a/solution.py
+++ b/solution.py
@@ -435,10 +435,11 @@
 
 def expert_kernel(
     n2_ref, gate_ref, dy_ref, gw_ref, uw_ref, dw_ref,
-    row_ref, gg_ref, sum_ref, dgw_ref, duw_ref, ddw_ref,
-    n2_all, gate_all, dy_buf, dy_cols, hs_all, gl_all, ul_all, own, sib, zin, gg_out, gg_in, stage, down_stage,
+    row_ref, gg_ref, sum_ref, wide_ref, down_ref, landing,
+    n2_all, gate_all, dy_buf, dy_cols, hs_all, gl_all, ul_all, own, sib, zin, gg_out, gg_in,
+    stage, kept, down_kept,
     n2_send, n2_recv, gt_send, gt_recv, own_send, sib_recv, zin_send, zin_recv,
-    gg_send, gg_recv, dy_sem, cols_sem, sum_sem, stage_sem,
+    gg_send, gg_recv, dy_sem, cols_sem, sum_sem, tile_send, tile_recv, load_sem, keep_sem,
 ):
     count = lax.axis_size("expert")
     depth = count // 2
@@ -449,6 +450,9 @@
     me = lax.axis_index("expert")
     z, core = me // 2, me % 2
     sibling = z * 2 + 1 - core
+    mine = lax.axis_index("dp")
+    y, x = mine // 2, mine % 2
+    others = (y * 2 + 1 - x, (1 - y) * 2 + 1 - x, (1 - y) * 2 + x)
 
     def at(zz):
         return {"expert": zz * 2 + core}
@@ -458,7 +462,9 @@
         pl.semaphore_signal(
             barrier, 1, device_id={"expert": lax.rem(me + other, count)}, device_id_type=MESH
         )
-    pl.semaphore_wait(barrier, count - 1)
+    for dp in others:
+        pl.semaphore_signal(barrier, 1, device_id={"dp": dp}, device_id_type=MESH)
+    pl.semaphore_wait(barrier, count - 1 + len(others))
 
     def chunk(k):
         return pl.ds(pl.multiple_of(k * rows, 16), rows)
@@ -674,72 +680,73 @@
     def sum_copy(k, slot):
         return pltpu.make_async_copy(own.at[slot], sum_ref.at[k], sum_sem.at[slot])
 
-    def sums(i, _):
-        slot = 2 * lax.rem(i, depth) + 1 - core
-
-        @pl.when(i < depth)
-        def _():
-            own_copy(i).wait_send()
-
-        @pl.when(i >= depth)
-        def _():
-            sum_copy(i, slot).wait()
-
-        wide = 512
-        for j in range(width // wide):
-            cols = slice(j * wide, (j + 1) * wide)
-            own[slot, :, cols] = mm(hs_all[chunk(i), :], dw_ref[:, cols]).astype(BF)
-        sum_copy(i, slot).start()
-        return 0
-
-    lax.fori_loop(0, count, sums, 0)
-
-    tile = 256
-
-    def stage_copy(ref, i, slot):
-        return pltpu.make_async_copy(
-            stage.at[slot], ref.at[pl.ds(pl.multiple_of(i * tile, 16), tile)], stage_sem.at[slot]
-        )
-
-    def col_copy(i, slot):
-        return pltpu.make_async_copy(
-            dy_ref.at[:, :, pl.ds(pl.multiple_of(i * tile, 128), tile)], dy_cols.at[slot], cols_sem.at[slot]
-        )
-
-    def weight_tiles(ref, grads, low, high, fresh):
+    def sums(low, high):
         def step(i, _):
-            slot = lax.rem(i, 2)
-
-            @pl.when(i >= 2 if fresh else i >= 0)
+            slot = 2 * lax.rem(i, depth) + 1 - core
+
+            @pl.when(i < depth)
             def _():
-                stage_copy(ref, i, slot).wait()
-
-            cols = pl.ds(pl.multiple_of(i * tile, 128), tile)
-            stage[slot] = mm_tn(n2_all[:, cols], grads[...]).astype(BF)
-            stage_copy(ref, i, slot).start()
+                own_copy(i).wait_send()
+
+            @pl.when(i >= depth)
+            def _():
+                sum_copy(i, slot).wait()
+
+            wide = 512
+            for j in range(width // wide):
+                cols = slice(j * wide, (j + 1) * wide)
+                own[slot, :, cols] = mm(hs_all[chunk(i), :], dw_ref[:, cols]).astype(BF)
+            sum_copy(i, slot).start()
             return 0
 
         lax.fori_loop(low, high, step, 0)
 
-    def down_copy(i, slot):
-        return pltpu.make_async_copy(
-            down_stage.at[slot],
-            ddw_ref.at[:, pl.ds(pl.multiple_of(i * tile, 128), tile)],
-            stage_sem.at[slot],
-        )
-
-    def down_tiles(low, high):
-        def step(i, _):
-            slot = lax.rem(i, 2)
-            down_copy(i, slot).wait()
-            col_copy(i, slot).wait()
-            cols = dy_cols[slot].reshape(count * rows, tile)
-            down_stage[slot] = mm_tn(hs_all[...], cols).astype(BF)
-            down_copy(i, slot).start()
-
-            @pl.when(i + 2 < width // tile)
+    quarter = width // 4
+
+    def owner(j):
+        return jnp.where(
+            j == 0, others[0], jnp.where(j == 1, others[1], jnp.where(j == 2, others[2], mine))
+        )
+
+    def cols_of(dp):
+        return pl.ds(pl.multiple_of(dp * quarter, 128), quarter)
+
+    def tile_slot(kind, j):
+        if kind == 0:
+            return stage.at[j]
+        return (gl_all, ul_all)[kind - 1].at[pl.ds(pl.multiple_of(j * quarter, 16), quarter)]
+
+    def tile_copy(kind, j):
+        return pltpu.make_async_remote_copy(
+            tile_slot(kind, j), landing.at[mine, kind], tile_send.at[kind, j],
+            tile_recv.at[mine, kind], device_id={"dp": owner(j)}, device_id_type=MESH,
+        )
+
+    def col_copy(j):
+        return pltpu.make_async_copy(dy_ref.at[:, :, cols_of(owner(j))], dy_cols, cols_sem)
+
+    def tiles(kind, low, high):
+        def step(j, _):
+            cols = cols_of(owner(j))
+            if kind == 2:
+                col_copy(j).wait()
+                tile = mm_tn(dy_cols[...].reshape(count * rows, quarter), hs_all[...])
+
+                @pl.when(j < 3)
+                def _():
+                    col_copy(j + 1).start()
+            else:
+                tile = mm_tn(n2_all[:, cols], (gl_all, ul_all)[kind][...])
+            tile = tile.astype(BF)
+
+            @pl.when(j < 3)
             def _():
-                col_copy(i + 2, slot).start()
+                tile_slot(kind, j)[...] = tile
+                tile_copy(kind, j).start()
+
+            @pl.when(j == 3)
+            def _():
+                kept[kind] = tile
 
             return 0
 
@@ -754,23 +761,18 @@
         def _():
             pass_on(zd, h, jnp.where(right, z + 1, z - 1), True)
 
-    col_copy(0, 0).start()
-    col_copy(1, 1).start()
-    tiles = width // tile
-    jobs = [
-        lambda: weight_tiles(dgw_ref, gl_all, 0, tiles // 2, True),
-        lambda: weight_tiles(dgw_ref, gl_all, tiles // 2, tiles, True),
-        lambda: weight_tiles(duw_ref, ul_all, 0, tiles // 2, False),
-        lambda: weight_tiles(duw_ref, ul_all, tiles // 2, tiles, False),
-        lambda: down_tiles(0, tiles // 2),
-        lambda: down_tiles(tiles // 2, tiles),
-    ]
+    col_copy(0).start()
+    jobs = [lambda k=kind, i=i: tiles(k, i, i + 2) for kind in range(3) for i in (0, 2)]
+    eighth = count // 4
+    jobs += [lambda i=i: sums(i * eighth, (i + 1) * eighth) for i in range(4)]
     for r in range(2, depth):
         for first in (True, False):
             for h in range(2):
+                if first or r == depth - 1:
+                    for _ in range(2 if r == 2 else 1):
+                        if jobs:
+                            jobs.pop(0)()
                 flow(r, first, h)
-                if jobs and (first or r == depth - 1):
-                    jobs.pop(0)()
     while jobs:
         jobs.pop(0)()
 
@@ -812,6 +814,43 @@
 
     gg_ref[...] = jnp.sum(gg_in[...], axis=0)
 
+    def tile_load(kind, i):
+        into = (gl_all, ul_all, hs_all)[kind]
+        return pltpu.make_async_copy(
+            landing.at[others[i], kind], into.at[pl.ds((3 + i) * quarter, quarter)], load_sem.at[kind, i]
+        )
+
+    keeps = [
+        pltpu.make_async_copy(kept.at[pl.ds(0, 2)], wide_ref, keep_sem.at[0]),
+        pltpu.make_async_copy(down_kept, down_ref, keep_sem.at[1]),
+    ]
+    for kind in range(3):
+        for i in range(3):
+            pltpu.make_async_remote_copy(
+                stage.at[0], landing.at[others[i], kind], tile_send.at[kind, i],
+                tile_recv.at[others[i], kind], device_id={"dp": others[i]}, device_id_type=MESH,
+            ).wait_recv()
+            tile_load(kind, i).start()
+    for kind in range(3):
+        for i in range(3):
+            tile_load(kind, i).wait()
+        into = (gl_all, ul_all, hs_all)[kind]
+
+        def add_up(i, _):
+            rr = pl.ds(pl.multiple_of(i * 128, 128), 128)
+            total = kept[kind, rr, :].astype(F32)
+            for j in range(3):
+                total = total + into[pl.ds(pl.multiple_of((3 + j) * quarter + i * 128, 128), 128), :].astype(F32)
+            if kind == 2:
+                down_kept[:, rr] = jnp.transpose(total).astype(BF)
+            else:
+                kept[kind, rr, :] = total.astype(BF)
+            return 0
+
+        lax.fori_loop(0, quarter // 128, add_up, 0)
+        if kind > 0:
+            keeps[kind - 1].start()
+
     for e in range(count):
 
         @pl.when(e != me)
@@ -844,8 +883,11 @@
             def _():
                 zin_copy(zd, h, z, zd).wait_send()
 
-    for slot in range(2):
-        down_copy(0, slot).wait()
+    for kind in range(3):
+        for j in range(3):
+            tile_copy(kind, j).wait_send()
+    for keep in keeps:
+        keep.wait()
 
 
 def expert_pass(n2, gate_rows, dy_all, gate_w, up_w, down_w):
@@ -861,9 +903,9 @@
         jax.ShapeDtypeStruct((rows, width), F32),
         jax.ShapeDtypeStruct((count, lanes), F32),
         jax.ShapeDtypeStruct((count, rows, width), BF),
-        jax.ShapeDtypeStruct((width, ff), BF),
-        jax.ShapeDtypeStruct((width, ff), BF),
-        jax.ShapeDtypeStruct((ff, width), BF),
+        jax.ShapeDtypeStruct((2, width // 4, ff), BF),
+        jax.ShapeDtypeStruct((ff, width // 4), BF),
+        jax.ShapeDtypeStruct((4, 3, width // 4, ff), BF),
     )
     return pl.pallas_call(
         expert_kernel,
@@ -875,7 +917,7 @@
             pltpu.VMEM((count * rows, width), BF),
             pltpu.VMEM((count, count, lanes), F32),
             pltpu.VMEM((2, rows, width), BF),
-            pltpu.VMEM((2, count, rows, 256), BF),
+            pltpu.VMEM((count, rows, width // 4), BF),
             pltpu.VMEM((count * rows, ff), BF),
             pltpu.VMEM((count * rows, ff), BF),
             pltpu.VMEM((count * rows, ff), BF),
@@ -884,11 +926,13 @@
             pltpu.VMEM((depth + 1, rows, width), BF),
             pltpu.VMEM((count, count, lanes), F32),
             pltpu.VMEM((count, count, lanes), F32),
-            pltpu.VMEM((2, 256, ff), BF),
-            pltpu.VMEM((2, ff, 256), BF),
+            pltpu.VMEM((3, width // 4, ff), BF),
+            pltpu.VMEM((3, width // 4, ff), BF),
+            pltpu.VMEM((ff, width // 4), BF),
             dma((count, 3)), dma((count,)), dma((count, 3)), dma((count,)),
             dma((depth,)), dma((depth,)), dma((depth, 2)), dma((depth + 1, 2)),
-            dma((count,)), dma((count,)), dma((2,)), dma((2,)), dma((count,)), dma((2,)),
+            dma((count,)), dma((count,)), dma((2,)), dma, dma((count,)), dma((3, 3)), dma((4, 3)),
+            dma((3, 3)), dma((2,)),
         ],
         compiler_params=pltpu.CompilerParams(
             collective_id=2, has_side_effects=True, vmem_limit_bytes=62 * 2**20
@@ -897,295 +941,6 @@
             flops=18 * count * rows * width * ff, bytes_accessed=60 * 2**20, transcendentals=0
         ),
     )(n2, gate_rows, dy_all, gate_w, up_w, down_w)
-
-
-def scatter_kernel(
-    w_ref, es_ref,
-    share_ref, sum_ref,
-    w, es, wsib, ra, rb, ra2, rb2, wz, esib, ez,
-    ws_send, ws_recv, a_send, a_recv, b_send, b_recv, a2_send, a2_recv, b2_send, b2_recv,
-    wz_send, wz_recv, es_send, es_recv, ez_send, ez_recv, w_sem, e_sem,
-):
-    depth = es_ref.shape[0] // 2
-    rows, width = es_ref.shape[1:]
-    shard, total = w_ref.shape[3:]
-    cut = ra.shape[3]
-    half = rows // 2
-    me, mine = lax.axis_index("expert"), lax.axis_index("dp")
-    z, core = me // 2, me % 2
-    y, x = mine // 2, mine % 2
-    xn, yn, diag = y * 2 + 1 - x, (1 - y) * 2 + x, (1 - y) * 2 + 1 - x
-    sibling = {"expert": z * 2 + 1 - core}
-
-    def at(zz):
-        return {"expert": zz * 2 + core}
-
-    greet(depth, z, at, (sibling, {"dp": xn}, {"dp": yn}))
-
-    def remote(src, dst, send, recv, target):
-        return pltpu.make_async_remote_copy(
-            src, dst, send, recv, device_id=target, device_id_type=MESH
-        )
-
-    def ws_copy(dp):
-        return remote(w_ref.at[dp, :, 1 - core], wsib.at[dp], ws_send.at[dp], ws_recv.at[dp], sibling)
-
-    def w_load(dp):
-        return pltpu.make_async_copy(w_ref.at[dp, :, core], w.at[dp], w_sem.at[dp])
-
-    def es_copy(zd):
-        return remote(es_ref.at[2 * zd + 1 - core], esib.at[zd], es_send.at[zd], es_recv.at[zd], sibling)
-
-    def es_load(zd):
-        return pltpu.make_async_copy(es_ref.at[2 * zd + core], es.at[zd], e_sem.at[zd])
-
-    first_cols, last_cols = slice(0, cut), slice(cut, total)
-
-    def a_copy(yy):
-        return remote(
-            w.at[yy * 2 + 1 - x, :, :, first_cols], ra.at[yy], a_send.at[yy], a_recv.at[yy], {"dp": xn}
-        )
-
-    def b_copy(xx):
-        return remote(
-            w.at[(1 - y) * 2 + xx, :, :, last_cols], rb.at[xx], b_send.at[xx], b_recv.at[xx], {"dp": yn}
-        )
-
-    def a2_copy():
-        return remote(w.at[yn, :, :, first_cols], ra2, a2_send, a2_recv, {"dp": yn})
-
-    def b2_copy():
-        return remote(w.at[xn, :, :, last_cols], rb2, b2_send, b2_recv, {"dp": xn})
-
-    def wz_copy(zd, nxt, slot):
-        return remote(w.at[mine, zd], wz.at[slot], wz_send.at[zd], wz_recv.at[slot], at(nxt))
-
-    def part(h):
-        return pl.ds(h * half, half)
-
-    def ez_copy(zd, h, nxt, slot):
-        return remote(
-            es.at[zd, part(h)], ez.at[slot, part(h)], ez_send.at[zd, h], ez_recv.at[slot, h], at(nxt)
-        )
-
-    for dp in (xn, diag, yn, mine):
-        ws_copy(dp).start()
-        w_load(dp).start()
-    for zd in range(depth):
-        es_copy(zd).start()
-        es_load(zd).start()
-
-    block = 16
-
-    def add(into, term):
-        def step(i, _):
-            zz, rr = i // (shard // block), pl.ds(pl.multiple_of(lax.rem(i, shard // block) * block, block), block)
-            into[zz, rr, :] = (into[zz, rr, :].astype(F32) + term[zz, rr, :].astype(F32)).astype(BF)
-            return 0
-
-        lax.fori_loop(0, depth * (shard // block), step, 0)
-
-    def combine(dp):
-        w_load(dp).wait()
-        ws_copy(dp).wait_recv()
-        add(w.at[dp], wsib.at[dp])
-
-    combine(xn)
-    a_copy(y).start()
-    combine(diag)
-    a_copy(1 - y).start()
-    b_copy(1 - x).start()
-    combine(yn)
-    b_copy(x).start()
-
-    def slot_for(zd, nxt):
-        return jnp.where((nxt == zd) & (nxt < z), depth, zd)
-
-    def rows_on(zd, h, nxt, with_in):
-        if h == 0:
-            es_load(zd).wait()
-            es_copy(zd).wait_recv()
-        if with_in:
-            ez_copy(zd, h, nxt, zd).wait_recv()
-
-        def step(i, _):
-            rr = pl.ds(pl.multiple_of(h * half + i * block, block), block)
-            value = es[zd, rr, :].astype(F32) + esib[zd, rr, :].astype(F32)
-            if with_in:
-                value = value + ez[zd, rr, :].astype(F32)
-            es[zd, rr, :] = value.astype(BF)
-            return 0
-
-        lax.fori_loop(0, half // block, step, 0)
-        ez_copy(zd, h, nxt, slot_for(zd, nxt)).start()
-
-    def shard_on(zd, nxt, with_in):
-        if with_in:
-            wz_copy(zd, nxt, zd).wait_recv()
-
-            def step(i, _):
-                rr = pl.ds(pl.multiple_of(i * block, block), block)
-                w[mine, zd, rr, :] = (w[mine, zd, rr, :].astype(F32) + wz[zd, rr, :].astype(F32)).astype(BF)
-                return 0
-
-            lax.fori_loop(0, shard // block, step, 0)
-        wz_copy(zd, nxt, slot_for(zd, nxt)).start()
-
-    end = (z == 0) | (z == depth - 1)
-
-    def from_end(d, action):
-        @pl.when(end)
-        def _():
-            action(jnp.where(z == 0, d, depth - 1 - d), jnp.where(z == 0, 1, depth - 2))
-
-    def flow(r, first, action):
-        right = (z < depth - 1 - z) if first else (z >= depth - 1 - z)
-        zd = jnp.where(right, r, depth - 1 - r)
-        valid = jnp.where(right, (z < zd) & (z > 0), (z > zd) & (z < depth - 1))
-
-        @pl.when(valid)
-        def _():
-            action(zd, jnp.where(right, z + 1, z - 1))
-
-    for d in range(1, depth):
-        for h in range(2):
-            from_end(d, lambda zd, nxt, h=h: rows_on(zd, h, nxt, False))
-    combine(mine)
-    for h in range(2):
-        flow(2, True, lambda zd, nxt, h=h: rows_on(zd, h, nxt, True))
-
-    a_copy(1 - y).wait_recv()
-    add(w.at[yn, :, :, first_cols], ra.at[1 - y])
-    a2_copy().start()
-    b_copy(1 - x).wait_recv()
-    add(w.at[xn, :, :, last_cols], rb.at[1 - x])
-    b2_copy().start()
-    a_copy(y).wait_recv()
-    add(w.at[mine, :, :, first_cols], ra.at[y])
-    b_copy(x).wait_recv()
-    add(w.at[mine, :, :, last_cols], rb.at[x])
-    for r in range(2, depth):
-        for first in (True, False):
-            if (r, first) == (2, True):
-                continue
-            for h in range(2):
-                flow(r, first, lambda zd, nxt, h=h: rows_on(zd, h, nxt, True))
-    a2_copy().wait_recv()
-    add(w.at[mine, :, :, first_cols], ra2)
-    b2_copy().wait_recv()
-    add(w.at[mine, :, :, last_cols], rb2)
-    for d in range(1, depth):
-        from_end(d, lambda zd, nxt: shard_on(zd, nxt, False))
-    for r in range(2, depth):
-        for first in (True, False):
-            flow(r, first, lambda zd, nxt: shard_on(zd, nxt, True))
-
-    es_load(z).wait()
-    es_copy(z).wait_recv()
-
-    @pl.when(z > 0)
-    def _():
-        for h in range(2):
-            ez_copy(z, h, z, z).wait_recv()
-
-    @pl.when(z < depth - 1)
-    def _():
-        for h in range(2):
-            ez_copy(z, h, z, depth).wait_recv()
-
-    def last_rows(i, _):
-        rr = pl.ds(pl.multiple_of(i * block, block), block)
-        sum_ref[rr, :] = es[z, rr, :].astype(F32) + esib[z, rr, :].astype(F32)
-
-        @pl.when(z > 0)
-        def _():
-            sum_ref[rr, :] += ez[z, rr, :].astype(F32)
-
-        @pl.when(z < depth - 1)
-        def _():
-            sum_ref[rr, :] += ez[depth, rr, :].astype(F32)
-
-        return 0
-
-    lax.fori_loop(0, rows // block, last_rows, 0)
-
-    @pl.when(z > 0)
-    def _():
-        wz_copy(z, z, z).wait_recv()
-
-    @pl.when(z < depth - 1)
-    def _():
-        wz_copy(z, z, depth).wait_recv()
-
-    share_ref[...] = w[mine, z].astype(F32)
-
-    @pl.when(z > 0)
-    def _():
-        share_ref[...] += wz[z].astype(F32)
-
-    @pl.when(z < depth - 1)
-    def _():
-        share_ref[...] += wz[depth].astype(F32)
-
-    for dp in range(w.shape[0]):
-        ws_copy(dp).wait_send()
-    for i in range(2):
-        a_copy(i).wait_send()
-        b_copy(i).wait_send()
-    a2_copy().wait_send()
-    b2_copy().wait_send()
-    for zd in range(depth):
-        es_copy(zd).wait_send()
-
-        @pl.when(zd != z)
-        def _():
-            wz_copy(zd, z, zd).wait_send()
-            for h in range(2):
-                ez_copy(zd, h, z, zd).wait_send()
-
-
-def scatter_pass(w_grads, sums):
-    planes = lax.axis_size("dp")
-    count = lax.axis_size("expert")
-    depth = count // 2
-    shard, total = w_grads.shape[1:]
-    rows, width = sums.shape[1:]
-    cut = total // 2 // 128 * 128 + 128
-    dma = pltpu.SemaphoreType.DMA
-    vmem = pl.BlockSpec(memory_space=pltpu.VMEM)
-    anywhere = pl.BlockSpec(memory_space=pl.ANY)
-    return pl.pallas_call(
-        scatter_kernel,
-        name="scatter_pass",
-        out_shape=(
-            jax.ShapeDtypeStruct((shard, total), F32),
-            jax.ShapeDtypeStruct((rows, width), F32),
-        ),
-        in_specs=[anywhere, anywhere],
-        out_specs=(vmem, vmem),
-        scratch_shapes=[
-            pltpu.VMEM((planes, depth, shard, total), BF),
-            pltpu.VMEM((depth, rows, width), BF),
-            pltpu.VMEM((planes, depth, shard, total), BF),
-            pltpu.VMEM((2, depth, shard, cut), BF),
-            pltpu.VMEM((2, depth, shard, total - cut), BF),
-            pltpu.VMEM((depth, shard, cut), BF),
-            pltpu.VMEM((depth, shard, total - cut), BF),
-            pltpu.VMEM((depth + 1, shard, total), BF),
-            pltpu.VMEM((depth, rows, width), BF),
-            pltpu.VMEM((depth + 1, rows, width), BF),
-            dma((planes,)), dma((planes,)), dma((2,)), dma((2,)), dma((2,)), dma((2,)),
-            dma, dma, dma, dma,
-            dma((depth,)), dma((depth + 1,)), dma((depth,)), dma((depth,)),
-            dma((depth, 2)), dma((depth + 1, 2)), dma((planes,)), dma((depth,)),
-        ],
-        compiler_params=pltpu.CompilerParams(
-            collective_id=3, has_side_effects=True, vmem_limit_bytes=60 * 2**20
-        ),
-        cost_estimate=pl.CostEstimate(
-            flops=10**9, bytes_accessed=200 * 2**20, transcendentals=0
-        ),
-    )(w_grads.reshape(planes, depth, 2, shard, total), sums)
 
 
 def greet(depth, z, at, targets):
@@ -1574,18 +1329,505 @@
     )(x, shard, cos, sin, bias, hits)
 
 
+def backward_kernel(
+    x_ref, dy_ref, gate_ref, gg_ref, n1_ref, q_ref, kv_ref, mixed_ref, n2_ref, lse_ref,
+    cos_ref, sin_ref, bias_ref, middle_any, row_ref, w_full, wide_ref, down_ref,
+    tok_ref, share_ref, wide_all, down_all,
+    middle, wbuf, wsmall, attended, mixed_grad, qg, dkv, kv_low, kv_in, w, wsib, legs, legs2, wz,
+    load_sem, ag_local, ag_xs, ag_xr, ag_ys, ag_yr, ag_fs, ag_fr, kv_send, kv_recv,
+    ws_send, ws_recv, a_send, a_recv, b_send, b_recv, a2_send, a2_recv, b2_send, b2_recv,
+    wz_send, wz_recv,
+):
+    depth = lax.axis_size("expert") // 2
+    rows, width = x_ref.shape
+    heads = q_ref.shape[1] // HEAD_SIZE
+    kv_width = kv_ref.shape[1]
+    groups = kv_width // (2 * HEAD_SIZE)
+    group = heads // groups
+    wide = heads * HEAD_SIZE
+    qkv_width = wide + kv_width
+    split = qkv_width + 128
+    shard, total = share_ref.shape
+    me, mine = lax.axis_index("expert"), lax.axis_index("dp")
+    z, core = me // 2, me % 2
+    y, x = mine // 2, mine % 2
+    xn, yn, diag = y * 2 + 1 - x, (1 - y) * 2 + x, (1 - y) * 2 + 1 - x
+    sibling = {"expert": z * 2 + 1 - core}
+
+    def at(zz):
+        return {"expert": zz * 2 + core}
+
+    greet(depth, z, at, (sibling, {"dp": xn}, {"dp": yn}, {"dp": diag}))
+
+    def remote(src, dst, send, recv, target):
+        return pltpu.make_async_remote_copy(
+            src, dst, send, recv, device_id=target, device_id_type=MESH
+        )
+
+    def load(src, dst, i):
+        return pltpu.make_async_copy(src, dst, load_sem.at[i])
+
+    load_rows = load(row_ref, tok_ref, 0)
+    load_out = load(w_full.at[:, pl.ds(split, width)], wbuf.at[:, pl.ds(0, width)], 1)
+    load_small = load(w_full.at[:, pl.ds(qkv_width, 128)], wsmall, 2)
+    load_qkv = load(w_full.at[:, pl.ds(0, qkv_width)], wbuf, 3)
+    load_middle = load(middle_any, middle, 4)
+    load_small.start()
+    load_rows.start()
+    load_middle.start()
+    load_out.start()
+
+    quarter = wide_ref.shape[1]
+    down_half = down_ref.shape[0] // 2
+
+    def quarter_of(piece, dp):
+        span = pl.ds(pl.multiple_of(dp * quarter, 128), quarter)
+        if piece < 2:
+            return wide_all.at[piece, span]
+        return down_all.at[pl.ds((piece - 2) * down_half, down_half), span]
+
+    def own_quarter(piece):
+        if piece < 2:
+            return wide_ref.at[piece]
+        return down_ref.at[pl.ds((piece - 2) * down_half, down_half)]
+
+    def keep_quarter(piece):
+        return pltpu.make_async_copy(own_quarter(piece), quarter_of(piece, mine), ag_local.at[piece])
+
+    def quarter_x(piece, dp):
+        return remote(own_quarter(piece), quarter_of(piece, dp), ag_xs.at[piece], ag_xr.at[piece], {"dp": xn})
+
+    def quarter_y(piece, dp):
+        return remote(own_quarter(piece), quarter_of(piece, dp), ag_ys.at[piece], ag_yr.at[piece], {"dp": yn})
+
+    def quarter_on(piece, dp, target):
+        ref = quarter_of(piece, dp)
+        return remote(ref, ref, ag_fs.at[piece], ag_fr.at[piece], target)
+
+    for piece in range(4):
+        quarter_x(piece, mine).start()
+        quarter_y(piece, mine).start()
+        keep_quarter(piece).start()
+
+    def quarters_on(first):
+        for piece in (0, 1) if first else (2, 3):
+            if piece % 2 == 0:
+                quarter_x(piece, xn).wait_recv()
+                quarter_on(piece, xn, {"dp": yn}).start()
+            else:
+                quarter_y(piece, yn).wait_recv()
+                quarter_on(piece, yn, {"dp": xn}).start()
+
+    bounds = ((split, total), (0, wide // 2), (wide // 2, wide), (wide, split))
+    cuts = tuple(low + ((high - low) // 128 + 1) // 2 * 128 for low, high in bounds)
+
+    def span(low, high):
+        return pl.ds(low, high - low)
+
+    def ws_copy(p, dp):
+        cols = span(*bounds[p])
+        return remote(
+            w.at[dp, :, 1 - core, :, cols], wsib.at[dp, :, :, cols],
+            ws_send.at[p, dp], ws_recv.at[p, dp], sibling,
+        )
+
+    def a_cols(p):
+        return span(bounds[p][0], cuts[p])
+
+    def b_cols(p):
+        return span(cuts[p], bounds[p][1])
+
+    def a_copy(p, yy):
+        return remote(
+            w.at[yy * 2 + 1 - x, :, core, :, a_cols(p)], legs.at[yy, :, :, a_cols(p)],
+            a_send.at[p, yy], a_recv.at[p, yy], {"dp": xn},
+        )
+
+    def b_copy(p, xx):
+        return remote(
+            w.at[(1 - y) * 2 + xx, :, core, :, b_cols(p)], legs.at[xx, :, :, b_cols(p)],
+            b_send.at[p, xx], b_recv.at[p, xx], {"dp": yn},
+        )
+
+    def a2_copy(p):
+        return remote(
+            w.at[yn, :, core, :, a_cols(p)], legs2.at[:, :, a_cols(p)], a2_send.at[p], a2_recv.at[p], {"dp": yn}
+        )
+
+    def b2_copy(p):
+        return remote(
+            w.at[xn, :, core, :, b_cols(p)], legs2.at[:, :, b_cols(p)], b2_send.at[p], b2_recv.at[p], {"dp": xn}
+        )
+
+    def wz_copy(p, zd, nxt, slot):
+        cols = span(*bounds[p])
+        return remote(
+            w.at[mine, zd, core, :, cols], wz.at[slot, :, cols], wz_send.at[p, zd], wz_recv.at[p, slot], at(nxt)
+        )
+
+    block = 16
+    steps = shard // block
+
+    def add(dp, term, cols):
+        def step(i, _):
+            zz, rr = i // steps, pl.ds(pl.multiple_of(lax.rem(i, steps) * block, block), block)
+            value = w[dp, zz, core, rr, cols].astype(F32) + term[zz, rr, cols].astype(F32)
+            w[dp, zz, core, rr, cols] = value.astype(BF)
+            return 0
+
+        lax.fori_loop(0, depth * steps, step, 0)
+
+    def begin(p):
+        for dp in (xn, diag, yn, mine):
+            ws_copy(p, dp).start()
+
+    def first_legs(p):
+        def combine(dp):
+            ws_copy(p, dp).wait_recv()
+            add(dp, wsib.at[dp], span(*bounds[p]))
+
+        combine(xn)
+        a_copy(p, y).start()
+        combine(diag)
+        a_copy(p, 1 - y).start()
+        b_copy(p, 1 - x).start()
+        combine(yn)
+        b_copy(p, x).start()
+        combine(mine)
+
+    def second_legs(p):
+        a_copy(p, 1 - y).wait_recv()
+        add(yn, legs.at[1 - y], a_cols(p))
+        a2_copy(p).start()
+        b_copy(p, 1 - x).wait_recv()
+        add(xn, legs.at[1 - x], b_cols(p))
+        b2_copy(p).start()
+        a_copy(p, y).wait_recv()
+        add(mine, legs.at[y], a_cols(p))
+        b_copy(p, x).wait_recv()
+        add(mine, legs.at[x], b_cols(p))
+
+    def slot_for(zd, nxt):
+        return jnp.where((nxt == zd) & (nxt < z), depth, zd)
+
+    def line(p):
+        a2_copy(p).wait_recv()
+        add(mine, legs2, a_cols(p))
+        b2_copy(p).wait_recv()
+        add(mine, legs2, b_cols(p))
+
+        @pl.when((z == 0) | (z == depth - 1))
+        def _():
+            nxt = jnp.where(z == 0, 1, depth - 2)
+            for d in range(1, depth):
+                zd = jnp.where(z == 0, depth - d, d - 1)
+                wz_copy(p, zd, nxt, slot_for(zd, nxt)).start()
+
+    def line_on(p):
+        cols = span(*bounds[p])
+        for r in range(depth - 1, 1, -1):
+            for first in (True, False):
+                right = (z < depth - 1 - z) if first else (z >= depth - 1 - z)
+                zd = jnp.where(right, r, depth - 1 - r)
+                nxt = jnp.where(right, z + 1, z - 1)
+                valid = jnp.where(right, (z < zd) & (z > 0), (z > zd) & (z < depth - 1))
+
+                @pl.when(valid)
+                def _():
+                    wz_copy(p, zd, nxt, zd).wait_recv()
+
+                    def step(i, _):
+                        rr = pl.ds(pl.multiple_of(i * block, block), block)
+                        value = w[mine, zd, core, rr, cols].astype(F32) + wz[zd, rr, cols].astype(F32)
+                        w[mine, zd, core, rr, cols] = value.astype(BF)
+                        return 0
+
+                    lax.fori_loop(0, steps, step, 0)
+                    wz_copy(p, zd, nxt, slot_for(zd, nxt)).start()
+
+    def line_end(p):
+        cols = span(*bounds[p])
+        share_ref[:, cols] = w[mine, z, core, :, cols].astype(F32)
+
+        @pl.when(z > 0)
+        def _():
+            wz_copy(p, z, z, z).wait_recv()
+            share_ref[:, cols] += wz[z, :, cols].astype(F32)
+
+        @pl.when(z < depth - 1)
+        def _():
+            wz_copy(p, z, z, depth).wait_recv()
+            share_ref[:, cols] += wz[depth, :, cols].astype(F32)
+
+    def weight_rows(left, right, low, size):
+        quarter_rows = width // 4
+
+        def step(i, _):
+            cols = pl.ds(pl.multiple_of(i * quarter_rows, 128), quarter_rows)
+            tile = mm_tn(left[:, cols], right).astype(BF)
+            w[i, :, :, :, low : low + size] = tile.reshape(depth, 2, shard, size)
+            return 0
+
+        lax.fori_loop(0, 4, step, 0)
+
+    experts = gate_ref.shape[0]
+    gates, gate_grad = gate_ref[:, :rows], gg_ref[:, :rows]
+    logit_grad = gates * (gate_grad - jnp.sum(gates * gate_grad, axis=0, keepdims=True))
+    high = logit_grad.astype(BF)
+    logit_two = jnp.concatenate([high.astype(F32), logit_grad - high.astype(F32)], axis=0).astype(BF)
+    load_small.wait()
+    small = jnp.transpose(wsmall[...].astype(F32))
+    router = small[:experts].astype(BF).astype(F32)
+    router_two = jnp.concatenate([router, router], axis=0).astype(BF)
+    gain_one, gain_two = small[experts : experts + 1], small[experts + 1 : experts + 2]
+    router_grad = mm(logit_two, n2_ref[...])
+    router_grad = router_grad[:experts] + router_grad[experts:]
+    load_rows.wait()
+    load_middle.wait()
+    tok_ref[...] += mm_tn(logit_two, router_two)
+
+    def norm_back(value, grad, gain):
+        scale = lax.rsqrt(jnp.mean(value * value, axis=1, keepdims=True) + EPS)
+        unit = value * scale
+        scaled = grad * gain
+        back = scale * (scaled - unit * jnp.mean(scaled * unit, axis=1, keepdims=True))
+        return back, jnp.sum(grad * unit, axis=0, keepdims=True)
+
+    def second_norm(i, carry):
+        rr = pl.ds(pl.multiple_of(i * block, block), block)
+        back, gain = norm_back(middle[rr, :], tok_ref[rr, :], gain_two)
+        back = back + dy_ref[rr, :].astype(F32)
+        tok_ref[rr, :] = back
+        attended[rr, :] = back.astype(BF)
+        return carry + gain
+
+    gain_two_grad = lax.fori_loop(0, rows // block, second_norm, jnp.zeros((1, width), F32))
+    weight_rows(mixed_ref, attended[...], split, width)
+    begin(0)
+    load_out.wait()
+    tile = 512
+
+    def mixed_step(i, _):
+        out_rows = pl.ds(pl.multiple_of(i * tile, tile), tile)
+        mixed_grad[:, out_rows] = mm_nt(attended[...], wbuf[out_rows, :width]).astype(BF)
+        return 0
+
+    lax.fori_loop(0, wide // tile, mixed_step, 0)
+    load_qkv.start()
+    first_legs(0)
+
+    lanes = lax.broadcasted_iota(jnp.int32, lse_ref.shape, 1)
+
+    def turn_back(value):
+        return value * cos_ref[...] - pltpu.roll(value, HEAD_SIZE // 2, 1) * sin_ref[...]
+
+    def kv_copy(g, i):
+        dp = (xn, diag, yn)[i]
+        return remote(
+            kv_low.at[g, pl.ds(pl.multiple_of(dp * rows, 16), rows)], kv_in.at[g, mine],
+            kv_send.at[g, i], kv_recv.at[g, mine], {"dp": dp},
+        )
+
+    def attend_group(g, polls):
+        low = 2 * g * HEAD_SIZE
+        key, value = kv_ref[:, low : low + HEAD_SIZE], kv_ref[:, low + HEAD_SIZE : low + 2 * HEAD_SIZE]
+
+        def attend(i, _):
+            for j, job in polls.items():
+                pl.when(i == j)(lambda job=job: (job(), None)[1])
+            h = g * group + i
+            cols = pl.ds(pl.multiple_of(h * HEAD_SIZE, HEAD_SIZE), HEAD_SIZE)
+            query, grad = q_ref[:, cols], mixed_grad[:, cols]
+            level = jnp.sum(jnp.where(lanes == h, lse_ref[...], 0.0), axis=1, keepdims=True)
+            scores = mm_nt(query, key) * (HEAD_SIZE**-0.5 * LOG2E) + bias_ref[...]
+            attn = jnp.exp2(scores - level)
+            attn_grad = mm_nt(grad, value)
+            mean = jnp.sum(attn * attn_grad, axis=1, keepdims=True)
+            score_grad = (attn * (attn_grad - mean)).astype(BF)
+            value_term = mm_tn(attn.astype(BF), grad)
+            key_term = mm_tn(score_grad, query)
+            qg[:, cols] = turn_back(mm(score_grad, key) * HEAD_SIZE**-0.5).astype(BF)
+
+            @pl.when(i == 0)
+            def _():
+                dkv[:, :HEAD_SIZE] = key_term
+                dkv[:, HEAD_SIZE:] = value_term
+
+            @pl.when(i > 0)
+            def _():
+                dkv[:, :HEAD_SIZE] += key_term
+                dkv[:, HEAD_SIZE:] += value_term
+
+            return 0
+
+        lax.fori_loop(0, group, attend, 0)
+        kv_low[g, :, :HEAD_SIZE] = (dkv[:, :HEAD_SIZE] * HEAD_SIZE**-0.5).astype(BF)
+        kv_low[g, :, HEAD_SIZE:] = dkv[:, HEAD_SIZE:].astype(BF)
+        for i in range(3):
+            kv_copy(g, i).start()
+        weight_rows(n1_ref, qg[:, g * wide // 2 : (g + 1) * wide // 2], g * wide // 2, wide // 2)
+        begin(1 + g)
+        first_legs(1 + g)
+
+    attend_group(0, {})
+    attend_group(1, {2: lambda: second_legs(0)})
+
+    def kv_sum(g):
+        for i in range(3):
+            dp = (xn, diag, yn)[i]
+            remote(
+                kv_low.at[g, pl.ds(0, rows)], kv_in.at[g, dp], kv_send.at[g, i], kv_recv.at[g, dp], {"dp": dp}
+            ).wait_recv()
+        terms = kv_low[g, pl.ds(pl.multiple_of(mine * rows, 16), rows), :].astype(F32)
+        for dp in (xn, diag, yn):
+            terms = terms + kv_in[g, dp].astype(F32)
+        low = wide + 2 * g * HEAD_SIZE
+        qg[:, low : low + HEAD_SIZE] = turn_back(terms[:, :HEAD_SIZE]).astype(BF)
+        qg[:, low + HEAD_SIZE : low + 2 * HEAD_SIZE] = terms[:, HEAD_SIZE:].astype(BF)
+
+    for g in range(groups):
+        kv_sum(g)
+    weight_rows(n1_ref, qg[:, wide:], wide, kv_width)
+    load_qkv.wait()
+
+    def first_grad(i, _):
+        out_rows = pl.ds(pl.multiple_of(i * tile, tile), tile)
+        middle[:, out_rows] = mm_nt(qg[...], wbuf[out_rows, :])
+        return 0
+
+    lax.fori_loop(0, width // tile, first_grad, 0)
+
+    def first_norm(i, carry):
+        rr = pl.ds(pl.multiple_of(i * block, block), block)
+        back, gain = norm_back(x_ref[rr, :].astype(F32), middle[rr, :], gain_one)
+        tok_ref[rr, :] += back
+        return carry + gain
+
+    gain_one_grad = lax.fori_loop(0, rows // block, first_norm, jnp.zeros((1, width), F32))
+    small_grad = jnp.concatenate(
+        [
+            router_grad,
+            gain_one_grad,
+            gain_two_grad,
+            jnp.zeros((128 - experts - 2, width), F32),
+        ],
+        axis=0,
+    )
+    small_grad = jnp.transpose(small_grad).astype(BF)
+    for i in range(4):
+        part = small_grad[i * width // 4 : (i + 1) * width // 4]
+        w[i, :, :, :, qkv_width:split] = part.reshape(depth, 2, shard, 128)
+    begin(3)
+    quarters_on(True)
+    first_legs(3)
+    second_legs(1)
+    quarters_on(False)
+    line(0)
+    second_legs(2)
+    line_on(0)
+    line(1)
+    second_legs(3)
+    line_on(1)
+    line(2)
+    line_on(2)
+    line(3)
+    line_on(3)
+    for p in range(4):
+        line_end(p)
+
+    for piece in range(4):
+        keep_quarter(piece).wait()
+        quarter_x(piece, mine).wait_send()
+        quarter_y(piece, mine).wait_send()
+        if piece % 2 == 0:
+            quarter_y(piece, yn).wait_recv()
+        else:
+            quarter_x(piece, xn).wait_recv()
+        quarter_on(piece, diag, {"dp": xn}).wait()
+    for g in range(groups):
+        for i in range(3):
+            kv_copy(g, i).wait_send()
+    for p in range(4):
+        for dp in range(4):
+            ws_copy(p, dp).wait_send()
+        for i in range(2):
+            a_copy(p, i).wait_send()
+            b_copy(p, i).wait_send()
+        a2_copy(p).wait_send()
+        b2_copy(p).wait_send()
+        for zd in range(depth):
+
+            @pl.when(zd != z)
+            def _():
+                wz_copy(p, zd, z, zd).wait_send()
+
+
+def backward_pass(
+    x, dy, middle, gates, gate_grads, n1, q, kv, mixed, n2, logs, cos, sin, bias, row_sum, w_full,
+    wide_part, down_part,
+):
+    depth = lax.axis_size("expert") // 2
+    rows, width = x.shape
+    total = w_full.shape[1]
+    shard = w_full.shape[0] // (4 * 2 * depth)
+    kv_width = kv.shape[1]
+    groups = kv_width // (2 * HEAD_SIZE)
+    qkv_width = q.shape[1] + kv_width
+    dma = pltpu.SemaphoreType.DMA
+    vmem = pl.BlockSpec(memory_space=pltpu.VMEM)
+    anywhere = pl.BlockSpec(memory_space=pl.ANY)
+    shape = jax.ShapeDtypeStruct
+    parts = 4
+    return pl.pallas_call(
+        backward_kernel,
+        name="backward_pass",
+        out_shape=(
+            shape((rows, width), F32),
+            shape((shard, total), F32),
+            shape((2, 4 * wide_part.shape[1], wide_part.shape[2]), BF),
+            shape((down_part.shape[0], 4 * down_part.shape[1]), BF),
+        ),
+        in_specs=[vmem] * 13 + [anywhere] * 5,
+        out_specs=(vmem, vmem, anywhere, anywhere),
+        scratch_shapes=[
+            pltpu.VMEM((rows, width), F32),
+            pltpu.VMEM((width, qkv_width), BF),
+            pltpu.VMEM((width, 128), BF),
+            pltpu.VMEM((rows, width), BF),
+            pltpu.VMEM((rows, q.shape[1]), BF),
+            pltpu.VMEM((rows, qkv_width), BF),
+            pltpu.VMEM((kv.shape[0], 2 * HEAD_SIZE), F32),
+            pltpu.VMEM((groups, kv.shape[0], 2 * HEAD_SIZE), BF),
+            pltpu.VMEM((groups, 4, rows, 2 * HEAD_SIZE), BF),
+            pltpu.VMEM((4, depth, 2, shard, total), BF),
+            pltpu.VMEM((4, depth, shard, total), BF),
+            pltpu.VMEM((2, depth, shard, total), BF),
+            pltpu.VMEM((depth, shard, total), BF),
+            pltpu.VMEM((depth + 1, shard, total), BF),
+            dma((5,)), dma((4,)), dma((4,)), dma((4,)), dma((4,)), dma((4,)), dma((4,)), dma((4,)),
+            dma((groups, 3)), dma((groups, 4)),
+            dma((parts, 4)), dma((parts, 4)), dma((parts, 2)), dma((parts, 2)), dma((parts, 2)), dma((parts, 2)),
+            dma((parts,)), dma((parts,)), dma((parts,)), dma((parts,)),
+            dma((parts, depth)), dma((parts, depth + 1)),
+        ],
+        compiler_params=pltpu.CompilerParams(
+            collective_id=3, has_side_effects=True, vmem_limit_bytes=63 * 2**20
+        ),
+        cost_estimate=pl.CostEstimate(
+            flops=2 * 10**10, bytes_accessed=200 * 2**20, transcendentals=0
+        ),
+    )(
+        x, dy, gates, gate_grads, n1, q, kv, mixed, n2, logs, cos, sin, bias,
+        middle, row_sum, w_full, wide_part, down_part,
+    )
+
+
 def rotation_rows(positions):
     half = HEAD_SIZE // 2
     frequency = jnp.power(THETA, -(jnp.arange(half, dtype=jnp.float32) * 2.0 / HEAD_SIZE))
     angles = positions.astype(jnp.float32)[:, None] * frequency[None, :]
     cosine, sine = jnp.cos(angles), jnp.sin(angles)
     return jnp.concatenate([cosine, cosine], axis=1), jnp.concatenate([-sine, sine], axis=1)
-
-
-def turn_back(values, cos, sin):
-    half = HEAD_SIZE // 2
-    swapped = jnp.concatenate([values[..., half:], values[..., :half]], axis=-1)
-    return values * cos - swapped * sin
 
 
 def tree_visibility(parent_row, query_ids, tree_length):
@@ -1604,10 +1846,6 @@
         (key_block < trunk) | (key_block == query_block[:, None]) | (key_block == above[:, None])
     )
     return related & (key_ids <= query_ids[:, None]), positions
-
-
-def rows_to_gather(parts):
-    return jnp.concatenate(parts, axis=1)
 
 
 def dense_on_device(
@@ -1627,7 +1865,6 @@
     down_weight,
 ):
     experts = router_weight.shape[1]
-    group = QUERY_HEADS // KEY_VALUE_HEADS
     heads_width = QUERY_HEADS * HEAD_SIZE
     kv_width = 2 * KEY_VALUE_HEADS * HEAD_SIZE
     qkv_width = heads_width + kv_width
@@ -1655,91 +1892,15 @@
     n1, query_low, kv_all, mixed, logs, middle, n2, gate_rows, full = attention_pass(
         inputs_low, shard, cos, sin, bias, hit_rows.astype(F32), kv_width
     )
-    row_sum, gate_grad_rows, sums, gate_w_grad, up_w_grad, down_grad = expert_pass(
+    row_sum, gate_grads, sums, wide_part, down_part, _ = expert_pass(
         n2, gate_rows, dy_all, gate_weight[0], up_weight[0], down_weight[0]
     )
-    gates = gate_rows[:, :total_rows]
-    gate_grad = gate_grad_rows[:, :total_rows]
-    logit_grad = gates * (gate_grad - jnp.sum(gates * gate_grad, axis=0, keepdims=True))
-    qkv_full = full[:, :qkv_width]
-    small_full = full[:, qkv_width : qkv_width + small_width]
-    out_full = full[:, qkv_width + small_width :]
-    router_full = small_full[:, :experts]
-    scale_one = small_full[:, experts].astype(F32)
-    scale_two = small_full[:, experts + 1].astype(F32)
-    inputs = inputs_low.astype(F32)
-    summed = tuple(
-        lax.psum(grad, "dp").astype(jnp.float32)[None]
-        for grad in (gate_w_grad, up_w_grad, down_grad)
-    )
-    router_wide = router_full.astype(jnp.float32)
-    n2_grad = (
-        jnp.einsum("er,de->rd", logit_grad, router_wide, precision=HIGH_PRECISION) + row_sum
-    )
-    router_grad = jnp.einsum(
-        "rd,er->de", n2.astype(jnp.float32), logit_grad, precision=HIGH_PRECISION
-    )
-    upstream = dy_low.astype(jnp.float32)
-    _, second_pull = jax.vjp(normalize, middle, scale_two)
-    middle_norm_grad, second_gain_grad = second_pull(n2_grad)
-    middle_grad = upstream + middle_norm_grad
-    attended_low = middle_grad.astype(jnp.bfloat16)
-    out_grad = jnp.einsum("rd,re->de", mixed, attended_low, preferred_element_type=jnp.float32)
-    mixed_grad = jnp.einsum("re,de->rd", attended_low, out_full, preferred_element_type=jnp.float32)
-    mixed_grad = mixed_grad.astype(jnp.bfloat16).reshape(total_rows, QUERY_HEADS, HEAD_SIZE)
-    query_rotated = query_low.reshape(total_rows, QUERY_HEADS, HEAD_SIZE)
-    query_parts = []
-    kv_parts = []
-    for head in range(KEY_VALUE_HEADS):
-        query_part = query_rotated[:, head * group : (head + 1) * group, :]
-        key_part = kv_all[:, 2 * head * HEAD_SIZE : (2 * head + 1) * HEAD_SIZE]
-        value_part = kv_all[:, (2 * head + 1) * HEAD_SIZE : (2 * head + 2) * HEAD_SIZE]
-        grad_part = mixed_grad[:, head * group : (head + 1) * group, :]
-        scores = jnp.einsum("rgd,kd->grk", query_part, key_part, preferred_element_type=F32)
-        scores = scores * (HEAD_SIZE**-0.5 * LOG2E) + bias
-        log_rows = logs[:, head * group : (head + 1) * group].T[:, :, None]
-        softmax_out = jnp.exp2(scores - log_rows)
-        value_grad = jnp.einsum(
-            "grk,rgd->kd", softmax_out.astype(BF), grad_part, preferred_element_type=F32
-        )
-        attn_grad = jnp.einsum("rgd,kd->grk", grad_part, value_part, preferred_element_type=F32)
-        score_grad = softmax_out * (
-            attn_grad - jnp.sum(softmax_out * attn_grad, axis=-1, keepdims=True)
-        )
-        score_low = score_grad.astype(BF)
-        query_parts.append(
-            jnp.einsum("grk,kd->rgd", score_low, key_part, preferred_element_type=F32)
-            * HEAD_SIZE ** (-0.5)
-        )
-        key_grad = jnp.einsum("grk,rgd->kd", score_low, query_part, preferred_element_type=F32)
-        kv_parts += [key_grad * HEAD_SIZE ** (-0.5), value_grad]
-    kv_sum = lax.psum_scatter(
-        jnp.concatenate(kv_parts, axis=1).astype(BF), "dp", scatter_dimension=0, tiled=True
-    ).astype(F32)
-    query_grad = turn_back(
-        jnp.concatenate(query_parts, axis=1), cos[:, None, :], sin[:, None, :]
-    ).reshape(total_rows, heads_width)
-    kv_grads = []
-    for head in range(KEY_VALUE_HEADS):
-        key_sum = kv_sum[:, 2 * head * HEAD_SIZE : (2 * head + 1) * HEAD_SIZE]
-        kv_grads += [
-            turn_back(key_sum, cos, sin),
-            kv_sum[:, (2 * head + 1) * HEAD_SIZE : (2 * head + 2) * HEAD_SIZE],
-        ]
-    qkv_grad = jnp.concatenate([query_grad, *kv_grads], axis=1).astype(BF)
-    qkv_w_grad = jnp.einsum("rd,re->de", n1, qkv_grad, preferred_element_type=F32)
-    n1_grad = jnp.einsum("re,de->rd", qkv_grad, qkv_full, preferred_element_type=F32)
-    _, first_pull = jax.vjp(normalize, inputs, scale_one)
-    input_norm_grad, first_gain_grad = first_pull(n1_grad)
-    input_grad = (middle_grad + input_norm_grad)[None]
-    small = jnp.concatenate(
-        [router_grad, first_gain_grad[:, None], second_gain_grad[:, None]], axis=1
-    )
-    small = jnp.pad(small, ((0, 0), (0, small_width - small.shape[1])))
-    all_grads = jnp.concatenate([qkv_w_grad, small, out_grad], axis=1).astype(BF)
-    shards = lax.axis_size("dp") * lax.axis_size("expert")
-    share, combined = scatter_pass(all_grads.reshape(shards, -1, all_grads.shape[1]), sums)
-    output = (middle + combined).astype(BF)[None]
+    combined = lax.psum_scatter(sums, "expert", scatter_dimension=0, tiled=True)[0]
+    input_grad, share, wide_grads, down_grad = backward_pass(
+        inputs_low, dy_low, middle, gate_rows, gate_grads, n1, query_low, kv_all, mixed, n2, logs,
+        cos, sin, bias, row_sum, full, wide_part, down_part,
+    )
+    output = (middle + combined.astype(F32)).astype(BF)[None]
     heads_of = [
         share[:, heads_width + i * HEAD_SIZE : heads_width + (i + 1) * HEAD_SIZE]
         for i in range(2 * KEY_VALUE_HEADS)
@@ -1751,7 +1912,7 @@
     out_share = share[:, qkv_width + small_width :]
     return (
         output,
-        input_grad,
+        input_grad[None],
         small_share[:, experts],
         small_share[:, experts + 1],
         query_share,
@@ -1759,7 +1920,9 @@
         value_share,
         out_share,
         small_share[:, :experts],
-        *summed,
+        wide_grads[0].astype(F32)[None],
+        wide_grads[1].astype(F32)[None],
+        down_grad.astype(F32)[None],
     )
 
 

time: 609 us -> 509 us (0.84)
  matrix products: 70.4 us -> 0 us
  Pallas kernels: 418 us -> 459 us
  waiting for transfers between devices: 27.7 us -> 0.72 us
  other arithmetic: 44.4 us -> 19.7 us
  local copies, waits for them, and re-layouts: 28.7 us -> 10.9 us
    dot_general x16 -> x0, matrix products: 70.4 us -> none  [the longest x2 15.8 us: dense_on_device(): jnp.einsum('rgd,kd->grk', query_part, key_part, preferred_element_type=F32)]
    pallas_call x1, Pallas kernels: 156 us -> 186 us  [expert_pass(): pl.pallas_call(expert_kernel, name='expert_pass', out_shape=outs, in_spec...]
    psum x1 -> x0, waiting for transfers between devices: 18.1 us -> none  [dense_on_device(): lax.psum(grad, 'dp').astype(jnp.float32)[None]]
    pallas_call x1, Pallas kernels: 138 us -> 148 us  [backward_pass(): pl.pallas_call(backward_kernel, name='backward_pass', out_shape=(shape((r...]
    reduce_scatter x1, waiting for transfers between devices: 8.84 us -> 0.01 us  [dense_on_device(): lax.psum_scatter(sums, 'expert', scatter_dimension=0, tiled=True)[0]]
    unnamed x86 -> x18, local copies, waits for them, and re-layouts: 14.1 us -> 5.82 us
    concatenate x5 -> x0, other arithmetic: 7.81 us -> none  [the longest x1 5 us: dense_on_device(): jnp.concatenate([qkv_w_grad, small, out_grad], axis=1).astype(BF)]
    broadcast_in_dim x5 -> x2, other arithmetic: 14.8 us -> 7.3 us  [the longest x1 4.65 us: dense_on_device(): down_grad.astype(F32)[None]]
  transfers between devices with their start and end apart: 3 -> 2, of which waited for: 2 -> 0; matrix products, arithmetic and copies ran while one was open for 12% -> 5% of each run, Pallas kernels for 43% -> 54%
where the time goes in v3:
time: 509 us; the launch traced here: 505 us
  Pallas kernels  459 us (90%)
  other arithmetic  19.7 us (4%)
  between operations  14.6 us (3%)
  local copies, waits for them, and re-layouts  10.9 us (2%)
    pallas_call x1, Pallas kernels, expert_pass(): pl.pallas_call(expert_kernel, name='expert_pass', out_shape=outs, in_spec...  186 us
    pallas_call x1, Pallas kernels, backward_pass(): pl.pallas_call(backward_kernel, name='backward_pass', out_shape=(shape((r...  148 us
    pallas_call x1, Pallas kernels, attention_pass(): pl.pallas_call(attention_kernel, name='attention_pass', out_shape=(shape(...  125 us
  transfers between devices with their start and end apart: 2, of which 0 were waited for; matrix products, arithmetic and copies ran while one was open for 5% of the time, Pallas kernels for 54%

profile of v3, /device:TPU:0, one launch (start us, length us, event | category | flops | bytes accessed | tf_op | source)
XLA Modules:
  0.0 505.1 jit_solution(8402600149791501402)
XLA Ops:
  7.2 0.0 all-gather.2.cloned.1.call-start
  7.2 0.7 all-gather.2.cloned.1.call-update
  7.9 0.0 reduce-scatter.2.cloned.1.call-start
  8.0 0.7 pad_maximum_fusion.4
  8.7 0.1 copy.39
  8.8 0.7 fusion.5
  9.5 0.6 convert_element_type.39.hits_ref
  10.2 0.9 constant_dynamic-update-slice_fusion.6
  11.1 0.7 constant_dynamic-update-slice_fusion.5
  11.8 0.7 constant_dynamic-update-slice_fusion.4
  12.5 0.7 constant_dynamic-update-slice_fusion.3
  13.3 0.7 constant_dynamic-update-slice_fusion.2
  14.0 0.7 select_reduce_fusion
  14.7 0.7 fusion.4
  15.4 0.9 pad_maximum_fusion
  16.4 2.2 fusion.2.bias_ref
  18.6 125.2 %attention_pass.1 = (bf16[352,1536]{1,0:T(8,128)(2,1)}, bf16[352,1536]{1,0:T(8,128)(2,1)}, bf16[1408,512]{1,0:T(8,128)(2,1)}, bf16[352,1536]{1,0:T(8,128)(2,1)},...) custom-call(bf16[352,1536]{1,0:T(8,128)(2,1)} %bitcast.27, ...), custom_call_target="tpu_custom_call" | custom-call | flops 10000000000 | bytes 314572800 | tf_op jit(solution)/shard_map/attention_pass/pallas_call | solution.py:1296
  143.8 0.0 all-gather.2.cloned.1.call-done.dy_ref
  143.8 186.4 %expert_pass.1 = (f32[352,1536]{1,0:T(8,128)}, f32[8,384]{1,0:T(8,128)}, bf16[8,352,1536]{2,1,0:T(8,128)(2,1)}, bf16[2,384,768]{2,1,0:T(8,128)(2,1)}, bf16[768,3...) custom-call(bf16[352,1536]{1,0:T(8,128)(2,1)} %get-tuple-element.31.n2_ref, f32[8,384]{1,0:T(8,128)} %get-tuple-element.32.gate_ref, ...), custom_call_target="tpu_custom_call" | custom-call | flops 59793997824 | bytes 62914560 | tf_op jit(solution)/shard_map/expert_pass/pallas_call | solution.py:910
  330.2 0.0 reduce-scatter.2.cloned.1.call-update
  330.3 147.6 %backward_pass.1 = (f32[352,1536]{1,0:T(8,128)}, f32[48,3712]{1,0:T(8,128)}, bf16[2,1536,768]{2,1,0:T(8,128)(2,1)}, bf16[768,1536]{1,0:T(8,128)(2,1)}) custom-call(bf16[352,1536]{1,0:T(8,128)(2,1)} %bitcast.28, bf16[352,1536]{1,0:T(8,128)(2,1)} %bitcast.19, f32[8,384]{1,0:T(8,128)} %get-tuple-element.32.gate_ref, f32[8,384]{1,0:T(8,128)} %get-tuple-element.34.gg_ref, ...), custom_call_target="tpu_custom_call" | custom-call | flops 20000000000 | bytes 209715200 | tf_op jit(solution)/shard_map/backward_pass/pallas_call | solution.py:1781
  477.8 0.7 slice.61
  478.6 0.7 copy.40
  479.2 1.5 slice_reduce_fusion
  480.7 0.8 fusion.17
  481.5 0.6 pad_maximum_fusion.3
  482.2 0.6 pad_maximum_fusion.2
  482.8 1.9 fusion.16
  484.7 4.6 bitcast_convert_fusion
  489.3 4.5 slice_convert_fusion
  493.8 2.7 fusion.3
  496.5 1.3 copy.48
  (19 shorter events, 0.1 us)
Async XLA Ops:
  7.2 9.2 %copy-start.3 = (bf16[48,1536]{1,0:T(8,128)(2,1)S(1)}, bf16[48,1536]{1,0:T(8,128)(2,1)}, u32[]{:S(2)}) copy-start(bf16[48,1536]{1,0:T(8,128)(2,1)} %param.23) | copy-start | bytes 442372
  7.2 136.6 %all-gather.2.cloned.1.call-start = ((), (), s32[]{:S(2)}) async-start(), calls=%async_computation.1 | async-start | bytes 9732096 | tf_op jit(solution)/shard_map/all_gather | solution.py:1882
  7.9 485.9 %reduce-scatter.2.cloned.1.call-start = ((), (), s32[]{:S(2)}) async-start(), calls=%async_computation.2 | async-start | bytes 9732096 | tf_op jit(solution)/shard_map/reduce_scatter | solution.py:1898
  16.4 2.2 copy-start.4
  484.7 4.7 copy-start
  489.3 4.5 copy-start.1
  493.8 2.7 copy-start.2
Sparse Core Ops, SparseCore 0:
  9.7 106.6 all-gather.1
  330.4 91.1 reduce-scatter.1

commit v4 on v3

--- a/solution.py
+++ b/solution.py
@@ -1,5 +1,6 @@
 import jax
 import jax.numpy as jnp
+import numpy as np
 from jax import lax
 from jax.experimental import pallas as pl
 from jax.experimental.pallas import tpu as pltpu
@@ -437,7 +438,7 @@
     n2_ref, gate_ref, dy_ref, gw_ref, uw_ref, dw_ref,
     row_ref, gg_ref, sum_ref, wide_ref, down_ref, landing,
     n2_all, gate_all, dy_buf, dy_cols, hs_all, gl_all, ul_all, own, sib, zin, gg_out, gg_in,
-    stage, kept, down_kept,
+    gate_cols, gg_cols, stage, kept, down_kept,
     n2_send, n2_recv, gt_send, gt_recv, own_send, sib_recv, zin_send, zin_recv,
     gg_send, gg_recv, dy_sem, cols_sem, sum_sem, tile_send, tile_recv, load_sem, keep_sem,
 ):
@@ -457,6 +458,10 @@
     def at(zz):
         return {"expert": zz * 2 + core}
 
+    n2_load = pltpu.make_async_copy(
+        n2_ref, n2_all.at[pl.ds(pl.multiple_of(me * rows, 16), rows)], cols_sem
+    )
+    n2_load.start()
     barrier = pltpu.get_barrier_semaphore()
     for other in range(1, count):
         pl.semaphore_signal(
@@ -469,9 +474,15 @@
     def chunk(k):
         return pl.ds(pl.multiple_of(k * rows, 16), rows)
 
-    def n2_copy(k, lane, target):
+    def piece(k, h):
+        return pl.ds(pl.multiple_of(k * rows + h * half, 16), half)
+
+    def part(h):
+        return pl.ds(h * half, half)
+
+    def n2_copy(k, h, lane, target):
         return pltpu.make_async_remote_copy(
-            n2_all.at[chunk(k)], n2_all.at[chunk(k)], n2_send.at[k, lane], n2_recv.at[k],
+            n2_all.at[piece(k, h)], n2_all.at[piece(k, h)], n2_send.at[k, h, lane], n2_recv.at[k, h],
             device_id=target, device_id_type=MESH,
         )
 
@@ -481,20 +492,23 @@
             device_id=target, device_id_type=MESH,
         )
 
-    def send_chunk(k, lane, target):
-        n2_copy(k, lane, target).start()
-        gt_copy(k, lane, target).start()
-
-    def sent_chunk(k, lane, target):
-        n2_copy(k, lane, target).wait_send()
-        gt_copy(k, lane, target).wait_send()
-
-    def arrived(k):
-        n2_copy(k, 0, at(z)).wait_recv()
-        gt_copy(k, 0, at(z)).wait_recv()
-
-    def dy_copy(k, slot):
-        return pltpu.make_async_copy(dy_ref.at[k], dy_buf.at[slot], dy_sem.at[slot])
+    def send_chunk(k, h, lane, target):
+        n2_copy(k, h, lane, target).start()
+        if h == 0:
+            gt_copy(k, lane, target).start()
+
+    def sent_chunk(k, h, lane, target):
+        n2_copy(k, h, lane, target).wait_send()
+        if h == 0:
+            gt_copy(k, lane, target).wait_send()
+
+    def arrived(k, h):
+        n2_copy(k, h, 0, at(z)).wait_recv()
+        if h == 0:
+            gt_copy(k, 0, at(z)).wait_recv()
+
+    def dy_copy(k, h, w, s):
+        return pltpu.make_async_copy(dy_ref.at[k, part(h)], dy_buf.at[w, s], dy_sem.at[w, s])
 
     def gg_copy(k):
         return pltpu.make_async_remote_copy(
@@ -502,14 +516,12 @@
             device_id={"expert": k}, device_id_type=MESH,
         )
 
-    def own_copy(zs):
+    def own_copy(zs, h):
         return pltpu.make_async_remote_copy(
-            own.at[2 * zs + 1 - core], sib.at[zs], own_send.at[zs], sib_recv.at[zs],
+            own.at[2 * zs + 1 - core, part(h)], sib.at[zs, part(h)],
+            own_send.at[zs, h], sib_recv.at[zs, h],
             device_id={"expert": sibling}, device_id_type=MESH,
         )
-
-    def part(h):
-        return pl.ds(h * half, half)
 
     def zin_copy(zd, h, nxt, slot):
         return pltpu.make_async_remote_copy(
@@ -518,31 +530,37 @@
             device_id=at(nxt), device_id_type=MESH,
         )
 
-    n2_all[chunk(me), :] = n2_ref[...]
+    n2_load.wait()
     gate_all[me] = gate_ref[...]
 
-    @pl.when(z < depth - 1)
-    def _():
-        send_chunk(me, 0, at(z + 1))
-
-    @pl.when(z > 0)
-    def _():
-        send_chunk(me, 1, at(z - 1))
-
-    send_chunk(me, 2, {"expert": sibling})
+    for h in range(2):
+
+        @pl.when(z < depth - 1)
+        def _():
+            send_chunk(me, h, 0, at(z + 1))
+
+        @pl.when(z > 0)
+        def _():
+            send_chunk(me, h, 1, at(z - 1))
+
+        send_chunk(me, h, 2, {"expert": sibling})
 
     row_ids = lax.broadcasted_iota(jnp.int32, (count, gate_ref.shape[1]), 0)
 
-    def compute(k, slot):
-        r = chunk(k)
-        gate_row = jnp.sum(jnp.where(row_ids == me, gate_all[k], 0.0), axis=0, keepdims=True)
-        gate_col = jnp.transpose(jnp.broadcast_to(gate_row, (128, gate_row.shape[1])))[:rows]
+    def hidden_part(k, h, w, s):
+        r = piece(k, h)
+        place = 2 * s + w
+        if h == 0:
+            gate_row = jnp.sum(jnp.where(row_ids == me, gate_all[k], 0.0), axis=0, keepdims=True)
+            gate_cols[place] = jnp.transpose(jnp.broadcast_to(gate_row, (128, gate_row.shape[1])))
+            gg_cols[place, rows:, :] = jnp.zeros((gate_ref.shape[1] - rows, 128), F32)
+        gate_col = gate_cols[place, part(h), :]
         tile = 256
         gate_wide = jnp.concatenate([gate_col] * (tile // 128), axis=1)
-        total = jnp.zeros((rows, 128), F32)
+        total = jnp.zeros((half, 128), F32)
         for j in range(ff // tile):
             cols = slice(j * tile, (j + 1) * tile)
-            back = mm_nt(dy_buf[slot], dw_ref[cols, :])
+            back = mm_nt(dy_buf[w, s], dw_ref[cols, :])
             gate_pre = mm(n2_all[r, :], gw_ref[:, cols])
             up_pre = mm(n2_all[r, :], uw_ref[:, cols])
             act, slope = gelu_both(gate_pre)
@@ -554,25 +572,26 @@
             back = gate_wide * back
             gl_all[r, cols] = (back * up_pre * slope).astype(BF)
             ul_all[r, cols] = (back * act).astype(BF)
-        padded = jnp.concatenate(
-            [total, jnp.zeros((gate_ref.shape[1] - rows, 128), F32)], axis=0
-        )
-        gg_row = jnp.sum(jnp.transpose(padded), axis=0, keepdims=True)
-        gg_tile = jnp.where(row_ids == me, gg_row, 0.0)
-        gg_out[k] = gg_tile
-
-        @pl.when(k == me)
-        def _():
-            gg_in[me] = gg_tile
-
-        @pl.when(k != me)
-        def _():
-            gg_copy(k).start()
-
+        gg_cols[place, part(h), :] = total
+        if h == 1:
+            gg_row = jnp.sum(jnp.transpose(gg_cols[place]), axis=0, keepdims=True)
+            gg_tile = jnp.where(row_ids == me, gg_row, 0.0)
+            gg_out[k] = gg_tile
+
+            @pl.when(k == me)
+            def _():
+                gg_in[me] = gg_tile
+
+            @pl.when(k != me)
+            def _():
+                gg_copy(k).start()
+
+    def row_part(k, h):
+        r = piece(k, h)
         wide = 512
         for j in range(width // wide):
             cols = slice(j * wide, (j + 1) * wide)
-            own[k, :, cols] = (
+            own[k, part(h), cols] = (
                 mm_nt(gl_all[r, :], gw_ref[cols, :]) + mm_nt(ul_all[r, :], uw_ref[cols, :])
             ).astype(BF)
 
@@ -593,88 +612,179 @@
         return jnp.where((nxt == zd) & (nxt < z), depth, zd)
 
     def pass_on(zd, h, nxt, with_in):
-        if h == 0:
-            own_copy(zd).wait_recv()
+        own_copy(zd, h).wait_recv()
         if with_in:
             zin_copy(zd, h, nxt, zd).wait_recv()
         combine(zd, h, with_in)
         zin_copy(zd, h, nxt, slot_for(zd, nxt)).start()
 
-    def pair(zs):
-        def one(w, _):
-            k = 2 * zs + jnp.where(w == 0, 1 - core, core)
-
-            @pl.when(w == 0)
-            def _():
-                arrived(k)
-
-            dy_copy(k, w).wait()
-            compute(k, w)
-
-            @pl.when(w == 0)
-            def _():
-                own_copy(zs).start()
+    quarter = width // 4
+    cut = ff // 2
+    order = (others[1], others[0], others[2], mine)
+
+    def owner(j):
+        return jnp.where(
+            j == 0, order[0], jnp.where(j == 1, order[1], jnp.where(j == 2, order[2], mine))
+        )
+
+    def cols_of(dp):
+        return pl.ds(pl.multiple_of(dp * quarter, 128), quarter)
+
+    def tile_slot(kind, j):
+        if kind == 0:
+            return stage.at[j]
+        return (gl_all, ul_all)[kind - 1].at[pl.ds(pl.multiple_of(j * quarter, 16), quarter)]
+
+    sides = (slice(0, cut), slice(cut, ff))
+    ends = ({"dp": others[0]}, {"dp": others[2]})
+    hops = ((0, 0, 1, 0), (0, 1, 1, 1), (1, 0, 0, 0), (2, 1, 0, 1), (2, 0, 2, 1), (1, 1, 2, 0))
+
+    def hop(kind, n):
+        j, side, slot, way = hops[n]
+        return pltpu.make_async_remote_copy(
+            tile_slot(kind, j).at[:, sides[side]], landing.at[kind, slot, :, sides[side]],
+            tile_send.at[kind, n], tile_recv.at[kind, slot, side],
+            device_id=ends[way], device_id_type=MESH,
+        )
+
+    def col_copy(j):
+        return pltpu.make_async_copy(dy_ref.at[:, :, cols_of(owner(j))], dy_cols, cols_sem)
+
+    def tiles(kind, low, high):
+        def step(j, _):
+            cols = cols_of(owner(j))
+            if kind == 2:
+                col_copy(j).wait()
+                tile = mm_tn(dy_cols[...].reshape(count * rows, quarter), hs_all[...])
+
+                @pl.when(j < 3)
+                def _():
+                    col_copy(j + 1).start()
+            else:
+                tile = mm_tn(n2_all[:, cols], (gl_all, ul_all)[kind][...])
+            tile = tile.astype(BF)
+
+            @pl.when(j < 3)
+            def _():
+                tile_slot(kind, j)[...] = tile
+
+            for n in range(4):
+
+                @pl.when(j == hops[n][0])
+                def _():
+                    hop(kind, n).start()
+
+            @pl.when(j == 3)
+            def _():
+                kept[kind] = tile
 
             return 0
 
-        lax.fori_loop(0, 2, one, 0)
-
-    def start_dy(zs):
-        dy_copy(2 * zs + 1 - core, 0).start()
-        dy_copy(2 * zs + core, 1).start()
+        lax.fori_loop(low, high, step, 0)
+
+    def spare(kind, i):
+        return (gl_all, ul_all, gl_all)[kind].at[pl.ds(6 * quarter, quarter)]
+
+    def second_leg(kind):
+        for side in range(2):
+            n = side
+            hop(kind, n).wait_recv()
+        load = pltpu.make_async_copy(landing.at[kind, 1], spare(kind, 6), load_sem.at[kind, 2])
+        load.start()
+        load.wait()
+        for n in (4, 5):
+            j, side, _, _ = hops[n]
+
+            def step(i, _):
+                rr = pl.ds(pl.multiple_of(i * 32, 32), 32)
+                into = tile_slot(kind, j)
+                value = into[rr, sides[side]].astype(F32) + spare(kind, 6)[rr, sides[side]].astype(F32)
+                into[rr, sides[side]] = value.astype(BF)
+                return 0
+
+            lax.fori_loop(0, quarter // 32, step, 0)
+            hop(kind, n).start()
 
     def by_distance(d, _):
         left, right = z - d, z + d
         has_left, has_right = left >= 0, (right < depth) & (d > 0)
 
-        @pl.when(has_left)
-        def _():
-            start_dy(left)
-
-        @pl.when(has_left & (d > 0))
-        def _():
-            k = 2 * left + core
-            arrived(k)
-
-            @pl.when(z < depth - 1)
-            def _():
-                send_chunk(k, 0, at(z + 1))
-
-            send_chunk(k, 2, {"expert": sibling})
-
-        @pl.when(has_right)
-        def _():
-            k = 2 * right + core
-            arrived(k)
-
-            @pl.when(z > 0)
-            def _():
-                send_chunk(k, 1, at(z - 1))
-
-            send_chunk(k, 2, {"expert": sibling})
-
-        def side(s, _):
-            zs = jnp.where(s == 0, left, right)
-
-            @pl.when(jnp.where(s == 0, has_left, has_right))
-            def _():
-                @pl.when(s == 1)
+        def other_chunk(zs):
+            return 2 * zs + 1 - core
+
+        for h in range(2):
+            for s, zs, there in ((0, left, has_left), (1, right, has_right)):
+
+                @pl.when(there)
                 def _():
-                    start_dy(right)
-
-                pair(zs)
-
-                @pl.when((d > 0) & ((z == 0) | (z == depth - 1)))
+                    dy_copy(other_chunk(zs), h, 0, s).start()
+                    dy_copy(2 * zs + core, h, 1, s).start()
+
+            @pl.when(has_left & (d > 0))
+            def _():
+                k = 2 * left + core
+                arrived(k, h)
+
+                @pl.when(z < depth - 1)
                 def _():
-                    nxt = jnp.where(z == 0, 1, depth - 2)
-                    for h in range(2):
-                        pass_on(zs, h, nxt, False)
-
-            return 0
-
-        lax.fori_loop(0, 2, side, 0)
+                    send_chunk(k, h, 0, at(z + 1))
+
+                send_chunk(k, h, 2, {"expert": sibling})
+
+            @pl.when(has_right)
+            def _():
+                k = 2 * right + core
+                arrived(k, h)
+
+                @pl.when(z > 0)
+                def _():
+                    send_chunk(k, h, 1, at(z - 1))
+
+                send_chunk(k, h, 2, {"expert": sibling})
+
+            def side(s, _):
+                zs = jnp.where(s == 0, left, right)
+
+                @pl.when(jnp.where(s == 0, has_left, has_right))
+                def _():
+                    def first(w, _):
+                        k = 2 * zs + jnp.where(w == 0, 1 - core, core)
+
+                        @pl.when(w == 0)
+                        def _():
+                            arrived(k, h)
+
+                        dy_copy(k, h, w, s).wait()
+                        hidden_part(k, h, w, s)
+                        return 0
+
+                    lax.fori_loop(0, 2, first, 0)
+                    if h == 1:
+                        @pl.when(d == jnp.maximum(z, depth - 1 - z))
+                        def _():
+                            tiles(0, 0, 3)
+
+                    def second(w, _):
+                        row_part(2 * zs + jnp.where(w == 0, 1 - core, core), h)
+
+                        @pl.when(w == 0)
+                        def _():
+                            own_copy(zs, h).start()
+
+                        return 0
+
+                    lax.fori_loop(0, 2, second, 0)
+
+                    @pl.when((d > 0) & ((z == 0) | (z == depth - 1)))
+                    def _():
+                        pass_on(zs, h, jnp.where(z == 0, 1, depth - 2), False)
+
+                return 0
+
+            lax.fori_loop(0, 2, side, 0)
         return 0
 
+    col_copy(0).start()
     lax.fori_loop(0, depth, by_distance, 0)
 
     def sum_copy(k, slot):
@@ -686,7 +796,8 @@
 
             @pl.when(i < depth)
             def _():
-                own_copy(i).wait_send()
+                for h in range(2):
+                    own_copy(i, h).wait_send()
 
             @pl.when(i >= depth)
             def _():
@@ -701,57 +812,6 @@
 
         lax.fori_loop(low, high, step, 0)
 
-    quarter = width // 4
-
-    def owner(j):
-        return jnp.where(
-            j == 0, others[0], jnp.where(j == 1, others[1], jnp.where(j == 2, others[2], mine))
-        )
-
-    def cols_of(dp):
-        return pl.ds(pl.multiple_of(dp * quarter, 128), quarter)
-
-    def tile_slot(kind, j):
-        if kind == 0:
-            return stage.at[j]
-        return (gl_all, ul_all)[kind - 1].at[pl.ds(pl.multiple_of(j * quarter, 16), quarter)]
-
-    def tile_copy(kind, j):
-        return pltpu.make_async_remote_copy(
-            tile_slot(kind, j), landing.at[mine, kind], tile_send.at[kind, j],
-            tile_recv.at[mine, kind], device_id={"dp": owner(j)}, device_id_type=MESH,
-        )
-
-    def col_copy(j):
-        return pltpu.make_async_copy(dy_ref.at[:, :, cols_of(owner(j))], dy_cols, cols_sem)
-
-    def tiles(kind, low, high):
-        def step(j, _):
-            cols = cols_of(owner(j))
-            if kind == 2:
-                col_copy(j).wait()
-                tile = mm_tn(dy_cols[...].reshape(count * rows, quarter), hs_all[...])
-
-                @pl.when(j < 3)
-                def _():
-                    col_copy(j + 1).start()
-            else:
-                tile = mm_tn(n2_all[:, cols], (gl_all, ul_all)[kind][...])
-            tile = tile.astype(BF)
-
-            @pl.when(j < 3)
-            def _():
-                tile_slot(kind, j)[...] = tile
-                tile_copy(kind, j).start()
-
-            @pl.when(j == 3)
-            def _():
-                kept[kind] = tile
-
-            return 0
-
-        lax.fori_loop(low, high, step, 0)
-
     def flow(r, first, h):
         right = (z < depth - 1 - z) if first else (z >= depth - 1 - z)
         zd = jnp.where(right, r, depth - 1 - r)
@@ -761,23 +821,31 @@
         def _():
             pass_on(zd, h, jnp.where(right, z + 1, z - 1), True)
 
-    col_copy(0).start()
-    jobs = [lambda k=kind, i=i: tiles(k, i, i + 2) for kind in range(3) for i in (0, 2)]
     eighth = count // 4
-    jobs += [lambda i=i: sums(i * eighth, (i + 1) * eighth) for i in range(4)]
+    jobs = [
+        lambda: tiles(0, 3, 4),
+        lambda: tiles(1, 0, 2),
+        lambda: tiles(1, 2, 4),
+        lambda: second_leg(0),
+        lambda: tiles(2, 0, 2),
+        lambda: tiles(2, 2, 4),
+        lambda: second_leg(1),
+        *[lambda i=i: sums(i * eighth, (i + 1) * eighth) for i in range(4)],
+        lambda: second_leg(2),
+    ]
     for r in range(2, depth):
         for first in (True, False):
             for h in range(2):
                 if first or r == depth - 1:
-                    for _ in range(2 if r == 2 else 1):
+                    for _ in range(2):
                         if jobs:
                             jobs.pop(0)()
                 flow(r, first, h)
     while jobs:
         jobs.pop(0)()
 
-    own_copy(z).wait_recv()
     for h in range(2):
+        own_copy(z, h).wait_recv()
 
         @pl.when(z > 0)
         def _():
@@ -817,7 +885,7 @@
     def tile_load(kind, i):
         into = (gl_all, ul_all, hs_all)[kind]
         return pltpu.make_async_copy(
-            landing.at[others[i], kind], into.at[pl.ds((3 + i) * quarter, quarter)], load_sem.at[kind, i]
+            landing.at[kind, 2 * i], into.at[pl.ds((3 + i) * quarter, quarter)], load_sem.at[kind, i]
         )
 
     keeps = [
@@ -825,21 +893,19 @@
         pltpu.make_async_copy(down_kept, down_ref, keep_sem.at[1]),
     ]
     for kind in range(3):
-        for i in range(3):
-            pltpu.make_async_remote_copy(
-                stage.at[0], landing.at[others[i], kind], tile_send.at[kind, i],
-                tile_recv.at[others[i], kind], device_id={"dp": others[i]}, device_id_type=MESH,
-            ).wait_recv()
+        for n in (2, 3, 4, 5):
+            hop(kind, n).wait_recv()
+        for i in range(2):
             tile_load(kind, i).start()
     for kind in range(3):
-        for i in range(3):
+        for i in range(2):
             tile_load(kind, i).wait()
         into = (gl_all, ul_all, hs_all)[kind]
 
         def add_up(i, _):
             rr = pl.ds(pl.multiple_of(i * 128, 128), 128)
             total = kept[kind, rr, :].astype(F32)
-            for j in range(3):
+            for j in range(2):
                 total = total + into[pl.ds(pl.multiple_of((3 + j) * quarter + i * 128, 128), 128), :].astype(F32)
             if kind == 2:
                 down_kept[:, rr] = jnp.transpose(total).astype(BF)
@@ -859,21 +925,19 @@
 
         zs = e // 2
 
-        @pl.when((e == me) | ((zs < z) & (e % 2 == core)))
-        def _():
-            @pl.when(z < depth - 1)
-            def _():
-                sent_chunk(e, 0, at(z + 1))
-
-        @pl.when((e == me) | ((zs > z) & (e % 2 == core)))
-        def _():
-            @pl.when(z > 0)
-            def _():
-                sent_chunk(e, 1, at(z - 1))
-
-        @pl.when(e % 2 == core)
-        def _():
-            sent_chunk(e, 2, {"expert": sibling})
+        for h in range(2):
+
+            @pl.when(((e == me) | ((zs < z) & (e % 2 == core))) & (z < depth - 1))
+            def _():
+                sent_chunk(e, h, 0, at(z + 1))
+
+            @pl.when(((e == me) | ((zs > z) & (e % 2 == core))) & (z > 0))
+            def _():
+                sent_chunk(e, h, 1, at(z - 1))
+
+            @pl.when(e % 2 == core)
+            def _():
+                sent_chunk(e, h, 2, {"expert": sibling})
 
     for zd in range(depth):
         sum_copy(zd, 2 * zd + 1 - core).wait()
@@ -884,8 +948,8 @@
                 zin_copy(zd, h, z, zd).wait_send()
 
     for kind in range(3):
-        for j in range(3):
-            tile_copy(kind, j).wait_send()
+        for n in range(len(hops)):
+            hop(kind, n).wait_send()
     for keep in keeps:
         keep.wait()
 
@@ -905,18 +969,18 @@
         jax.ShapeDtypeStruct((count, rows, width), BF),
         jax.ShapeDtypeStruct((2, width // 4, ff), BF),
         jax.ShapeDtypeStruct((ff, width // 4), BF),
-        jax.ShapeDtypeStruct((4, 3, width // 4, ff), BF),
+        jax.ShapeDtypeStruct((3, 3, width // 4, ff), BF),
     )
     return pl.pallas_call(
         expert_kernel,
         name="expert_pass",
         out_shape=outs,
-        in_specs=[vmem, vmem, anywhere, vmem, vmem, vmem],
+        in_specs=[anywhere, vmem, anywhere, vmem, vmem, vmem],
         out_specs=(vmem, vmem, anywhere, anywhere, anywhere, anywhere),
         scratch_shapes=[
             pltpu.VMEM((count * rows, width), BF),
             pltpu.VMEM((count, count, lanes), F32),
-            pltpu.VMEM((2, rows, width), BF),
+            pltpu.VMEM((2, 2, rows // 2, width), BF),
             pltpu.VMEM((count, rows, width // 4), BF),
             pltpu.VMEM((count * rows, ff), BF),
             pltpu.VMEM((count * rows, ff), BF),
@@ -926,12 +990,14 @@
             pltpu.VMEM((depth + 1, rows, width), BF),
             pltpu.VMEM((count, count, lanes), F32),
             pltpu.VMEM((count, count, lanes), F32),
+            pltpu.VMEM((4, lanes, 128), F32),
+            pltpu.VMEM((4, lanes, 128), F32),
             pltpu.VMEM((3, width // 4, ff), BF),
             pltpu.VMEM((3, width // 4, ff), BF),
             pltpu.VMEM((ff, width // 4), BF),
-            dma((count, 3)), dma((count,)), dma((count, 3)), dma((count,)),
-            dma((depth,)), dma((depth,)), dma((depth, 2)), dma((depth + 1, 2)),
-            dma((count,)), dma((count,)), dma((2,)), dma, dma((count,)), dma((3, 3)), dma((4, 3)),
+            dma((count, 2, 3)), dma((count, 2)), dma((count, 3)), dma((count,)),
+            dma((depth, 2)), dma((depth, 2)), dma((depth, 2)), dma((depth + 1, 2)),
+            dma((count,)), dma((count,)), dma((2, 2)), dma, dma((count,)), dma((3, 6)), dma((3, 3, 2)),
             dma((3, 3)), dma((2,)),
         ],
         compiler_params=pltpu.CompilerParams(
@@ -961,15 +1027,16 @@
 
 
 def attention_kernel(
-    x_ref, shard_ref, cos_ref, sin_ref, bias_ref, hits_ref,
-    n1_ref, q_ref, kv_ref, mixed_ref, lse_ref, middle_ref, n2_ref, gate_ref, w_out,
-    w, n1, q, kv, mixed,
+    x_ref, wq_ref, wk_ref, wv_ref, ws_ref, wo_ref, freq_ref, parent_ref, hits_ref, dy_ref,
+    n1_ref, q_ref, kv_ref, mixed_ref, lse_ref, middle_ref, n2_ref, gate_ref, cos_ref, sin_ref,
+    bias_ref, w_out, dy_all,
+    w, n1, q, kv, mixed, bias,
     z_send, z_recv, x_send, x_recv, y_send, y_recv, a_send, a_recv, b_send, b_recv, s_send, s_recv,
-    kx_send, kx_recv, ky_send, ky_recv, ka_send, ka_recv, kb_send, kb_recv, out_sem, keep_sem,
+    kx_send, kx_recv, ky_send, ky_recv, ka_send, ka_recv, kb_send, kb_recv, dy_send, dy_recv, out_sem, keep_sem, dy_sem,
 ):
     count = lax.axis_size("expert")
     depth = count // 2
-    shard, total = shard_ref.shape
+    shard, total = wq_ref.shape[0], w.shape[1]
     rows, width = x_ref.shape
     heads = q.shape[1] // HEAD_SIZE
     kv_width = kv.shape[1]
@@ -994,8 +1061,8 @@
             src, dst, send, recv, device_id=target, device_id_type=MESH
         )
 
-    bounds = ((0, split), (split, total))
-    cuts = (bounds[0][1] // 256 * 128, split + (total - split) // 256 * 128)
+    bounds = ((wide, split), (0, wide), (split, total))
+    cuts = tuple(low + ((high - low) // 128 + 1) // 2 * 128 for low, high in bounds)
 
     def place(dp, zz, cc):
         return pl.ds(pl.multiple_of((dp * count + 2 * zz + cc) * shard, 16), shard)
@@ -1049,7 +1116,6 @@
             def _():
                 z_copy(p, z, 1, at(z - 1)).start()
 
-            spread(p, z)
             return
 
         def action(zz, from_left):
@@ -1065,9 +1131,10 @@
                 def _():
                     z_copy(p, zz, 1, at(z - 1)).start()
 
-            spread(p, zz)
-
         on_sides(d, action)
+
+    def spread_step(p, d):
+        on_sides(d, lambda zz, _: spread(p, zz))
 
     def xy_step(p, d):
         def action(zz, _):
@@ -1111,18 +1178,125 @@
             for dp in range(4):
                 s_copy(p, dp, zz).wait_send()
 
-    w[place(mine, z, core), :] = shard_ref[...]
+    def dy_copy(k, lane, target):
+        return remote(dy_all.at[k], dy_all.at[k], dy_send.at[k, lane], dy_recv.at[k], target)
+
+    def dy_own(lane, target):
+        return remote(dy_ref, dy_all.at[me], dy_send.at[me, lane], dy_recv.at[me], target)
+
+    dy_keep = pltpu.make_async_copy(dy_ref, dy_all.at[me], dy_sem)
+
+    def dy_step(d):
+        if d == 0:
+            dy_own(2, sibling).start()
+            dy_keep.start()
+
+            @pl.when(z < depth - 1)
+            def _():
+                dy_own(0, at(z + 1)).start()
+
+            @pl.when(z > 0)
+            def _():
+                dy_own(1, at(z - 1)).start()
+
+            return
+
+        def action(zz, from_left):
+            k = 2 * zz + core
+            dy_copy(k, 0, sibling).wait_recv()
+            if from_left:
+
+                @pl.when(z < depth - 1)
+                def _():
+                    dy_copy(k, 0, at(z + 1)).start()
+            else:
+
+                @pl.when(z > 0)
+                def _():
+                    dy_copy(k, 1, at(z - 1)).start()
+
+            dy_copy(k, 2, sibling).start()
+
+        on_sides(d, action)
+
+    def dy_end():
+        dy_keep.wait()
+        for zz in range(depth):
+            dy_copy(2 * zz + 1 - core, 2, sibling).wait_recv()
+            k = 2 * zz + core
+            dy_copy(k, 2, sibling).wait_send()
+
+            @pl.when((zz <= z) & (z < depth - 1))
+            def _():
+                dy_copy(k, 0, sibling).wait_send()
+
+            @pl.when((zz >= z) & (z > 0))
+            def _():
+                dy_copy(k, 1, sibling).wait_send()
+
+    home = place(mine, z, core)
+    w[home, 0:wide] = wq_ref[...]
+    for g in range(groups):
+        low, head = wide + 2 * g * HEAD_SIZE, slice(g * HEAD_SIZE, (g + 1) * HEAD_SIZE)
+        w[home, low : low + HEAD_SIZE] = wk_ref[:, head]
+        w[home, low + HEAD_SIZE : low + 2 * HEAD_SIZE] = wv_ref[:, head]
+    w[home, qkv_width:split] = ws_ref[...]
+    w[home, split:total] = wo_ref[...]
     z_step(0, 0)
+    spread_step(0, 0)
+
+    blocks = parent_ref.shape[1]
+    trunk = blocks - BRANCHES - LEAVES
+    ids = mine * rows + lax.broadcasted_iota(jnp.int32, (rows, 1), 0)
+    query_block = lax.div(ids, SEG)
+    level = jnp.minimum(query_block, trunk) + (query_block >= trunk + BRANCHES).astype(jnp.int32)
+    positions = (level * SEG + lax.rem(ids, SEG)).astype(F32)
+    angles = positions * freq_ref[...]
+    cos_ref[...] = jnp.cos(angles)
+    turned = lax.broadcasted_iota(jnp.int32, angles.shape, 1) < HEAD_SIZE // 2
+    sine = jnp.sin(angles)
+    sin_ref[...] = jnp.where(turned, -sine, sine)
     z_step(0, 1)
+    spread_step(0, 1)
     xy_step(0, 0)
-    for d in range(2, depth):
-        z_step(0, d)
-        xy_step(0, d - 1)
-    xy_step(0, depth - 1)
+    block_ids = lax.broadcasted_iota(jnp.int32, (rows, blocks), 1)
+    parent = jnp.sum(jnp.where(block_ids == query_block, parent_ref[...], 0), axis=1, keepdims=True)
+    above = jnp.where(query_block >= trunk + BRANCHES, parent, query_block)
+    keys = bias.shape[1] // 128
+
+    def visible(i, _):
+        cols = pl.ds(pl.multiple_of(i * 128, 128), 128)
+        key_ids = i * 128 + lax.broadcasted_iota(jnp.int32, (rows, 128), 1)
+        key_block = lax.div(key_ids, SEG)
+        related = (key_block < trunk) | (key_block == query_block) | (key_block == above)
+        bias[:, cols] = jnp.where(related & (key_ids <= ids), 0.0, NEGATIVE)
+        return 0
+
+    z_step(0, 2)
+    spread_step(0, 2)
+    z_step(1, 0)
+    xy_step(0, 1)
+    lax.fori_loop(0, keys, visible, 0)
+    z_step(0, 3)
+    spread_step(0, 3)
+    z_step(2, 0)
+    spread_step(1, 0)
+    z_step(1, 1)
+    spread_step(1, 1)
+    xy_step(0, 2)
+    z_step(2, 1)
+    xy_step(0, 3)
+    z_step(1, 2)
+    spread_step(1, 2)
     for d in range(depth):
         diag_step(0, d)
+    z_step(2, 2)
+    xy_step(1, 0)
+    z_step(1, 3)
+    spread_step(1, 3)
+    z_step(2, 3)
+    dy_step(0)
     all_here(0)
-    z_step(1, 0)
 
     def keep(p):
         low, high = bounds[p]
@@ -1190,6 +1364,18 @@
     for g in range(groups):
         kx(g, mine).start()
         ky(g, mine).start()
+    xy_step(1, 1)
+    xy_step(1, 2)
+    kv_on(0)
+    xy_step(1, 3)
+    kv_on(1)
+    for d in range(depth):
+        diag_step(1, d)
+        spread_step(2, d)
+    kv_here(0)
+    all_here(1)
+    keep(1).start()
+    dy_step(1)
 
     def project(h, _):
         cols = pl.ds(pl.multiple_of(h * 2 * HEAD_SIZE, 2 * HEAD_SIZE), 2 * HEAD_SIZE)
@@ -1200,17 +1386,14 @@
         return 0
 
     lax.fori_loop(0, heads // 2, project, 0)
-    kv_on(0)
-    z_step(1, 1)
-    kv_here(0)
     later = [
-        lambda: (kv_on(1), xy_step(1, 0), z_step(1, 2)),
-        lambda: (xy_step(1, 1), z_step(1, 3)),
-        lambda: xy_step(1, 2),
-        lambda: xy_step(1, 3),
-        lambda: (diag_step(1, 0), diag_step(1, 1)),
-        lambda: (diag_step(1, 2), diag_step(1, 3)),
+        lambda: xy_step(2, 0),
+        lambda: xy_step(2, 1),
+        lambda: xy_step(2, 2),
+        lambda: xy_step(2, 3),
         lambda: kv_here(1),
+        lambda: (diag_step(2, 0), diag_step(2, 1)),
+        lambda: (diag_step(2, 2), diag_step(2, 3)),
     ]
     lse_ref[...] = jnp.zeros_like(lse_ref)
     lanes = lax.broadcasted_iota(jnp.int32, lse_ref.shape, 1)
@@ -1222,7 +1405,7 @@
         cols = pl.ds(pl.multiple_of(h * HEAD_SIZE, HEAD_SIZE), HEAD_SIZE)
         k_cols = pl.ds(pl.multiple_of(g * 2 * HEAD_SIZE, HEAD_SIZE), HEAD_SIZE)
         v_cols = pl.ds(pl.multiple_of(g * 2 * HEAD_SIZE + HEAD_SIZE, HEAD_SIZE), HEAD_SIZE)
-        scores = mm_nt(q[:, cols], kv[:, k_cols]) * (HEAD_SIZE**-0.5 * LOG2E) + bias_ref[...]
+        scores = mm_nt(q[:, cols], kv[:, k_cols]) * (HEAD_SIZE**-0.5 * LOG2E) + bias[...]
         top = jnp.max(scores, axis=1, keepdims=True)
         power = jnp.exp2(scores - top)
         sums = jnp.sum(power, axis=1, keepdims=True)
@@ -1234,13 +1417,14 @@
     keeps = [
         pltpu.make_async_copy(src, dst, out_sem.at[i])
         for i, (src, dst) in enumerate(
-            ((n1, n1_ref), (q, q_ref), (kv, kv_ref), (mixed, mixed_ref))
+            ((n1, n1_ref), (q, q_ref), (kv, kv_ref), (mixed, mixed_ref), (bias, bias_ref))
         )
     ]
     for copy in keeps:
         copy.start()
-    all_here(1)
-    keep(1).start()
+    all_here(2)
+    keep(2).start()
+    dy_step(2)
     tile = 512
 
     def project_out(i, _):
@@ -1266,33 +1450,38 @@
     gate_ref[...] = jnp.zeros_like(gate_ref)
     gate_ref[:, :rows] = power / jnp.sum(power, axis=0, keepdims=True)
 
+    dy_step(3)
+    dy_end()
     for g in range(groups):
         kx(g, mine).wait_send()
         ky(g, mine).wait_send()
         ka(g, xn).wait_send()
         kb(g, yn).wait_send()
-    for p in range(2):
+    for p in range(3):
         all_sent(p)
         keep(p).wait()
     for copy in keeps:
         copy.wait()
 
 
-def attention_pass(x, shard, cos, sin, bias, hits, kv_width):
+def attention_pass(x, shards, freq, parent, hits, dy):
     count = lax.axis_size("expert")
     depth = count // 2
     rows, width = x.shape
     lanes = rows + -rows % 128
+    shard = shards[0].shape[0]
     devices = 4 * count
-    wide = width
+    wide = shards[0].shape[1]
+    kv_width = 2 * shards[1].shape[1]
     dma = pltpu.SemaphoreType.DMA
     vmem = pl.BlockSpec(memory_space=pltpu.VMEM)
     anywhere = pl.BlockSpec(memory_space=pl.ANY)
     shape = jax.ShapeDtypeStruct
-    pair = dma((2, depth))
+    parts = 3
+    pair = dma((parts, depth))
     groups = kv_width // (2 * HEAD_SIZE)
     tree = 4 * rows
-    total = shard.shape[1]
+    total = kv_width + sum(part.shape[1] for part in (shards[0], *shards[3:]))
     return pl.pallas_call(
         attention_kernel,
         name="attention_pass",
@@ -1305,20 +1494,25 @@
             shape((rows, width), F32),
             shape((rows, width), BF),
             shape((hits.shape[0], lanes), F32),
-            shape((devices * shard.shape[0], total), BF),
+            shape((rows, HEAD_SIZE), F32),
+            shape((rows, HEAD_SIZE), F32),
+            shape((rows, tree), F32),
+            shape((devices * shard, total), BF),
+            shape((count, rows, width), BF),
         ),
-        in_specs=[vmem] * 6,
-        out_specs=(anywhere,) * 4 + (vmem,) * 4 + (anywhere,),
+        in_specs=[vmem] * 9 + [anywhere],
+        out_specs=(anywhere,) * 4 + (vmem,) * 6 + (anywhere,) * 3,
         scratch_shapes=[
-            pltpu.VMEM((devices * shard.shape[0], total), BF),
+            pltpu.VMEM((devices * shard, total), BF),
             pltpu.VMEM((rows, width), BF),
             pltpu.VMEM((rows, wide), BF),
             pltpu.VMEM((tree, kv_width), BF),
             pltpu.VMEM((rows, wide), BF),
-            dma((2, depth, 2)), pair, pair, pair, pair, pair, pair, pair, pair, pair,
-            dma((2, 4, depth)), dma((2, 4, depth)),
+            pltpu.VMEM((rows, tree), F32),
+            dma((parts, depth, 2)), pair, pair, pair, pair, pair, pair, pair, pair, pair,
+            dma((parts, 4, depth)), dma((parts, 4, depth)),
             *[dma((groups,)) for _ in range(8)],
-            dma((4,)), dma((2,)),
+            dma((count, 3)), dma((count,)), dma((5,)), dma((parts,)), dma,
         ],
         compiler_params=pltpu.CompilerParams(
             collective_id=1, has_side_effects=True, vmem_limit_bytes=56 * 2**20
@@ -1326,7 +1520,7 @@
         cost_estimate=pl.CostEstimate(
             flops=10**10, bytes_accessed=300 * 2**20, transcendentals=0
         ),
-    )(x, shard, cos, sin, bias, hits)
+    )(x, *shards, freq, parent, hits, dy)
 
 
 def backward_kernel(
@@ -1404,19 +1598,20 @@
         ref = quarter_of(piece, dp)
         return remote(ref, ref, ag_fs.at[piece], ag_fr.at[piece], target)
 
-    for piece in range(4):
+    def quarters(piece):
         quarter_x(piece, mine).start()
         quarter_y(piece, mine).start()
         keep_quarter(piece).start()
 
-    def quarters_on(first):
-        for piece in (0, 1) if first else (2, 3):
-            if piece % 2 == 0:
-                quarter_x(piece, xn).wait_recv()
-                quarter_on(piece, xn, {"dp": yn}).start()
-            else:
-                quarter_y(piece, yn).wait_recv()
-                quarter_on(piece, yn, {"dp": xn}).start()
+    def quarters_on(piece):
+        if piece % 2 == 0:
+            quarter_x(piece, xn).wait_recv()
+            quarter_on(piece, xn, {"dp": yn}).start()
+        else:
+            quarter_y(piece, yn).wait_recv()
+            quarter_on(piece, yn, {"dp": xn}).start()
+
+    quarters(0)
 
     bounds = ((split, total), (0, wide // 2), (wide // 2, wide), (wide, split))
     cuts = tuple(low + ((high - low) // 128 + 1) // 2 * 128 for low, high in bounds)
@@ -1615,6 +1810,7 @@
     lax.fori_loop(0, wide // tile, mixed_step, 0)
     load_qkv.start()
     first_legs(0)
+    quarters(1)
 
     lanes = lax.broadcasted_iota(jnp.int32, lse_ref.shape, 1)
 
@@ -1668,9 +1864,10 @@
         weight_rows(n1_ref, qg[:, g * wide // 2 : (g + 1) * wide // 2], g * wide // 2, wide // 2)
         begin(1 + g)
         first_legs(1 + g)
-
-    attend_group(0, {})
-    attend_group(1, {2: lambda: second_legs(0)})
+        quarters(2 + g)
+
+    attend_group(0, {3: lambda: quarters_on(0)})
+    attend_group(1, {1: lambda: second_legs(0), 4: lambda: quarters_on(1)})
 
     def kv_sum(g):
         for i in range(3):
@@ -1687,6 +1884,7 @@
 
     for g in range(groups):
         kv_sum(g)
+    second_legs(1)
     weight_rows(n1_ref, qg[:, wide:], wide, kv_width)
     load_qkv.wait()
 
@@ -1696,6 +1894,7 @@
         return 0
 
     lax.fori_loop(0, width // tile, first_grad, 0)
+    quarters_on(2)
 
     def first_norm(i, carry):
         rr = pl.ds(pl.multiple_of(i * block, block), block)
@@ -1718,12 +1917,10 @@
         part = small_grad[i * width // 4 : (i + 1) * width // 4]
         w[i, :, :, :, qkv_width:split] = part.reshape(depth, 2, shard, 128)
     begin(3)
-    quarters_on(True)
     first_legs(3)
-    second_legs(1)
-    quarters_on(False)
     line(0)
     second_legs(2)
+    quarters_on(3)
     line_on(0)
     line(1)
     second_legs(3)
@@ -1822,32 +2019,6 @@
     )
 
 
-def rotation_rows(positions):
-    half = HEAD_SIZE // 2
-    frequency = jnp.power(THETA, -(jnp.arange(half, dtype=jnp.float32) * 2.0 / HEAD_SIZE))
-    angles = positions.astype(jnp.float32)[:, None] * frequency[None, :]
-    cosine, sine = jnp.cos(angles), jnp.sin(angles)
-    return jnp.concatenate([cosine, cosine], axis=1), jnp.concatenate([-sine, sine], axis=1)
-
-
-def tree_visibility(parent_row, query_ids, tree_length):
-    blocks = parent_row.shape[0]
-    trunk = blocks - BRANCHES - LEAVES
-    leaf_from = trunk + BRANCHES
-    query_block = query_ids // SEG
-    block_ids = jnp.arange(blocks, dtype=jnp.int32)
-    depth_of = jnp.minimum(query_block, trunk) + (query_block >= leaf_from).astype(jnp.int32)
-    positions = depth_of * SEG + query_ids % SEG
-    parent = jnp.sum(jnp.where(query_block[:, None] == block_ids, parent_row, 0), axis=1)
-    above = jnp.where(query_block >= leaf_from, parent, query_block)
-    key_ids = jnp.arange(tree_length, dtype=jnp.int32)[None, :]
-    key_block = key_ids // SEG
-    related = (
-        (key_block < trunk) | (key_block == query_block[:, None]) | (key_block == above[:, None])
-    )
-    return related & (key_ids <= query_ids[:, None]), positions
-
-
 def dense_on_device(
     tokens,
     cotangent,
@@ -1868,29 +2039,22 @@
     heads_width = QUERY_HEADS * HEAD_SIZE
     kv_width = 2 * KEY_VALUE_HEADS * HEAD_SIZE
     qkv_width = heads_width + kv_width
-    kv_shards = []
-    for head in range(KEY_VALUE_HEADS):
-        cols = slice(head * HEAD_SIZE, (head + 1) * HEAD_SIZE)
-        kv_shards += [key_matrix[:, cols], value_matrix[:, cols]]
     small_shard = jnp.concatenate(
         [router_weight, first_gain[:, None], second_gain[:, None]], axis=1
     )
     small_shard = jnp.pad(small_shard, ((0, 0), (0, -small_shard.shape[1] % 128)))
     small_width = small_shard.shape[1]
-    shard = jnp.concatenate([query_weight, *kv_shards, small_shard, out_weight], axis=1)
+    shards = (query_weight, key_matrix, value_matrix, small_shard, out_weight)
     dy_low = cotangent[0]
-    dy_all = lax.all_gather(dy_low, "expert", axis=0)
     inputs_low = tokens[0]
     total_rows = inputs_low.shape[0]
-    tree_length = parents.shape[1] * SEG
-    query_ids = lax.axis_index("dp") * total_rows + jnp.arange(total_rows, dtype=jnp.int32)
-    visible, query_positions = tree_visibility(parents[0], query_ids, tree_length)
-    bias = jnp.where(visible, 0.0, NEGATIVE)
-    cos, sin = rotation_rows(query_positions)
+    half = HEAD_SIZE // 2
+    frequency = THETA ** -(np.arange(half, dtype=np.float64) * 2.0 / HEAD_SIZE)
+    freq = np.concatenate([frequency, frequency]).astype(np.float32)[None]
     expert_ids = jnp.arange(experts, dtype=jnp.int32)
-    hit_rows = jnp.any(routes[0][None, :, :] == expert_ids[:, None, None], axis=2)
-    n1, query_low, kv_all, mixed, logs, middle, n2, gate_rows, full = attention_pass(
-        inputs_low, shard, cos, sin, bias, hit_rows.astype(F32), kv_width
+    hit_rows = jnp.any(routes[0][None, :, :] == expert_ids[:, None, None], axis=2).astype(F32)
+    n1, query_low, kv_all, mixed, logs, middle, n2, gate_rows, cos, sin, bias, full, dy_all = (
+        attention_pass(inputs_low, shards, freq, parents, hit_rows, dy_low)
     )
     row_sum, gate_grads, sums, wide_part, down_part, _ = expert_pass(
         n2, gate_rows, dy_all, gate_weight[0], up_weight[0], down_weight[0]

time: 509 us -> 448 us (0.88)
  Pallas kernels: 459 us -> 409 us
  other arithmetic: 19.7 us -> 14.5 us
    pallas_call x1, Pallas kernels: 186 us -> 154 us  [expert_pass(): pl.pallas_call(expert_kernel, name='expert_pass', out_shape=outs, in_spec...]
    pallas_call x1, Pallas kernels: 125 us -> 112 us  [attention_pass(): pl.pallas_call(attention_kernel, name='attention_pass', out_shape=(shape(...]
  transfers between devices with their start and end apart: 2 -> 1, of which waited for: 0 -> 0; matrix products, arithmetic and copies ran while one was open for 5% -> 3% of each run, Pallas kernels for 54% -> 32%
where the time goes in v4:
time: 448 us; the launch traced here: 445 us
  Pallas kernels  409 us (91%)
  other arithmetic  14.5 us (3%)
  between operations  14.5 us (3%)
  local copies, waits for them, and re-layouts  7.68 us (2%)
    pallas_call x1, Pallas kernels, expert_pass(): pl.pallas_call(expert_kernel, name='expert_pass', out_shape=outs, in_spec...  154 us
    pallas_call x1, Pallas kernels, backward_pass(): pl.pallas_call(backward_kernel, name='backward_pass', out_shape=(shape((r...  143 us
    pallas_call x1, Pallas kernels, attention_pass(): pl.pallas_call(attention_kernel, name='attention_pass', out_shape=(shape(...  112 us
  transfers between devices with their start and end apart: 1, of which 0 were waited for; matrix products, arithmetic and copies ran while one was open for 3% of the time, Pallas kernels for 32%

profile of v4, /device:TPU:0, one launch (start us, length us, event | category | flops | bytes accessed | tf_op | source)
XLA Modules:
  0.0 445.4 jit_solution(4502867133209251046)
XLA Ops:
  7.2 0.0 reduce-scatter.2.cloned.1.call-start
  7.2 0.7 fusion.2
  7.9 0.7 pad_maximum_fusion.2
  8.7 0.1 copy.40
  8.8 0.6 convert_element_type.23.hits_ref
  9.4 0.6 pad.4.ws_ref
  10.0 111.6 %attention_pass.1 = (bf16[352,1536]{1,0:T(8,128)(2,1)}, bf16[352,1536]{1,0:T(8,128)(2,1)}, bf16[1408,512]{1,0:T(8,128)(2,1)}, bf16[352,1536]{1,0:T(8,128)(2,1)},...) custom-call(bf16[352,1536]{1,0:T(8,128)(2,1)} %bitcast.24, ...), custom_call_target="tpu_custom_call" | custom-call | flops 10000000000 | bytes 314572800 | tf_op jit(solution)/shard_map/attention_pass/pallas_call | solution.py:1485
  121.6 153.9 %expert_pass.1 = (f32[352,1536]{1,0:T(8,128)}, f32[8,384]{1,0:T(8,128)}, bf16[8,352,1536]{2,1,0:T(8,128)(2,1)}, bf16[2,384,768]{2,1,0:T(8,128)(2,1)}, bf16[768,3...) custom-call(bf16[352,1536]{1,0:T(8,128)(2,1)} %get-tuple-element.35.n2_ref, f32[8,384]{1,0:T(8,128)} %get-tuple-element.36.gate_ref, ...), custom_call_target="tpu_custom_call" | custom-call | flops 59793997824 | bytes 62914560 | tf_op jit(solution)/shard_map/expert_pass/pallas_call | solution.py:974
  275.5 0.0 reduce-scatter.2.cloned.1.call-update
  275.5 143.2 %backward_pass.1 = (f32[352,1536]{1,0:T(8,128)}, f32[48,3712]{1,0:T(8,128)}, bf16[2,1536,768]{2,1,0:T(8,128)(2,1)}, bf16[768,1536]{1,0:T(8,128)(2,1)}) custom-call(bf16[352,1536]{1,0:T(8,128)(2,1)} %bitcast.25, bf16[352,1536]{1,0:T(8,128)(2,1)} %bitcast.27, f32[8,384]{1,0:T(8,128)} %get-tuple-element.36.gate_ref, f32[8,384]{1,0:T(8,128)} %get-tuple-element.39.gg_ref, ...), custom_call_target="tpu_custom_call" | custom-call | flops 20000000000 | bytes 209715200 | tf_op jit(solution)/shard_map/backward_pass/pallas_call | solution.py:1978
  418.7 0.7 slice.45
  419.4 0.7 copy.41
  420.1 1.5 slice_reduce_fusion
  421.6 0.8 fusion.4
  422.4 0.6 pad_maximum_fusion
  423.0 1.9 fusion.3
  424.9 0.0 copy-start
  424.9 4.6 %bitcast_convert_fusion = f32[1,768,1536]{2,1,0:T(8,128)} fusion(bf16[768,1536]{1,0:T(8,128)(2,1)} %get-tuple-element.55), kind=kLoop, calls=%fused_computation | loop fusion | flops 1179648 | bytes 7077888 | tf_op jit(solution)/shard_map/broadcast_in_dim | solution.py:2089
  429.6 0.0 copy-done
  429.6 0.0 copy-start.1
  429.6 4.5 %slice_convert_fusion = (f32[1,1536,768]{2,1,0:T(8,128)}, f32[1,1536,768]{2,1,0:T(8,128)}) fusion(bf16[2,1536,768]{2,1,0:T(8,128)(2,1)S(1)} %copy-done), kind=kLoop, calls=%fused_computation.1 | loop fusion | flops 2359296 | bytes 14155776 | tf_op jit(solution)/shard_map/convert_element_type | solution.py:2088
  434.1 0.0 reduce-scatter.2.cloned.1.call-done
  434.1 0.0 copy-done.1
  434.1 0.0 copy-start.2
  434.1 2.7 fusion.1
  436.7 0.0 copy-done.2
  436.7 1.3 copy.43
Async XLA Ops:
  7.2 426.9 %reduce-scatter.2.cloned.1.call-start = ((), (), s32[]{:S(2)}) async-start(), calls=%async_computation.1 | async-start | bytes 9732096 | tf_op jit(solution)/shard_map/reduce_scatter | solution.py:2062
  424.9 4.7 %copy-start = (bf16[2,1536,768]{2,1,0:T(8,128)(2,1)S(1)}, bf16[2,1536,768]{2,1,0:T(8,128)(2,1)}, u32[]{:S(2)}) copy-start(bf16[2,1536,768]{2,1,0:T(8,128)(2,1)} %get-tuple-element.54) | copy-start | bytes 14155780
  429.6 4.5 %copy-start.1 = (f32[352,1536]{1,0:T(8,128)S(1)}, f32[352,1536]{1,0:T(8,128)}, u32[]{:S(2)}) copy-start(f32[352,1536]{1,0:T(8,128)} %get-tuple-element.34.middle_any) | copy-start | bytes 6488068
  434.1 2.7 copy-start.2
Sparse Core Ops, SparseCore 0:
  275.6 90.4 reduce-scatter.1

commit v5 on v4

--- a/solution.py
+++ b/solution.py
@@ -435,12 +435,12 @@
 
 
 def expert_kernel(
-    n2_ref, gate_ref, dy_ref, gw_ref, uw_ref, dw_ref,
+    n2_ref, gate_ref, dy_ref, gw_any, uw_any, dw_any,
     row_ref, gg_ref, sum_ref, wide_ref, down_ref, landing,
-    n2_all, gate_all, dy_buf, dy_cols, hs_all, gl_all, ul_all, own, sib, zin, gg_out, gg_in,
+    gw_ref, uw_ref, dw_ref, n2_all, gate_all, dy_buf, dy_cols, hs_all, gl_all, ul_all, own, sib, zin, gg_out, gg_in,
     gate_cols, gg_cols, stage, kept, down_kept,
     n2_send, n2_recv, gt_send, gt_recv, own_send, sib_recv, zin_send, zin_recv,
-    gg_send, gg_recv, dy_sem, cols_sem, sum_sem, tile_send, tile_recv, load_sem, keep_sem,
+    gg_send, gg_recv, dy_sem, cols_sem, sum_sem, tile_send, tile_recv, load_sem, keep_sem, weight_sem,
 ):
     count = lax.axis_size("expert")
     depth = count // 2
@@ -462,6 +462,12 @@
         n2_ref, n2_all.at[pl.ds(pl.multiple_of(me * rows, 16), rows)], cols_sem
     )
     n2_load.start()
+    weight_loads = [
+        pltpu.make_async_copy(src, dst, weight_sem.at[i])
+        for i, (src, dst) in enumerate(((dw_any, dw_ref), (gw_any, gw_ref), (uw_any, uw_ref)))
+    ]
+    for load in weight_loads:
+        load.start()
     barrier = pltpu.get_barrier_semaphore()
     for other in range(1, count):
         pl.semaphore_signal(
@@ -784,6 +790,8 @@
             lax.fori_loop(0, 2, side, 0)
         return 0
 
+    for load in weight_loads:
+        load.wait()
     col_copy(0).start()
     lax.fori_loop(0, depth, by_distance, 0)
 
@@ -975,9 +983,12 @@
         expert_kernel,
         name="expert_pass",
         out_shape=outs,
-        in_specs=[anywhere, vmem, anywhere, vmem, vmem, vmem],
+        in_specs=[anywhere, vmem] + [anywhere] * 4,
         out_specs=(vmem, vmem, anywhere, anywhere, anywhere, anywhere),
         scratch_shapes=[
+            pltpu.VMEM((width, ff), BF),
+            pltpu.VMEM((width, ff), BF),
+            pltpu.VMEM((ff, width), BF),
             pltpu.VMEM((count * rows, width), BF),
             pltpu.VMEM((count, count, lanes), F32),
             pltpu.VMEM((2, 2, rows // 2, width), BF),
@@ -998,7 +1009,7 @@
             dma((count, 2, 3)), dma((count, 2)), dma((count, 3)), dma((count,)),
             dma((depth, 2)), dma((depth, 2)), dma((depth, 2)), dma((depth + 1, 2)),
             dma((count,)), dma((count,)), dma((2, 2)), dma, dma((count,)), dma((3, 6)), dma((3, 3, 2)),
-            dma((3, 3)), dma((2,)),
+            dma((3, 3)), dma((2,)), dma((3,)),
         ],
         compiler_params=pltpu.CompilerParams(
             collective_id=2, has_side_effects=True, vmem_limit_bytes=62 * 2**20
@@ -1524,9 +1535,10 @@
 
 
 def backward_kernel(
-    x_ref, dy_ref, gate_ref, gg_ref, n1_ref, q_ref, kv_ref, mixed_ref, n2_ref, lse_ref,
-    cos_ref, sin_ref, bias_ref, middle_any, row_ref, w_full, wide_ref, down_ref,
+    gate_ref, gg_ref, x_any, dy_any, n1_any, q_any, kv_any, mixed_any, n2_any, lse_any,
+    cos_any, sin_any, bias_any, middle_any, row_ref, w_full, wide_ref, down_ref,
     tok_ref, share_ref, wide_all, down_all,
+    x_ref, dy_ref, n1_ref, q_ref, kv_ref, mixed_ref, n2_ref, lse_ref, cos_ref, sin_ref, bias_ref,
     middle, wbuf, wsmall, attended, mixed_grad, qg, dkv, kv_low, kv_in, w, wsib, legs, legs2, wz,
     load_sem, ag_local, ag_xs, ag_xr, ag_ys, ag_yr, ag_fs, ag_fr, kv_send, kv_recv,
     ws_send, ws_recv, a_send, a_recv, b_send, b_recv, a2_send, a2_recv, b2_send, b2_recv,
@@ -1551,8 +1563,6 @@
     def at(zz):
         return {"expert": zz * 2 + core}
 
-    greet(depth, z, at, (sibling, {"dp": xn}, {"dp": yn}, {"dp": diag}))
-
     def remote(src, dst, send, recv, target):
         return pltpu.make_async_remote_copy(
             src, dst, send, recv, device_id=target, device_id_type=MESH
@@ -1566,10 +1576,21 @@
     load_small = load(w_full.at[:, pl.ds(qkv_width, 128)], wsmall, 2)
     load_qkv = load(w_full.at[:, pl.ds(0, qkv_width)], wbuf, 3)
     load_middle = load(middle_any, middle, 4)
-    load_small.start()
-    load_rows.start()
-    load_middle.start()
-    load_out.start()
+    load_n2, load_dy, load_mixed, *load_rest = [
+        load(src, dst, 5 + i)
+        for i, (src, dst) in enumerate(
+            (
+                (n2_any, n2_ref), (dy_any, dy_ref), (mixed_any, mixed_ref), (q_any, q_ref),
+                (kv_any, kv_ref), (lse_any, lse_ref), (bias_any, bias_ref), (cos_any, cos_ref),
+                (sin_any, sin_ref), (n1_any, n1_ref), (x_any, x_ref),
+            )
+        )
+    ]
+    for first in (load_small, load_n2, load_rows, load_middle, load_dy, load_mixed, load_out):
+        first.start()
+    for rest in load_rest:
+        rest.start()
+    greet(depth, z, at, (sibling, {"dp": xn}, {"dp": yn}, {"dp": diag}))
 
     quarter = wide_ref.shape[1]
     down_half = down_ref.shape[0] // 2
@@ -1775,10 +1796,12 @@
     router = small[:experts].astype(BF).astype(F32)
     router_two = jnp.concatenate([router, router], axis=0).astype(BF)
     gain_one, gain_two = small[experts : experts + 1], small[experts + 1 : experts + 2]
+    load_n2.wait()
     router_grad = mm(logit_two, n2_ref[...])
     router_grad = router_grad[:experts] + router_grad[experts:]
     load_rows.wait()
     load_middle.wait()
+    load_dy.wait()
     tok_ref[...] += mm_tn(logit_two, router_two)
 
     def norm_back(value, grad, gain):
@@ -1797,6 +1820,7 @@
         return carry + gain
 
     gain_two_grad = lax.fori_loop(0, rows // block, second_norm, jnp.zeros((1, width), F32))
+    load_mixed.wait()
     weight_rows(mixed_ref, attended[...], split, width)
     begin(0)
     load_out.wait()
@@ -1811,6 +1835,8 @@
     load_qkv.start()
     first_legs(0)
     quarters(1)
+    for rest in load_rest:
+        rest.wait()
 
     lanes = lax.broadcasted_iota(jnp.int32, lse_ref.shape, 1)
 
@@ -1984,9 +2010,10 @@
             shape((2, 4 * wide_part.shape[1], wide_part.shape[2]), BF),
             shape((down_part.shape[0], 4 * down_part.shape[1]), BF),
         ),
-        in_specs=[vmem] * 13 + [anywhere] * 5,
+        in_specs=[vmem] * 2 + [anywhere] * 16,
         out_specs=(vmem, vmem, anywhere, anywhere),
         scratch_shapes=[
+            *[pltpu.VMEM(a.shape, a.dtype) for a in (x, dy, n1, q, kv, mixed, n2, logs, cos, sin, bias)],
             pltpu.VMEM((rows, width), F32),
             pltpu.VMEM((width, qkv_width), BF),
             pltpu.VMEM((width, 128), BF),
@@ -2001,7 +2028,7 @@
             pltpu.VMEM((2, depth, shard, total), BF),
             pltpu.VMEM((depth, shard, total), BF),
             pltpu.VMEM((depth + 1, shard, total), BF),
-            dma((5,)), dma((4,)), dma((4,)), dma((4,)), dma((4,)), dma((4,)), dma((4,)), dma((4,)),
+            dma((16,)), dma((4,)), dma((4,)), dma((4,)), dma((4,)), dma((4,)), dma((4,)), dma((4,)),
             dma((groups, 3)), dma((groups, 4)),
             dma((parts, 4)), dma((parts, 4)), dma((parts, 2)), dma((parts, 2)), dma((parts, 2)), dma((parts, 2)),
             dma((parts,)), dma((parts,)), dma((parts,)), dma((parts,)),
@@ -2014,9 +2041,80 @@
             flops=2 * 10**10, bytes_accessed=200 * 2**20, transcendentals=0
         ),
     )(
-        x, dy, gates, gate_grads, n1, q, kv, mixed, n2, logs, cos, sin, bias,
+        gates, gate_grads, x, dy, n1, q, kv, mixed, n2, logs, cos, sin, bias,
         middle, row_sum, w_full, wide_part, down_part,
     )
+
+
+def finish_kernel(
+    wide_ref, down_ref, share_ref, middle_ref, sum_ref, tok_in,
+    out_ref, tok_ref, first_ref, second_ref, query_ref, key_ref, value_ref, proj_ref, router_ref,
+    gate_ref, up_ref, dgrad_ref,
+):
+    gate_ref[...] = wide_ref[0].astype(F32)
+    up_ref[...] = wide_ref[1].astype(F32)
+    dgrad_ref[...] = down_ref[...].astype(F32)
+    out_ref[...] = (middle_ref[...] + sum_ref[...].astype(F32)).astype(BF)
+    tok_ref[...] = tok_in[...]
+
+    @pl.when(pl.program_id(0) == 0)
+    def _():
+        wide = query_ref.shape[1]
+        groups = key_ref.shape[1] // HEAD_SIZE
+        query_ref[...] = share_ref[:, :wide]
+        for g in range(groups):
+            low, head = wide + 2 * g * HEAD_SIZE, slice(g * HEAD_SIZE, (g + 1) * HEAD_SIZE)
+            key_ref[:, head] = share_ref[:, low : low + HEAD_SIZE]
+            value_ref[:, head] = share_ref[:, low + HEAD_SIZE : low + 2 * HEAD_SIZE]
+        start = wide + 2 * groups * HEAD_SIZE
+        small = share_ref[:, start : start + 128]
+        experts = router_ref.shape[1]
+        router_ref[...] = small[:, :experts]
+        rows = small.shape[0]
+        turned = jnp.transpose(
+            jnp.concatenate([small, jnp.zeros((128 - rows, 128), F32)], axis=0)
+        )
+        first_ref[...] = turned[experts : experts + 1, :rows]
+        second_ref[...] = turned[experts + 1 : experts + 2, :rows]
+        proj_ref[...] = share_ref[:, start + 128 :]
+
+
+def finish_pass(wide, down, share, middle, sums, tok, experts):
+    steps = 3
+    rows, width = middle.shape
+    piece = rows // 2
+    shard = share.shape[0]
+    heads, kv = QUERY_HEADS * HEAD_SIZE, KEY_VALUE_HEADS * HEAD_SIZE
+    _, tall, ff = wide.shape
+    shape = jax.ShapeDtypeStruct
+
+    def whole(*dims):
+        return pl.BlockSpec(dims, lambda i: (0,) * len(dims))
+
+    token_rows = pl.BlockSpec((piece, width), lambda i: (jnp.minimum(i, rows // piece - 1), 0))
+    tall_rows = pl.BlockSpec((tall // steps, ff), lambda i: (i, 0))
+    down_rows = pl.BlockSpec((ff // steps, tall), lambda i: (i, 0))
+    return pl.pallas_call(
+        finish_kernel,
+        name="finish_pass",
+        grid=(steps,),
+        in_specs=[
+            pl.BlockSpec((2, tall // steps, ff), lambda i: (0, i, 0)),
+            down_rows, whole(*share.shape), token_rows, token_rows, token_rows,
+        ],
+        out_specs=(
+            token_rows, token_rows, whole(1, shard), whole(1, shard), whole(shard, heads),
+            whole(shard, kv), whole(shard, kv), whole(shard, width), whole(shard, experts),
+            tall_rows, tall_rows, down_rows,
+        ),
+        out_shape=(
+            shape((rows, width), BF), shape((rows, width), F32), shape((1, shard), F32),
+            shape((1, shard), F32), shape((shard, heads), F32), shape((shard, kv), F32),
+            shape((shard, kv), F32), shape((shard, width), F32), shape((shard, experts), F32),
+            shape((tall, ff), F32), shape((tall, ff), F32), shape((ff, tall), F32),
+        ),
+        compiler_params=pltpu.CompilerParams(vmem_limit_bytes=62 * 2**20),
+    )(wide, down, share, middle, sums, tok)
 
 
 def dense_on_device(
@@ -2036,18 +2134,13 @@
     down_weight,
 ):
     experts = router_weight.shape[1]
-    heads_width = QUERY_HEADS * HEAD_SIZE
-    kv_width = 2 * KEY_VALUE_HEADS * HEAD_SIZE
-    qkv_width = heads_width + kv_width
     small_shard = jnp.concatenate(
         [router_weight, first_gain[:, None], second_gain[:, None]], axis=1
     )
     small_shard = jnp.pad(small_shard, ((0, 0), (0, -small_shard.shape[1] % 128)))
-    small_width = small_shard.shape[1]
     shards = (query_weight, key_matrix, value_matrix, small_shard, out_weight)
     dy_low = cotangent[0]
     inputs_low = tokens[0]
-    total_rows = inputs_low.shape[0]
     half = HEAD_SIZE // 2
     frequency = THETA ** -(np.arange(half, dtype=np.float64) * 2.0 / HEAD_SIZE)
     freq = np.concatenate([frequency, frequency]).astype(np.float32)[None]
@@ -2064,29 +2157,22 @@
         inputs_low, dy_low, middle, gate_rows, gate_grads, n1, query_low, kv_all, mixed, n2, logs,
         cos, sin, bias, row_sum, full, wide_part, down_part,
     )
-    output = (middle + combined.astype(F32)).astype(BF)[None]
-    heads_of = [
-        share[:, heads_width + i * HEAD_SIZE : heads_width + (i + 1) * HEAD_SIZE]
-        for i in range(2 * KEY_VALUE_HEADS)
-    ]
-    query_share = share[:, :heads_width]
-    key_share = jnp.concatenate(heads_of[0::2], axis=1)
-    value_share = jnp.concatenate(heads_of[1::2], axis=1)
-    small_share = share[:, qkv_width : qkv_width + small_width]
-    out_share = share[:, qkv_width + small_width :]
+    output, input_grad, gain_one, gain_two, query, key, value, proj, router, gate, up, down = finish_pass(
+        wide_grads, down_grad, share, middle, combined, input_grad, experts
+    )
     return (
-        output,
+        output[None],
         input_grad[None],
-        small_share[:, experts],
-        small_share[:, experts + 1],
-        query_share,
-        key_share,
-        value_share,
-        out_share,
-        small_share[:, :experts],
-        wide_grads[0].astype(F32)[None],
-        wide_grads[1].astype(F32)[None],
-        down_grad.astype(F32)[None],
+        gain_one[0],
+        gain_two[0],
+        query,
+        key,
+        value,
+        proj,
+        router,
+        gate[None],
+        up[None],
+        down[None],
     )
 
 

time: 448 us -> 434 us (0.969)
  other arithmetic: 14.5 us -> 2.03 us
  local copies, waits for them, and re-layouts: 7.68 us -> 2.11 us
    pallas_call x0 -> x1, Pallas kernels: none -> 10.1 us  [finish_pass(): pl.pallas_call(finish_kernel, name='finish_pass', grid=(steps,), in_specs...]
    broadcast_in_dim x2 -> x0, other arithmetic: 7.3 us -> none  [the longest x1 4.65 us: dense_on_device(): down_grad.astype(F32)[None]]
    slice x4 -> x0, local copies, waits for them, and re-layouts: 4.96 us -> none  [the longest x1 1.9 us: dense_on_device(): out_share = share[:, qkv_width + small_width:]]
    convert_element_type x1 -> x0, other arithmetic: 4.48 us -> none  [dense_on_device(): wide_grads[1].astype(F32)[None]]
  transfers between devices with their start and end apart: 1 -> 1, of which waited for: 0 -> 0; matrix products, arithmetic and copies ran while one was open for 3% -> 0% of each run, Pallas kernels for 32% -> 32%
where the time goes in v5:
time: 434 us; the launch traced here: 431 us
  Pallas kernels  412 us (95%)
  between operations  14.5 us (3%)
    pallas_call x1, Pallas kernels, expert_pass(): pl.pallas_call(expert_kernel, name='expert_pass', out_shape=outs, in_spec...  152 us
    pallas_call x1, Pallas kernels, backward_pass(): pl.pallas_call(backward_kernel, name='backward_pass', out_shape=(shape((r...  139 us
    pallas_call x1, Pallas kernels, attention_pass(): pl.pallas_call(attention_kernel, name='attention_pass', out_shape=(shape(...  112 us
    pallas_call x1, Pallas kernels, finish_pass(): pl.pallas_call(finish_kernel, name='finish_pass', grid=(steps,), in_specs...  10.1 us
  transfers between devices with their start and end apart: 1, of which 0 were waited for; matrix products, arithmetic and copies ran while one was open for 0% of the time, Pallas kernels for 32%

profile of v5, /device:TPU:0, one launch (start us, length us, event | category | flops | bytes accessed | tf_op | source)
XLA Modules:
  0.0 431.1 jit_solution(8547257112506904862)
XLA Ops:
  7.2 0.0 reduce-scatter.2.cloned.1.call-start
  7.2 0.7 fusion
  7.9 0.7 pad_maximum_fusion
  8.7 0.1 copy.35
  8.8 0.6 convert_element_type.5.hits_ref
  9.4 0.6 pad.4.ws_ref
  10.0 111.6 %attention_pass.1 = (bf16[352,1536]{1,0:T(8,128)(2,1)}, bf16[352,1536]{1,0:T(8,128)(2,1)}, bf16[1408,512]{1,0:T(8,128)(2,1)}, bf16[352,1536]{1,0:T(8,128)(2,1)},...) custom-call(bf16[352,1536]{1,0:T(8,128)(2,1)} %bitcast.27, ...), custom_call_target="tpu_custom_call" | custom-call | flops 10000000000 | bytes 314572800 | tf_op jit(solution)/shard_map/attention_pass/pallas_call | solution.py:1496
  121.6 151.6 %expert_pass.1 = (f32[352,1536]{1,0:T(8,128)}, f32[8,384]{1,0:T(8,128)}, bf16[8,352,1536]{2,1,0:T(8,128)(2,1)}, bf16[2,384,768]{2,1,0:T(8,128)(2,1)}, bf16[768,3...) custom-call(bf16[352,1536]{1,0:T(8,128)(2,1)} %get-tuple-element.47.n2_ref.n2_any, f32[8,384]{1,0:T(8,128)} %get-tuple-element.46.gate_ref, ...), custom_call_target="tpu_custom_call" | custom-call | flops 59793997824 | bytes 62914560 | tf_op jit(solution)/shard_map/expert_pass/pallas_call | solution.py:982
  273.2 0.0 reduce-scatter.2.cloned.1.call-update
  273.2 139.1 %backward_pass.1 = (f32[352,1536]{1,0:T(8,128)}, f32[48,3712]{1,0:T(8,128)}, bf16[2,1536,768]{2,1,0:T(8,128)(2,1)}, bf16[768,1536]{1,0:T(8,128)(2,1)}) custom-call(f32[8,384]{1,0:T(8,128)} %get-tuple-element.46.gate_ref, f32[8,384]{1,0:T(8,128)} %get-tuple-element.49.gg_ref, bf16[352,1536]{1,0:T(8,128)(2,1)} %bitcast.28, bf16[352,1536]{1,0:T(8,128)(2,1)} %bitcast.30, ...), custom_call_target="tpu_custom_call" | custom-call | flops 20000000000 | bytes 209715200 | tf_op jit(solution)/shard_map/backward_pass/pallas_call | solution.py:2004
  412.4 0.0 reduce-scatter.2.cloned.1.call-done
  412.4 10.1 %finish_pass.1 = (bf16[352,1536]{1,0:T(8,128)(2,1)}, f32[352,1536]{1,0:T(8,128)}, f32[1,48]{1,0:T(1,128)}, f32[1,48]{1,0:T(1,128)}, f32[48,1536]{1,0:T(8,128)}, ...) custom-call(bf16[2,1536,768]{2,1,0:T(8,128)(2,1)} %get-tuple-element, ...), custom_call_target="tpu_custom_call" | custom-call | tf_op jit(solution)/shard_map/finish_pass/pallas_call | solution.py:2097
  422.4 1.4 copy.36
Async XLA Ops:
  7.2 405.2 %reduce-scatter.2.cloned.1.call-start = ((), (), s32[]{:S(2)}) async-start(), calls=%async_computation.1 | async-start | bytes 9732096 | tf_op jit(solution)/shard_map/reduce_scatter | solution.py:2155
Sparse Core Ops, SparseCore 0:
  273.3 90.3 reduce-scatter.1

commit v6 on v5

--- a/solution.py
+++ b/solution.py
@@ -1296,17 +1296,17 @@
     spread_step(1, 1)
     xy_step(0, 2)
     z_step(2, 1)
-    xy_step(0, 3)
     z_step(1, 2)
     spread_step(1, 2)
-    for d in range(depth):
-        diag_step(0, d)
     z_step(2, 2)
-    xy_step(1, 0)
     z_step(1, 3)
     spread_step(1, 3)
     z_step(2, 3)
     dy_step(0)
+    xy_step(0, 3)
+    for d in range(depth):
+        diag_step(0, d)
+    xy_step(1, 0)
     all_here(0)
 
     def keep(p):
@@ -1405,6 +1405,8 @@
         lambda: kv_here(1),
         lambda: (diag_step(2, 0), diag_step(2, 1)),
         lambda: (diag_step(2, 2), diag_step(2, 3)),
+        lambda: (),
+        lambda: dy_step(2),
     ]
     lse_ref[...] = jnp.zeros_like(lse_ref)
     lanes = lax.broadcasted_iota(jnp.int32, lse_ref.shape, 1)
@@ -1435,7 +1437,6 @@
         copy.start()
     all_here(2)
     keep(2).start()
-    dy_step(2)
     tile = 512
 
     def project_out(i, _):
@@ -2134,10 +2135,16 @@
     down_weight,
 ):
     experts = router_weight.shape[1]
+    shard_rows = router_weight.shape[0]
     small_shard = jnp.concatenate(
-        [router_weight, first_gain[:, None], second_gain[:, None]], axis=1
-    )
-    small_shard = jnp.pad(small_shard, ((0, 0), (0, -small_shard.shape[1] % 128)))
+        [
+            router_weight,
+            first_gain[:, None],
+            second_gain[:, None],
+            jnp.zeros((shard_rows, -(experts + 2) % 128), BF),
+        ],
+        axis=1,
+    )
     shards = (query_weight, key_matrix, value_matrix, small_shard, out_weight)
     dy_low = cotangent[0]
     inputs_low = tokens[0]
@@ -2145,7 +2152,7 @@
     frequency = THETA ** -(np.arange(half, dtype=np.float64) * 2.0 / HEAD_SIZE)
     freq = np.concatenate([frequency, frequency]).astype(np.float32)[None]
     expert_ids = jnp.arange(experts, dtype=jnp.int32)
-    hit_rows = jnp.any(routes[0][None, :, :] == expert_ids[:, None, None], axis=2).astype(F32)
+    hit_rows = jnp.sum((routes[0][None, :, :] == expert_ids[:, None, None]).astype(F32), axis=2)
     n1, query_low, kv_all, mixed, logs, middle, n2, gate_rows, cos, sin, bias, full, dy_all = (
         attention_pass(inputs_low, shards, freq, parents, hit_rows, dy_low)
     )

time: 434 us -> 434 us (level)
  no operation moved by 1% of the time
where the time goes in v6:
time: 434 us; the launch traced here: 431 us
  Pallas kernels  411 us (95%)
  between operations  14.5 us (3%)
    pallas_call x1, Pallas kernels, expert_pass(): pl.pallas_call(expert_kernel, name='expert_pass', out_shape=outs, in_spec...  152 us
    pallas_call x1, Pallas kernels, backward_pass(): pl.pallas_call(backward_kernel, name='backward_pass', out_shape=(shape((r...  139 us
    pallas_call x1, Pallas kernels, attention_pass(): pl.pallas_call(attention_kernel, name='attention_pass', out_shape=(shape(...  110 us
    pallas_call x1, Pallas kernels, finish_pass(): pl.pallas_call(finish_kernel, name='finish_pass', grid=(steps,), in_specs...  10.1 us
  transfers between devices with their start and end apart: 1, of which 0 were waited for; matrix products, arithmetic and copies ran while one was open for 0% of the time, Pallas kernels for 32%

profile of v6, /device:TPU:0, one launch (start us, length us, event | category | flops | bytes accessed | tf_op | source)
XLA Modules:
  0.0 431.1 jit_solution(12152930900321440769)
XLA Ops:
  7.2 0.0 reduce-scatter.2.cloned.1.call-start
  7.2 1.3 convert_reduce_fusion.hits_ref
  8.5 0.8 copy.33
  9.3 0.8 copy.34
  10.0 0.8 copy.32
  10.8 0.1 pad.3.clone
  10.9 0.7 maximum_maximum_fusion.ws_ref
  11.6 109.7 %attention_pass.1 = (bf16[352,1536]{1,0:T(8,128)(2,1)}, bf16[352,1536]{1,0:T(8,128)(2,1)}, bf16[1408,512]{1,0:T(8,128)(2,1)}, bf16[352,1536]{1,0:T(8,128)(2,1)},...) custom-call(bf16[352,1536]{1,0:T(8,128)(2,1)} %bitcast.27, ...), custom_call_target="tpu_custom_call" | custom-call | flops 10000000000 | bytes 314572800 | tf_op jit(solution)/shard_map/attention_pass/pallas_call | solution.py:1497
  121.3 151.6 %expert_pass.1 = (f32[352,1536]{1,0:T(8,128)}, f32[8,384]{1,0:T(8,128)}, bf16[8,352,1536]{2,1,0:T(8,128)(2,1)}, bf16[2,384,768]{2,1,0:T(8,128)(2,1)}, bf16[768,3...) custom-call(bf16[352,1536]{1,0:T(8,128)(2,1)} %get-tuple-element.47.n2_ref.n2_any, f32[8,384]{1,0:T(8,128)} %get-tuple-element.46.gate_ref, ...), custom_call_target="tpu_custom_call" | custom-call | flops 59793997824 | bytes 62914560 | tf_op jit(solution)/shard_map/expert_pass/pallas_call | solution.py:982
  272.9 0.0 reduce-scatter.2.cloned.1.call-update
  272.9 139.4 %backward_pass.1 = (f32[352,1536]{1,0:T(8,128)}, f32[48,3712]{1,0:T(8,128)}, bf16[2,1536,768]{2,1,0:T(8,128)(2,1)}, bf16[768,1536]{1,0:T(8,128)(2,1)}) custom-call(f32[8,384]{1,0:T(8,128)} %get-tuple-element.46.gate_ref, f32[8,384]{1,0:T(8,128)} %get-tuple-element.49.gg_ref, bf16[352,1536]{1,0:T(8,128)(2,1)} %bitcast.28, bf16[352,1536]{1,0:T(8,128)(2,1)} %bitcast.30, ...), custom_call_target="tpu_custom_call" | custom-call | flops 20000000000 | bytes 209715200 | tf_op jit(solution)/shard_map/backward_pass/pallas_call | solution.py:2005
  412.4 0.0 reduce-scatter.2.cloned.1.call-done
  412.4 10.1 %finish_pass.1 = (bf16[352,1536]{1,0:T(8,128)(2,1)}, f32[352,1536]{1,0:T(8,128)}, f32[1,48]{1,0:T(1,128)}, f32[1,48]{1,0:T(1,128)}, f32[48,1536]{1,0:T(8,128)}, ...) custom-call(bf16[2,1536,768]{2,1,0:T(8,128)(2,1)} %get-tuple-element, ...), custom_call_target="tpu_custom_call" | custom-call | tf_op jit(solution)/shard_map/finish_pass/pallas_call | solution.py:2098
  422.5 1.4 copy.35
  (1 shorter events, 0.0 us)
Async XLA Ops:
  7.2 405.2 %reduce-scatter.2.cloned.1.call-start = ((), (), s32[]{:S(2)}) async-start(), calls=%async_computation.1 | async-start | bytes 9732096 | tf_op jit(solution)/shard_map/reduce_scatter | solution.py:2162
Sparse Core Ops, SparseCore 0:
  273.1 90.6 reduce-scatter.1
